TPU v7x, 32 devices: a whole 2x2x4 slice. The times are simulated.
32 devices in a mesh: dom: 4 (over y, x), dev: 8 (over z, core).
Axes of the slice: x: 2, y: 2, z: 4, core: 2. Of those that a mesh axis runs over, the one named last changes fastest.
Arguments:
- features: float32 [32768, 512], P(('dom', 'dev')), may hold values from -6 to 6
- tile_rows: int32 [2560], P(('dom', 'dev')), may hold values from 0 to 7
- tile_cols: int32 [2560], P(('dom', 'dev')), may hold values from 0 to 19
- tile_vals: float32 [2560, 128, 128], P(('dom', 'dev')), may hold values from -0.21875 to 0.21875
- tile_count: int32 [32], P(('dom', 'dev')), may hold values from 1 to 80, as said below
- near_send: int32 [32, 8, 1], P(('dom', 'dev')), may hold values from 0 to 7
- far_send: int32 [32, 2, 2], P(('dom', 'dev')), may hold values from 0 to 7
- skew_raw: float32 [2, 512, 512], replicated, may hold values from -0.25 to 0.25
Outputs:
- features_out: float32 [32768, 512], P(('dom', 'dev'))
Inputs may be any that keep to these rules, and one draw needn't show every extreme that they name: The first tile_count[i] tile slots of device i are live, the others are ignored; some device holds 80 live tiles.
All inputs are finite; a program needn't handle non-finite values.
Results may differ from a plain program's by a relative error of at most 0.0001.
Values sent between devices are 32-bit elements; how exact they have to be, the bound alone decides.
No kernel may reach another device: no remote copies, remote signals or barrier semaphores. Data moves between devices by JAX's collectives and lax.ppermute only.
A program may use at most 128 MiB of HBM per device.

v0:
```python
import functools

import jax
import jax.numpy as jnp
from jax import lax
from jax.experimental import pallas as pl
from jax.experimental.pallas import tpu as pltpu
from jax.sharding import PartitionSpec as P

TILE = 128
STEP = 2
MIB = 1024 * 1024
SMALL = pl.CostEstimate(flops=1, bytes_accessed=1, transcendentals=0)


def split(x):
    high = x.astype(jnp.bfloat16)
    return high, (x - high.astype(jnp.float32)).astype(jnp.bfloat16)


def dot3(a_high, a_low, b_high, b_low):
    dot = functools.partial(jnp.dot, preferred_element_type=jnp.float32)
    return dot(a_high, b_high) + (dot(a_high, b_low) + dot(a_low, b_high))


def smem():
    return pl.BlockSpec(memory_space=pltpu.SMEM)


def whole(shape):
    return pl.BlockSpec(shape, lambda i: (0,) * len(shape))


def of_layer(weight):
    array, layer = weight
    return pl.BlockSpec((None,) + array.shape[1:], lambda i: (layer, 0, 0))


def rows_of(shape):
    return pl.BlockSpec((STEP,) + shape[1:], lambda i: (i,) + (0,) * (len(shape) - 1))


def dense_kernel(rows_ref, cols_ref, count_ref, vals_ref, *refs):
    outs, total = refs[:-1], refs[-1]
    total[...] = jnp.zeros_like(total)

    def add(t, carry):
        total[rows_ref[t], cols_ref[t]] += vals_ref[t]
        return carry

    lax.fori_loop(0, count_ref[0], add, 0)

    def write(r, carry):
        first = 0
        for high_ref, low_ref in zip(outs[::2], outs[1::2]):
            for c in range(high_ref.shape[2] // TILE):
                high, low = split(total[r, first + c])
                high_ref[r, :, c * TILE : (c + 1) * TILE] = high
                low_ref[r, :, c * TILE : (c + 1) * TILE] = low
            first += high_ref.shape[2] // TILE
        return carry

    lax.fori_loop(0, total.shape[0], write, 0)


def dense_adjacency(tile_rows, places, tile_count, tile_vals, row_blocks, widths):
    vmem = pl.BlockSpec(memory_space=pltpu.VMEM)
    out_shape = []
    for w in widths:
        out_shape += [jax.ShapeDtypeStruct((row_blocks, TILE, w * TILE), jnp.bfloat16)] * 2
    flat = pl.pallas_call(
        dense_kernel,
        out_shape=out_shape,
        in_specs=[smem(), smem(), smem(), vmem],
        out_specs=[vmem] * len(out_shape),
        scratch_shapes=[pltpu.VMEM((row_blocks, sum(widths), TILE, TILE), jnp.float32)],
        compiler_params=pltpu.CompilerParams(vmem_limit_bytes=60 * MIB),
        cost_estimate=SMALL,
    )(tile_rows, places, tile_count, tile_vals)
    return [(flat[2 * g], flat[2 * g + 1]) for g in range(len(widths))]


def weights_kernel(raw_ref, *refs):
    raw = raw_ref[0]
    skew = 0.5 * (raw - raw.T)
    square = 0.5 * jnp.dot(
        skew, skew, precision=lax.Precision.HIGHEST, preferred_element_type=jnp.float32
    )
    for ref, part in zip(refs, split(skew) + split(square)):
        ref[0] = part


def weights(skew_raw):
    block = pl.BlockSpec((1,) + skew_raw.shape[1:], lambda i: (i, 0, 0))
    return pl.pallas_call(
        weights_kernel,
        grid=(skew_raw.shape[0],),
        out_shape=[jax.ShapeDtypeStruct(skew_raw.shape, jnp.bfloat16)] * 4,
        in_specs=[block],
        out_specs=[block] * 4,
        compiler_params=pltpu.CompilerParams(vmem_limit_bytes=40 * MIB),
        cost_estimate=SMALL,
    )(skew_raw)


def load_split(x_refs, high, low):
    at = 0
    for x_ref in x_refs:
        for b in range(x_ref.shape[0]):
            high[at : at + TILE, :], low[at : at + TILE, :] = split(x_ref[b])
            at += TILE


def flat_rows(ref):
    return ref[...].reshape(-1, ref.shape[-1])


def load_product(x_refs, square_refs, high, low):
    load_split(x_refs, high, low)
    if square_refs:
        product = dot3(high[...], low[...], square_refs[0][...], square_refs[1][...])
        high[...], low[...] = split(product)


def apply_kernel(n_x, has_acc, squared, ah_ref, al_ref, *refs):
    x_refs = refs[:n_x]
    acc_ref = refs[n_x] if has_acc else None
    square_refs = refs[-5:-3] if squared else ()
    o_ref, high, low = refs[-3:]

    @pl.when(pl.program_id(0) == 0)
    def _():
        load_product(x_refs, square_refs, high, low)

    out = dot3(flat_rows(ah_ref), flat_rows(al_ref), high[...], low[...])
    if has_acc:
        out = out + flat_rows(acc_ref)
    o_ref[...] = out.reshape(o_ref.shape)


def front(x, count):
    return whole((count,) + x.shape[1:])


def apply_dense(dense, xs, acc=None, square=()):
    ah, al = dense
    width = xs[0][0].shape[-1]
    out = jax.ShapeDtypeStruct((ah.shape[0], TILE, width), jnp.float32)
    depth = ah.shape[2]
    args = [ah, al] + [x for x, _ in xs]
    specs = [rows_of(ah.shape), rows_of(al.shape)] + [front(x, n) for x, n in xs]
    if acc is not None:
        args.append(acc)
        specs.append(rows_of(acc.shape))
    args += [q for q, _ in square]
    specs += [of_layer(q) for q in square]
    return pl.pallas_call(
        functools.partial(apply_kernel, len(xs), acc is not None, bool(square)),
        grid=(ah.shape[0] // STEP,),
        out_shape=out,
        in_specs=specs,
        out_specs=rows_of(out.shape),
        scratch_shapes=[pltpu.VMEM((depth, width), jnp.bfloat16)] * 2,
        compiler_params=pltpu.CompilerParams(vmem_limit_bytes=40 * MIB),
        cost_estimate=SMALL,
    )(*args)


def mix_kernel(x_ref, once_ref, twice_ref, sh_ref, sl_ref, qh_ref, ql_ref, o_ref):
    out = flat_rows(x_ref) + dot3(*split(flat_rows(once_ref)), sh_ref[...], sl_ref[...])
    out = out + dot3(*split(flat_rows(twice_ref)), qh_ref[...], ql_ref[...])
    o_ref[...] = out.reshape(o_ref.shape)


def mix(x, once, twice, skew, square):
    block = rows_of(x.shape)
    factors = [*skew, *square]
    width = x.shape[-1]
    return pl.pallas_call(
        mix_kernel,
        grid=(x.shape[0] // STEP,),
        out_shape=jax.ShapeDtypeStruct(x.shape, jnp.float32),
        in_specs=[block] * 3 + [of_layer(w) for w in factors],
        out_specs=block,
        compiler_params=pltpu.CompilerParams(vmem_limit_bytes=40 * MIB),
        cost_estimate=SMALL,
    )(x, once, twice, *[w for w, _ in factors])


def picked(plan, me, near_ref, far_ref):
    for entries in plan:
        blocks = []
        for kind, index in entries:
            if kind == "near":
                peer = me ^ index
                blocks += [near_ref[peer, i] for i in range(near_ref.shape[1])]
            else:
                blocks += [far_ref[index, i] for i in range(far_ref.shape[1])]
        yield blocks


def copy_out(plan, me_ref, near_ref, far_ref, source, send_refs, sems):
    copies = []
    for ref, blocks in zip(send_refs, picked(plan, me_ref[0], near_ref, far_ref)):
        for i, block in enumerate(blocks):
            copies.append(pltpu.make_async_copy(source.at[block], ref.at[i], sems.at[len(copies)]))
            copies[-1].start()
    for copy in copies:
        copy.wait()


def plan_sizes(plan, near, far):
    return [sum(near.shape[1] if kind == "near" else far.shape[1] for kind, _ in e) for e in plan]


def pick_kernel(plan, me_ref, near_ref, far_ref, x_ref, *refs):
    copy_out(plan, me_ref, near_ref, far_ref, x_ref, refs[:-1], refs[-1])


def pick(x, route):
    plan, me, near, far = route
    sizes = plan_sizes(plan, near, far)
    hbm = pl.BlockSpec(memory_space=pl.ANY)
    return pl.pallas_call(
        functools.partial(pick_kernel, plan),
        out_shape=[jax.ShapeDtypeStruct((n,) + x.shape[1:], x.dtype) for n in sizes],
        in_specs=[smem()] * 3 + [pl.BlockSpec(memory_space=pltpu.VMEM)],
        out_specs=[hbm] * len(sizes),
        scratch_shapes=[pltpu.SemaphoreType.DMA((sum(sizes),))],
        compiler_params=pltpu.CompilerParams(vmem_limit_bytes=16 * MIB),
        cost_estimate=SMALL,
    )(me, near, far, x)


def finish_kernel(plan, n_x, squared, n_send, me_ref, near_ref, far_ref, ah_ref, al_ref, acc_ref, *refs):
    refs = list(refs)
    x_refs = [refs.pop(0) for _ in range(n_x)]
    square_refs = [refs.pop(0) for _ in range(2 * squared)]
    o_ref = refs.pop(0)
    send_refs = [refs.pop(0) for _ in range(n_send)]
    high, low = refs.pop(0), refs.pop(0)
    step = pl.program_id(0)

    @pl.when(step == 0)
    def _():
        load_product(x_refs, square_refs, high, low)

    out = dot3(flat_rows(ah_ref), flat_rows(al_ref), high[...], low[...]) + flat_rows(acc_ref)
    if squared:
        width = out.shape[1]
        even = lax.broadcasted_iota(jnp.int32, out.shape, 1) % 2 == 0
        after, before = pltpu.roll(out, width - 1, 1), pltpu.roll(out, 1, 1)
        out = jnp.where(even, jnp.minimum(out, after), jnp.maximum(out, before))
    out = out.reshape(o_ref.shape)
    o_ref[...] = out
    if n_send:
        kept, sems = refs
        kept[pl.ds(step * STEP, STEP)] = out

        @pl.when(step == pl.num_programs(0) - 1)
        def _():
            copy_out(plan, me_ref, near_ref, far_ref, kept, send_refs, sems)


def finish(dense, xs, acc, route, square=(), send=True):
    plan, me, near, far = route
    sizes = plan_sizes(plan, near, far) if send else []
    ah, al = dense
    depth, width = ah.shape[2], acc.shape[2]
    field = jax.ShapeDtypeStruct(acc.shape, jnp.float32)
    args = [me, near, far, ah, al, acc] + [x for x, _ in xs]
    specs = [smem()] * 3 + [rows_of(ah.shape), rows_of(al.shape), rows_of(acc.shape)]
    specs += [front(x, n) for x, n in xs]
    args += [q for q, _ in square]
    specs += [of_layer(q) for q in square]
    scratch = [pltpu.VMEM((depth, width), jnp.bfloat16)] * 2
    if send:
        scratch += [pltpu.VMEM(acc.shape, jnp.float32), pltpu.SemaphoreType.DMA((sum(sizes),))]
    return pl.pallas_call(
        functools.partial(finish_kernel, plan, len(xs), bool(square), len(sizes)),
        grid=(acc.shape[0] // STEP,),
        out_shape=[field] + [jax.ShapeDtypeStruct((n, TILE, width), jnp.float32) for n in sizes],
        in_specs=specs,
        out_specs=[rows_of(acc.shape)] + [pl.BlockSpec(memory_space=pl.ANY)] * len(sizes),
        scratch_shapes=scratch,
        compiler_params=pltpu.CompilerParams(vmem_limit_bytes=40 * MIB),
        cost_estimate=SMALL,
    )(*args)


def tie(values, *others):
    done = lax.optimization_barrier(tuple(values) + tuple(others))
    return list(done[: len(values)]), list(done[len(values) :])


def local(features, tile_rows, tile_cols, tile_vals, tile_count, near_send, far_send, skew_raw):
    width = features.shape[1]
    row_blocks = features.shape[0] // TILE
    peers, cap, hcap = near_send.shape[1], near_send.shape[2], far_send.shape[2]
    domains = lax.axis_size("dom")
    d = lax.axis_index("dev")
    me = d.astype(jnp.int32).reshape(1)

    chips = list(range(1, peers // 2))[::-1]
    plan = tuple(
        [(("near", 2 * j), ("near", 2 * j + 1)) for j in chips]
        + [(("far", 0),), (("far", 1),), (("near", 1),)]
    )
    route = (plan, me, near_send[0], far_send[0])

    widths = (row_blocks, 2 * hcap + cap * len(chips), cap * (1 + len(chips)))
    place_of = [0] * peers
    for at, j in enumerate(chips):
        place_of[2 * j] = row_blocks + 2 * hcap + at * cap
    for at, j in enumerate([0] + chips):
        place_of[2 * j + 1] = row_blocks + widths[1] + at * cap
    slot = tile_cols
    near_at = slot - row_blocks
    source, item = near_at // cap, near_at % cap
    source_safe = jnp.clip(source, 0, peers - 1)
    near_place = jnp.take(jnp.array(place_of, jnp.int32), source_safe ^ d) + item
    self_place = jnp.take(near_send[0].reshape(-1), d * cap + item)
    near_place = jnp.where(source_safe == d, self_place, near_place)
    far_place = slot - row_blocks - peers * cap + row_blocks
    places = jnp.where(
        slot < row_blocks, slot, jnp.where(slot < row_blocks + peers * cap, near_place, far_place)
    ).astype(jnp.int32)

    own_a, direct_a, core_a = dense_adjacency(tile_rows, places, tile_count, tile_vals, row_blocks, widths)

    def swap(x, k):
        return lax.ppermute(x, "dev", [(i, i ^ k) for i in range(peers)])

    up = [(i, (i + 1) % domains) for i in range(domains)]
    down = [(j, i) for i, j in up]

    def start(sends):
        n = len(chips)
        near = [swap(s, 2 * j) for s, j in zip(sends[:n], chips)]
        lower = lax.ppermute(sends[n], "dom", up)
        upper = lax.ppermute(sends[n + 1], "dom", down)
        return near, lower, upper, sends[n + 2]

    def arrive(flight, acc, square=()):
        near, lower, upper, to_core = flight
        near, (lower, upper, to_core, acc) = tie(near, lower, upper, to_core, acc)
        passed = swap(jnp.concatenate([to_core] + [r[cap:] for r in near], axis=0), 1)
        direct = [(lower, hcap), (upper, hcap)] + [(r, cap) for r in near]
        return apply_dense(direct_a, direct, acc, square), [(passed, passed.shape[0])]

    current = features.reshape(row_blocks, TILE, width)
    sends = pick(current, route)
    parts = weights(skew_raw)
    layers = skew_raw.shape[0]
    for layer in range(layers):
        flight = start(sends)
        skew, square = [(w, layer) for w in parts[:2]], [(w, layer) for w in parts[2:]]
        acc, passed = arrive(flight, apply_dense(own_a, [(current, row_blocks)]))
        once, *sends = finish(core_a, passed, acc, route)
        flight = start(sends)
        base = mix(current, once, apply_dense(own_a, [(once, row_blocks)]), skew, square)
        base, passed = arrive(flight, base, square)
        current, *sends = finish(core_a, passed, base, route, square, layer < layers - 1)
    return current.reshape(features.shape)


def solution(mesh):
    nodes = ("dom", "dev")
    in_specs = (
        P(nodes, None),
        P(nodes),
        P(nodes),
        P(nodes, None, None),
        P(nodes),
        P(nodes, None, None),
        P(nodes, None, None),
        P(),
    )
    return jax.shard_map(local, mesh=mesh, in_specs=in_specs, out_specs=P(nodes, None), check_vma=False)
```

profile of v0, /device:TPU:0, one launch (start us, length us, event | category | flops | bytes accessed | tf_op | source)
XLA Modules:
  0.0 251.5 jit_solution(5706628618611120976)
XLA Ops:
  5.4 5.1 %collective-permute-start = (f32[2,128,512]{2,1,0:T(8,128)}, f32[2,128,512]{2,1,0:T(8,128)}, u32[]{:S(2)}, u32[]{:S(2)}) collective-permute-start(f32[2,128,512]{2,1,0:T(8,128)} %get-tuple-element.74), channel_id=1, source_target_pairs={{0,6},{1,7},{2,4},{3,5},{4,2},{5,3},{6,0},{7,1},{8,14},{9,15},{10,... | collective-permute-start | bytes 1572872 | tf_op jit(solution)/shard_map/ppermute | solution.py:332
  21.0 9.3 %shard_map.91 = (bf16[8,128,1024]{2,1,0:T(8,128)(2,1)}, bf16[8,128,1024]{2,1,0:T(8,128)(2,1)}, bf16[8,128,896]{2,1,0:T(8,128)(2,1)}, bf16[8,128,896]{2,1,0:T(8,1...) custom-call(s32[80]{0:T(128)} %rows_ref.1, s32[80]{0:T(128)} %compare_select_fusion.1.cols_ref, ...), custom_call_target="tpu_custom_call" | custom-call | flops 1 | bytes 1 | tf_op jit(solution)/shard_map/pallas_call | solution.py:71
  33.5 4.2 %shard_map.93.refs_5_ = f32[8,128,512]{2,1,0:T(8,128)S(1)} custom-call(bf16[8,128,1024]{2,1,0:T(8,128)(2,1)S(1)} %copy-done, bf16[8,128,1024]{2,1,0:T(8,128)(2,1)S(1)} %copy-done.2, f32[8,128,512]{2,1,0:T(8,128)S(1)} %bitcast.14), custom_call_target="tpu_custom_call" | custom-call | flops 1 | bytes 1 | tf_op jit(solution)/shard_map/pallas_call | solution.py:157
  37.8 17.8 %collective-permute-done.1.refs_3_ = f32[2,128,512]{2,1,0:T(8,128)} collective-permute-done((f32[2,128,512]{2,1,0:T(8,128)}, f32[2,128,512]{2,1,0:T(8,128)}, u32[]{:S(2)}, u32[]{:S(2)}) %collective-permute-start.1) | collective-permute-done | bytes 524320 | tf_op jit(solution)/shard_map/ppermute | solution.py:332
  58.7 5.8 %shard_map.94.acc_ref = f32[8,128,512]{2,1,0:T(8,128)S(1)} custom-call(bf16[8,128,896]{2,1,0:T(8,128)(2,1)S(1)} %copy-done.4, bf16[8,128,896]{2,1,0:T(8,128)(2,1)S(1)} %copy-done.5, f32[2,128,512]{2,1,0:T(8,128)} %collective-permute-done.3.refs_0_, f32[2,128,512]{2,1,0:T(8,128)} %collective-permute-done.4.refs_1_, ...), custom_call_target="tpu_custom_call" | custom-call | flops 1 | bytes 1 | tf_op jit(solution)/shard_map/pallas_call | solution.py:157
  64.7 4.8 %shard_map.95 = (f32[8,128,512]{2,1,0:T(8,128)S(1)}, f32[2,128,512]{2,1,0:T(8,128)}, f32[2,128,512]{2,1,0:T(8,128)}, f32[2,128,512]{2,1,0:T(8,128)}, f32[2,128,5...) custom-call(s32[1]{0:T(128)} %bitcast.me_ref, s32[8,1]{1,0:T(8,128)S(1)} %copy.14.near_ref, ...), custom_call_target="tpu_custom_call" | custom-call | flops 1 | bytes 1 | tf_op jit(solution)/shard_map/pallas_call | solution.py:279
  69.5 2.5 %collective-permute-start.6 = (f32[2,128,512]{2,1,0:T(8,128)}, f32[2,128,512]{2,1,0:T(8,128)S(1)}, u32[]{:S(2)}, u32[]{:S(2)}) collective-permute-start(f32[2,128,512]{2,1,0:T(8,128)} %get-tuple-element.89), channel_id=1, source_target_pairs={{0,6},{1,7},{2,4},{3,5},{4,2},{5,3},{6,0},{7,1},{8,14},{9,15},{10,... | collective-permute-start | bytes 1572872 | tf_op jit(solution)/shard_map/ppermute | solution.py:332
  76.8 4.1 %shard_map.97 = (bf16[2,512,512]{2,1,0:T(8,128)(2,1)S(1)}, bf16[2,512,512]{2,1,0:T(8,128)(2,1)S(1)}, bf16[2,512,512]{2,1,0:T(8,128)(2,1)S(1)}, bf16[2,512,512]{2,1,0:T(8,128)(2,1)S(1)}) custom-call(f32[2,512,512]{2,1,0:T(8,128)S(1)} %copy-done.20), custom_call_target="tpu_custom_call" | custom-call | flops 1 | bytes 1 | tf_op jit(solution)/shard_map/pallas_call | solution.py:95
  81.0 4.3 %shard_map.96.twice_ref = f32[8,128,512]{2,1,0:T(8,128)S(1)} custom-call(bf16[8,128,1024]{2,1,0:T(8,128)(2,1)S(1)} %copy-done.1, bf16[8,128,1024]{2,1,0:T(8,128)(2,1)S(1)} %copy-done.3, f32[8,128,512]{2,1,0:T(8,128)S(1)} %get-tuple-element.95.refs_0_.once_ref), custom_call_target="tpu_custom_call" | custom-call | flops 1 | bytes 1 | tf_op jit(solution)/shard_map/pallas_call | solution.py:157
  86.9 4.0 %shard_map.98.refs_5_ = f32[8,128,512]{2,1,0:T(8,128)S(1)} custom-call(f32[8,128,512]{2,1,0:T(8,128)S(1)} %bitcast.15, f32[8,128,512]{2,1,0:T(8,128)S(1)} %copy-done.15, f32[8,128,512]{2,1,0:T(8,128)S(1)} %shard_map.96.twice_ref, bf16[2,512,512]{2,1,0:T(8,128)(2,1)S(1)} %get-tuple-element.96.sh_ref, bf16[2,512,512]{2,1,0:T(8,128)(2,1)S(1)} %get-tuple-element.97.sl_ref, ...), custom_call_target="tpu_custom_call" | custom-call | flops 1 | bytes 1 | tf_op jit(solution)/shard_map/pallas_call | solution.py:179
  90.9 25.9 %collective-permute-done.7.refs_3_ = f32[2,128,512]{2,1,0:T(8,128)S(1)} collective-permute-done((f32[2,128,512]{2,1,0:T(8,128)}, f32[2,128,512]{2,1,0:T(8,128)S(1)}, u32[]{:S(2)}, u32[]{:S(2)}) %collective-permute-start.7) | collective-permute-done | bytes 524320 | tf_op jit(solution)/shard_map/ppermute | solution.py:332
  118.8 6.7 %shard_map.99.acc_ref = f32[8,128,512]{2,1,0:T(8,128)S(1)} custom-call(bf16[8,128,896]{2,1,0:T(8,128)(2,1)S(1)} %copy-done.4, bf16[8,128,896]{2,1,0:T(8,128)(2,1)S(1)} %copy-done.5, f32[2,128,512]{2,1,0:T(8,128)} %collective-permute-done.9.refs_0_, f32[2,128,512]{2,1,0:T(8,128)} %collective-permute-done.10.refs_1_, ...), custom_call_target="tpu_custom_call" | custom-call | flops 1 | bytes 1 | tf_op jit(solution)/shard_map/pallas_call | solution.py:157
  125.6 6.2 %shard_map.100 = (f32[8,128,512]{2,1,0:T(8,128)S(1)}, f32[2,128,512]{2,1,0:T(8,128)}, f32[2,128,512]{2,1,0:T(8,128)}, f32[2,128,512]{2,1,0:T(8,128)S(1)}, f32[2,...) custom-call(s32[1]{0:T(128)} %bitcast.me_ref, s32[8,1]{1,0:T(8,128)S(1)} %copy.14.near_ref, ...), custom_call_target="tpu_custom_call" | custom-call | flops 1 | bytes 1 | tf_op jit(solution)/shard_map/pallas_call | solution.py:279
  133.3 3.0 %collective-permute-start.14 = (f32[2,128,512]{2,1,0:T(8,128)S(1)}, f32[2,128,512]{2,1,0:T(8,128)S(1)}, u32[]{:S(2)}, u32[]{:S(2)}) collective-permute-start(f32[2,128,512]{2,1,0:T(8,128)S(1)} %get-tuple-element.109), channel_id=1, source_target_pairs={{0,2},{1,3},{2,0},{3,1},{4,6},{5,7},{6,4},{7,5},{8,10},{9,11},{10,... | collective-permute-start | bytes 1572872 | tf_op jit(solution)/shard_map/ppermute | solution.py:332
  139.2 4.3 %shard_map.101.refs_5_ = f32[8,128,512]{2,1,0:T(8,128)S(1)} custom-call(bf16[8,128,1024]{2,1,0:T(8,128)(2,1)S(1)} %copy-done.1, bf16[8,128,1024]{2,1,0:T(8,128)(2,1)S(1)} %copy-done.3, f32[8,128,512]{2,1,0:T(8,128)S(1)} %get-tuple-element.113.refs_0_.x_ref), custom_call_target="tpu_custom_call" | custom-call | flops 1 | bytes 1 | tf_op jit(solution)/shard_map/pallas_call | solution.py:157
  143.5 5.3 %collective-permute-done.12.refs_2_ = f32[2,128,512]{2,1,0:T(8,128)S(1)} collective-permute-done((f32[2,128,512]{2,1,0:T(8,128)}, f32[2,128,512]{2,1,0:T(8,128)S(1)}, u32[]{:S(2)}, u32[]{:S(2)}) %collective-permute-start.12) | collective-permute-done | bytes 524320 | tf_op jit(solution)/shard_map/ppermute | solution.py:332
  148.8 29.3 %collective-permute-done.13.refs_3_ = f32[2,128,512]{2,1,0:T(8,128)S(1)} collective-permute-done((f32[2,128,512]{2,1,0:T(8,128)}, f32[2,128,512]{2,1,0:T(8,128)S(1)}, u32[]{:S(2)}, u32[]{:S(2)}) %collective-permute-start.13) | collective-permute-done | bytes 524320 | tf_op jit(solution)/shard_map/ppermute | solution.py:332
  178.3 4.2 %shard_map.102.acc_ref = f32[8,128,512]{2,1,0:T(8,128)S(1)} custom-call(bf16[8,128,896]{2,1,0:T(8,128)(2,1)S(1)} %copy-done.4, bf16[8,128,896]{2,1,0:T(8,128)(2,1)S(1)} %copy-done.5, f32[2,128,512]{2,1,0:T(8,128)S(1)} %collective-permute-done.15.refs_0_, f32[2,128,512]{2,1,0:T(8,128)S(1)} %collective-permute-done.16.refs_1_, ...), custom_call_target="tpu_custom_call" | custom-call | flops 1 | bytes 1 | tf_op jit(solution)/shard_map/pallas_call | solution.py:157
  182.6 4.8 %shard_map.103 = (f32[8,128,512]{2,1,0:T(8,128)S(1)}, f32[2,128,512]{2,1,0:T(8,128)}, f32[2,128,512]{2,1,0:T(8,128)}, f32[2,128,512]{2,1,0:T(8,128)}, f32[2,128,...) custom-call(s32[1]{0:T(128)} %bitcast.me_ref, s32[8,1]{1,0:T(8,128)S(1)} %copy.14.near_ref, ...), custom_call_target="tpu_custom_call" | custom-call | flops 1 | bytes 1 | tf_op jit(solution)/shard_map/pallas_call | solution.py:279
  194.8 4.2 %shard_map.104.twice_ref = f32[8,128,512]{2,1,0:T(8,128)S(1)} custom-call(bf16[8,128,1024]{2,1,0:T(8,128)(2,1)S(1)} %copy-done.1, bf16[8,128,1024]{2,1,0:T(8,128)(2,1)S(1)} %copy-done.3, f32[8,128,512]{2,1,0:T(8,128)S(1)} %get-tuple-element.127.refs_0_.once_ref), custom_call_target="tpu_custom_call" | custom-call | flops 1 | bytes 1 | tf_op jit(solution)/shard_map/pallas_call | solution.py:157
  199.0 4.0 %shard_map.105.refs_5_ = f32[8,128,512]{2,1,0:T(8,128)S(1)} custom-call(f32[8,128,512]{2,1,0:T(8,128)S(1)} %copy-done.13, f32[8,128,512]{2,1,0:T(8,128)S(1)} %get-tuple-element.127.refs_0_.once_ref, f32[8,128,512]{2,1,0:T(8,128)S(1)} %shard_map.104.twice_ref, bf16[2,512,512]{2,1,0:T(8,128)(2,1)S(1)} %copy-done.17, bf16[2,512,512]{2,1,0:T(8,128)(2,1)S(1)} %copy-done.19, ...), custom_call_target="tpu_custom_call" | custom-call | flops 1 | bytes 1 | tf_op jit(solution)/shard_map/pallas_call | solution.py:179
  204.3 30.5 %collective-permute-done.19.refs_3_ = f32[2,128,512]{2,1,0:T(8,128)S(1)} collective-permute-done((f32[2,128,512]{2,1,0:T(8,128)}, f32[2,128,512]{2,1,0:T(8,128)S(1)}, u32[]{:S(2)}, u32[]{:S(2)}) %collective-permute-start.19) | collective-permute-done | bytes 524320 | tf_op jit(solution)/shard_map/ppermute | solution.py:332
  239.0 6.6 %shard_map.106.acc_ref = f32[8,128,512]{2,1,0:T(8,128)S(1)} custom-call(bf16[8,128,896]{2,1,0:T(8,128)(2,1)S(1)} %copy-done.4, bf16[8,128,896]{2,1,0:T(8,128)(2,1)S(1)} %copy-done.5, f32[2,128,512]{2,1,0:T(8,128)S(1)} %collective-permute-done.21.refs_0_, f32[2,128,512]{2,1,0:T(8,128)} %collective-permute-done.22.refs_1_, f32[2,128,512]{2,1,0:T(8,128)S(1)} %copy-done.22, ...), custom_call_target="tpu_custom_call" | custom-call | flops 1 | bytes 1 | tf_op jit(solution)/shard_map/pallas_call | solution.py:157
  245.6 5.9 %shard_map.107 = f32[8,128,512]{2,1,0:T(8,128)} custom-call(s32[1]{0:T(128)} %bitcast.me_ref, s32[8,1]{1,0:T(8,128)S(1)} %copy.14.near_ref, s32[2,2]{1,0:T(2,128)S(1)} %bitcast.20, bf16[8,128,512]{2,1,0:T(8,128)(2,1)S(1)} %copy-done.9, bf16[8,128,512]{2,1,0:T(8,128)(2,1)S(1)} %copy-done.11, f32[8,128,512]{2,1,0:T(8,128)S(1)} %shard_map.106.acc_ref, ...), custom_call_target="tpu_custom_call" | custom-call | flops 1 | bytes 1 | tf_op jit(solution)/shard_map/pallas_call | solution.py:279
  (126 shorter events, 42.3 us)
Async XLA Ops:
  5.4 32.4 %collective-permute-start = (f32[2,128,512]{2,1,0:T(8,128)}, f32[2,128,512]{2,1,0:T(8,128)}, u32[]{:S(2)}, u32[]{:S(2)}) collective-permute-start(f32[2,128,512]{2,1,0:T(8,128)} %get-tuple-element.74), channel_id=1, source_target_pairs={{0,6},{1,7},{2,4},{3,5},{4,2},{5,3},{6,0},{7,1},{8,14},{9,15},{10,... | collective-permute-start | bytes 1572872 | tf_op jit(solution)/shard_map/ppermute | solution.py:332
  10.5 45.1 %collective-permute-start.1 = (f32[2,128,512]{2,1,0:T(8,128)}, f32[2,128,512]{2,1,0:T(8,128)}, u32[]{:S(2)}, u32[]{:S(2)}) collective-permute-start(f32[2,128,512]{2,1,0:T(8,128)} %get-tuple-element.75), channel_id=1, source_target_pairs={{0,4},{1,5},{2,6},{3,7},{4,0},{5,1},{6,2},{7,3},{8,12},{9,13},{10,... | collective-permute-start | bytes 1572872 | tf_op jit(solution)/shard_map/ppermute | solution.py:332
  10.5 45.1 %collective-permute-start.2 = (f32[2,128,512]{2,1,0:T(8,128)}, f32[2,128,512]{2,1,0:T(8,128)}, u32[]{:S(2)}, u32[]{:S(2)}) collective-permute-start(f32[2,128,512]{2,1,0:T(8,128)} %get-tuple-element.76), channel_id=1, source_target_pairs={{0,2},{1,3},{2,0},{3,1},{4,6},{5,7},{6,4},{7,5},{8,10},{9,11},{10,... | collective-permute-start | bytes 1572872 | tf_op jit(solution)/shard_map/ppermute | solution.py:332
  11.1 44.5 %collective-permute-start.3 = (f32[2,128,512]{2,1,0:T(8,128)}, f32[2,128,512]{2,1,0:T(8,128)}, u32[]{:S(2)}, u32[]{:S(2)}) collective-permute-start(f32[2,128,512]{2,1,0:T(8,128)} %get-tuple-element.77), channel_id=1, source_target_pairs={{0,8},{8,16},{16,24},{24,0},{1,9},{9,17},{17,25},{25,1},{2,10},{10... | collective-permute-start | bytes 1572872 | tf_op jit(solution)/shard_map/ppermute | solution.py:340
  12.8 42.8 %collective-permute-start.4 = (f32[2,128,512]{2,1,0:T(8,128)}, f32[2,128,512]{2,1,0:T(8,128)}, u32[]{:S(2)}, u32[]{:S(2)}) collective-permute-start(f32[2,128,512]{2,1,0:T(8,128)} %get-tuple-element.78), channel_id=1, source_target_pairs={{8,0},{16,8},{24,16},{0,24},{9,1},{17,9},{25,17},{1,25},{10,2},{18... | collective-permute-start | bytes 1572872 | tf_op jit(solution)/shard_map/ppermute | solution.py:341
  58.6 6.0 %collective-permute-start.5 = (f32[4,128,512]{2,1,0:T(8,128)S(1)}, f32[4,128,512]{2,1,0:T(8,128)S(1)}, u32[]{:S(2)}, u32[]{:S(2)}) collective-permute-start(f32[4,128,512]{2,1,0:T(8,128)S(1)} %pad_maximum_fusion), channel_id=1, source_target_pairs={{0,1},{1,0},{2,3},{3,2},{4,5},{5,4},{6,7},{7,6},{8,9},{9,8},{10,11... | collective-permute-start | bytes 3145736 | tf_op jit(solution)/shard_map/ppermute | solution.py:332
  69.5 21.4 %collective-permute-start.6 = (f32[2,128,512]{2,1,0:T(8,128)}, f32[2,128,512]{2,1,0:T(8,128)S(1)}, u32[]{:S(2)}, u32[]{:S(2)}) collective-permute-start(f32[2,128,512]{2,1,0:T(8,128)} %get-tuple-element.89), channel_id=1, source_target_pairs={{0,6},{1,7},{2,4},{3,5},{4,2},{5,3},{6,0},{7,1},{8,14},{9,15},{10,... | collective-permute-start | bytes 1572872 | tf_op jit(solution)/shard_map/ppermute | solution.py:332
  72.0 44.8 %collective-permute-start.7 = (f32[2,128,512]{2,1,0:T(8,128)}, f32[2,128,512]{2,1,0:T(8,128)S(1)}, u32[]{:S(2)}, u32[]{:S(2)}) collective-permute-start(f32[2,128,512]{2,1,0:T(8,128)} %get-tuple-element.90), channel_id=1, source_target_pairs={{0,4},{1,5},{2,6},{3,7},{4,0},{5,1},{6,2},{7,3},{8,12},{9,13},{10,... | collective-permute-start | bytes 1572872 | tf_op jit(solution)/shard_map/ppermute | solution.py:332
  72.0 44.8 %collective-permute-start.8 = (f32[2,128,512]{2,1,0:T(8,128)}, f32[2,128,512]{2,1,0:T(8,128)S(1)}, u32[]{:S(2)}, u32[]{:S(2)}) collective-permute-start(f32[2,128,512]{2,1,0:T(8,128)} %get-tuple-element.91), channel_id=1, source_target_pairs={{0,2},{1,3},{2,0},{3,1},{4,6},{5,7},{6,4},{7,5},{8,10},{9,11},{10,... | collective-permute-start | bytes 1572872 | tf_op jit(solution)/shard_map/ppermute | solution.py:332
  73.9 42.9 %collective-permute-start.9 = (f32[2,128,512]{2,1,0:T(8,128)}, f32[2,128,512]{2,1,0:T(8,128)}, u32[]{:S(2)}, u32[]{:S(2)}) collective-permute-start(f32[2,128,512]{2,1,0:T(8,128)} %get-tuple-element.92), channel_id=1, source_target_pairs={{0,8},{8,16},{16,24},{24,0},{1,9},{9,17},{17,25},{25,1},{2,10},{10... | collective-permute-start | bytes 1572872 | tf_op jit(solution)/shard_map/ppermute | solution.py:340
  75.4 41.4 %collective-permute-start.10 = (f32[2,128,512]{2,1,0:T(8,128)}, f32[2,128,512]{2,1,0:T(8,128)}, u32[]{:S(2)}, u32[]{:S(2)}) collective-permute-start(f32[2,128,512]{2,1,0:T(8,128)} %get-tuple-element.93), channel_id=1, source_target_pairs={{8,0},{16,8},{24,16},{0,24},{9,1},{17,9},{25,17},{1,25},{10,2},{18... | collective-permute-start | bytes 1572872 | tf_op jit(solution)/shard_map/ppermute | solution.py:341
  117.6 8.0 %collective-permute-start.11 = (f32[4,128,512]{2,1,0:T(8,128)S(1)}, f32[4,128,512]{2,1,0:T(8,128)S(1)}, u32[]{:S(2)}, u32[]{:S(2)}) collective-permute-start(f32[4,128,512]{2,1,0:T(8,128)S(1)} %pad_maximum_fusion.1), channel_id=1, source_target_pairs={{0,1},{1,0},{2,3},{3,2},{4,5},{5,4},{6,7},{7,6},{8,9},{9,8},{10,11... | collective-permute-start | bytes 3145736 | tf_op jit(solution)/shard_map/ppermute | solution.py:332
  131.8 17.0 %collective-permute-start.12 = (f32[2,128,512]{2,1,0:T(8,128)}, f32[2,128,512]{2,1,0:T(8,128)S(1)}, u32[]{:S(2)}, u32[]{:S(2)}) collective-permute-start(f32[2,128,512]{2,1,0:T(8,128)} %get-tuple-element.107), channel_id=1, source_target_pairs={{0,6},{1,7},{2,4},{3,5},{4,2},{5,3},{6,0},{7,1},{8,14},{9,15},{10,... | collective-permute-start | bytes 1572872 | tf_op jit(solution)/shard_map/ppermute | solution.py:332
  133.2 44.8 %collective-permute-start.13 = (f32[2,128,512]{2,1,0:T(8,128)}, f32[2,128,512]{2,1,0:T(8,128)S(1)}, u32[]{:S(2)}, u32[]{:S(2)}) collective-permute-start(f32[2,128,512]{2,1,0:T(8,128)} %get-tuple-element.108), channel_id=1, source_target_pairs={{0,4},{1,5},{2,6},{3,7},{4,0},{5,1},{6,2},{7,3},{8,12},{9,13},{10,... | collective-permute-start | bytes 1572872 | tf_op jit(solution)/shard_map/ppermute | solution.py:332
  133.3 44.8 %collective-permute-start.14 = (f32[2,128,512]{2,1,0:T(8,128)S(1)}, f32[2,128,512]{2,1,0:T(8,128)S(1)}, u32[]{:S(2)}, u32[]{:S(2)}) collective-permute-start(f32[2,128,512]{2,1,0:T(8,128)S(1)} %get-tuple-element.109), channel_id=1, source_target_pairs={{0,2},{1,3},{2,0},{3,1},{4,6},{5,7},{6,4},{7,5},{8,10},{9,11},{10,... | collective-permute-start | bytes 1572872 | tf_op jit(solution)/shard_map/ppermute | solution.py:332
  136.3 41.8 %collective-permute-start.15 = (f32[2,128,512]{2,1,0:T(8,128)S(1)}, f32[2,128,512]{2,1,0:T(8,128)S(1)}, u32[]{:S(2)}, u32[]{:S(2)}) collective-permute-start(f32[2,128,512]{2,1,0:T(8,128)S(1)} %get-tuple-element.110), channel_id=1, source_target_pairs={{0,8},{8,16},{16,24},{24,0},{1,9},{9,17},{17,25},{25,1},{2,10},{10... | collective-permute-start | bytes 1572872 | tf_op jit(solution)/shard_map/ppermute | solution.py:340
  137.8 40.3 %collective-permute-start.16 = (f32[2,128,512]{2,1,0:T(8,128)S(1)}, f32[2,128,512]{2,1,0:T(8,128)S(1)}, u32[]{:S(2)}, u32[]{:S(2)}) collective-permute-start(f32[2,128,512]{2,1,0:T(8,128)S(1)} %get-tuple-element.111), channel_id=1, source_target_pairs={{8,0},{16,8},{24,16},{0,24},{9,1},{17,9},{25,17},{1,25},{10,2},{18... | collective-permute-start | bytes 1572872 | tf_op jit(solution)/shard_map/ppermute | solution.py:341
  178.2 4.3 %collective-permute-start.17 = (f32[4,128,512]{2,1,0:T(8,128)S(1)}, f32[4,128,512]{2,1,0:T(8,128)S(1)}, u32[]{:S(2)}, u32[]{:S(2)}) collective-permute-start(f32[4,128,512]{2,1,0:T(8,128)S(1)} %pad_maximum_fusion.2), channel_id=1, source_target_pairs={{0,1},{1,0},{2,3},{3,2},{4,5},{5,4},{6,7},{7,6},{8,9},{9,8},{10,11... | collective-permute-start | bytes 3145736 | tf_op jit(solution)/shard_map/ppermute | solution.py:332
  187.4 16.9 %collective-permute-start.18 = (f32[2,128,512]{2,1,0:T(8,128)}, f32[2,128,512]{2,1,0:T(8,128)S(1)}, u32[]{:S(2)}, u32[]{:S(2)}) collective-permute-start(f32[2,128,512]{2,1,0:T(8,128)} %get-tuple-element.121), channel_id=1, source_target_pairs={{0,6},{1,7},{2,4},{3,5},{4,2},{5,3},{6,0},{7,1},{8,14},{9,15},{10,... | collective-permute-start | bytes 1572872 | tf_op jit(solution)/shard_map/ppermute | solution.py:332
  189.9 44.9 %collective-permute-start.19 = (f32[2,128,512]{2,1,0:T(8,128)}, f32[2,128,512]{2,1,0:T(8,128)S(1)}, u32[]{:S(2)}, u32[]{:S(2)}) collective-permute-start(f32[2,128,512]{2,1,0:T(8,128)} %get-tuple-element.122), channel_id=1, source_target_pairs={{0,4},{1,5},{2,6},{3,7},{4,0},{5,1},{6,2},{7,3},{8,12},{9,13},{10,... | collective-permute-start | bytes 1572872 | tf_op jit(solution)/shard_map/ppermute | solution.py:332
  189.9 44.9 %collective-permute-start.20 = (f32[2,128,512]{2,1,0:T(8,128)}, f32[2,128,512]{2,1,0:T(8,128)S(1)}, u32[]{:S(2)}, u32[]{:S(2)}) collective-permute-start(f32[2,128,512]{2,1,0:T(8,128)} %get-tuple-element.123), channel_id=1, source_target_pairs={{0,2},{1,3},{2,0},{3,1},{4,6},{5,7},{6,4},{7,5},{8,10},{9,11},{10,... | collective-permute-start | bytes 1572872 | tf_op jit(solution)/shard_map/ppermute | solution.py:332
  191.8 43.0 %collective-permute-start.21 = (f32[2,128,512]{2,1,0:T(8,128)}, f32[2,128,512]{2,1,0:T(8,128)S(1)}, u32[]{:S(2)}, u32[]{:S(2)}) collective-permute-start(f32[2,128,512]{2,1,0:T(8,128)} %get-tuple-element.124), channel_id=1, source_target_pairs={{0,8},{8,16},{16,24},{24,0},{1,9},{9,17},{17,25},{25,1},{2,10},{10... | collective-permute-start | bytes 1572872 | tf_op jit(solution)/shard_map/ppermute | solution.py:340
  193.3 41.6 %collective-permute-start.22 = (f32[2,128,512]{2,1,0:T(8,128)}, f32[2,128,512]{2,1,0:T(8,128)}, u32[]{:S(2)}, u32[]{:S(2)}) collective-permute-start(f32[2,128,512]{2,1,0:T(8,128)} %get-tuple-element.125), channel_id=1, source_target_pairs={{8,0},{16,8},{24,16},{0,24},{9,1},{17,9},{25,17},{1,25},{10,2},{18... | collective-permute-start | bytes 1572872 | tf_op jit(solution)/shard_map/ppermute | solution.py:341
  235.9 9.7 %collective-permute-start.23 = (f32[4,128,512]{2,1,0:T(8,128)S(1)}, f32[4,128,512]{2,1,0:T(8,128)S(1)}, u32[]{:S(2)}, u32[]{:S(2)}) collective-permute-start(f32[4,128,512]{2,1,0:T(8,128)S(1)} %pad_maximum_fusion.3), channel_id=1, source_target_pairs={{0,1},{1,0},{2,3},{3,2},{4,5},{5,4},{6,7},{7,6},{8,9},{9,8},{10,11... | collective-permute-start | bytes 3145736 | tf_op jit(solution)/shard_map/ppermute | solution.py:332
  (33 other events, 253.7 us)
where the time goes:
time: 252 us
  waiting for transfers between devices  110 us (44%)
  Pallas kernels  85.7 us (34%)
  starting transfers between devices  31 us (12%)
  local copies, waits for them, and re-layouts  17.4 us (7%)
  between operations  6.29 us (2%)
    ppermute x16, waiting for transfers between devices, swap(): return lax.ppermute(x, 'dev', [(i, i ^ k) for i in range(peers)])  110 us
    pallas_call x8, Pallas kernels, apply_dense(): pl.pallas_call(functools.partial(apply_kernel, len(xs), acc is not None,...  40.4 us
    pallas_call x4, Pallas kernels, finish(): pl.pallas_call(functools.partial(finish_kernel, plan, len(xs), bool(squar...  21.6 us
    ppermute x16, starting transfers between devices, swap(): return lax.ppermute(x, 'dev', [(i, i ^ k) for i in range(peers)])  19.3 us
    unnamed x66, local copies, waits for them, and re-layouts  12.9 us
    pallas_call x1, Pallas kernels, dense_adjacency(): pl.pallas_call(dense_kernel, out_shape=out_shape, in_specs=[smem(), smem(...  9.27 us
    pallas_call x2, Pallas kernels, mix(): pl.pallas_call(mix_kernel, grid=(x.shape[0] // STEP,), out_shape=jax.Shap...  7.97 us
    ppermute x4, starting transfers between devices, start(): lower = lax.ppermute(sends[n], 'dom', up)  6.1 us
  transfers between devices with their start and end apart: 24, of which 6 were waited for; matrix products, arithmetic and copies ran while one was open for 1% of the time, Pallas kernels for 25%

commit v1 on v0

--- a/solution.py
+++ b/solution.py
@@ -68,13 +68,14 @@
     out_shape = []
     for w in widths:
         out_shape += [jax.ShapeDtypeStruct((row_blocks, TILE, w * TILE), jnp.bfloat16)] * 2
+    need = 4 * TILE * TILE * (tile_vals.shape[0] + 2 * row_blocks * sum(widths))
     flat = pl.pallas_call(
         dense_kernel,
         out_shape=out_shape,
         in_specs=[smem(), smem(), smem(), vmem],
         out_specs=[vmem] * len(out_shape),
         scratch_shapes=[pltpu.VMEM((row_blocks, sum(widths), TILE, TILE), jnp.float32)],
-        compiler_params=pltpu.CompilerParams(vmem_limit_bytes=60 * MIB),
+        compiler_params=pltpu.CompilerParams(vmem_limit_bytes=need + 4 * MIB),
         cost_estimate=SMALL,
     )(tile_rows, places, tile_count, tile_vals)
     return [(flat[2 * g], flat[2 * g + 1]) for g in range(len(widths))]
@@ -98,7 +99,7 @@
         out_shape=[jax.ShapeDtypeStruct(skew_raw.shape, jnp.bfloat16)] * 4,
         in_specs=[block],
         out_specs=[block] * 4,
-        compiler_params=pltpu.CompilerParams(vmem_limit_bytes=40 * MIB),
+        compiler_params=pltpu.CompilerParams(vmem_limit_bytes=24 * MIB),
         cost_estimate=SMALL,
     )(skew_raw)
 
@@ -161,7 +162,7 @@
         in_specs=specs,
         out_specs=rows_of(out.shape),
         scratch_shapes=[pltpu.VMEM((depth, width), jnp.bfloat16)] * 2,
-        compiler_params=pltpu.CompilerParams(vmem_limit_bytes=40 * MIB),
+        compiler_params=pltpu.CompilerParams(vmem_limit_bytes=24 * MIB),
         cost_estimate=SMALL,
     )(*args)
 
@@ -182,7 +183,7 @@
         out_shape=jax.ShapeDtypeStruct(x.shape, jnp.float32),
         in_specs=[block] * 3 + [of_layer(w) for w in factors],
         out_specs=block,
-        compiler_params=pltpu.CompilerParams(vmem_limit_bytes=40 * MIB),
+        compiler_params=pltpu.CompilerParams(vmem_limit_bytes=24 * MIB),
         cost_estimate=SMALL,
     )(x, once, twice, *[w for w, _ in factors])
 
@@ -283,7 +284,7 @@
         in_specs=specs,
         out_specs=[rows_of(acc.shape)] + [pl.BlockSpec(memory_space=pl.ANY)] * len(sizes),
         scratch_shapes=scratch,
-        compiler_params=pltpu.CompilerParams(vmem_limit_bytes=40 * MIB),
+        compiler_params=pltpu.CompilerParams(vmem_limit_bytes=24 * MIB),
         cost_estimate=SMALL,
     )(*args)
 
@@ -301,19 +302,22 @@
     d = lax.axis_index("dev")
     me = d.astype(jnp.int32).reshape(1)
 
-    chips = list(range(1, peers // 2))[::-1]
+    late = list(range(peers // 4, peers // 2))[::-1]
+    early = list(range(1, peers // 4))
     plan = tuple(
-        [(("near", 2 * j), ("near", 2 * j + 1)) for j in chips]
+        [(("near", 2 * j), ("near", 2 * j + 1)) for j in late + early]
         + [(("far", 0),), (("far", 1),), (("near", 1),)]
     )
     route = (plan, me, near_send[0], far_send[0])
 
-    widths = (row_blocks, 2 * hcap + cap * len(chips), cap * (1 + len(chips)))
+    early_k = [2 * j for j in early] + [1] + [2 * j + 1 for j in early]
+    late_k = [2 * j for j in late] + [2 * j + 1 for j in late]
+    widths = (row_blocks, 2 * hcap + cap * len(early_k), cap * len(late_k))
     place_of = [0] * peers
-    for at, j in enumerate(chips):
-        place_of[2 * j] = row_blocks + 2 * hcap + at * cap
-    for at, j in enumerate([0] + chips):
-        place_of[2 * j + 1] = row_blocks + widths[1] + at * cap
+    for at, k in enumerate(early_k):
+        place_of[k] = row_blocks + 2 * hcap + at * cap
+    for at, k in enumerate(late_k):
+        place_of[k] = row_blocks + widths[1] + at * cap
     slot = tile_cols
     near_at = slot - row_blocks
     source, item = near_at // cap, near_at % cap
@@ -326,7 +330,7 @@
         slot < row_blocks, slot, jnp.where(slot < row_blocks + peers * cap, near_place, far_place)
     ).astype(jnp.int32)
 
-    own_a, direct_a, core_a = dense_adjacency(tile_rows, places, tile_count, tile_vals, row_blocks, widths)
+    own_a, early_a, late_a = dense_adjacency(tile_rows, places, tile_count, tile_vals, row_blocks, widths)
 
     def swap(x, k):
         return lax.ppermute(x, "dev", [(i, i ^ k) for i in range(peers)])
@@ -335,18 +339,21 @@
     down = [(j, i) for i, j in up]
 
     def start(sends):
-        n = len(chips)
-        near = [swap(s, 2 * j) for s, j in zip(sends[:n], chips)]
-        lower = lax.ppermute(sends[n], "dom", up)
-        upper = lax.ppermute(sends[n + 1], "dom", down)
-        return near, lower, upper, sends[n + 2]
+        chips = late + early
+        near = [swap(s, 2 * j) for s, j in zip(sends, chips)]
+        lower = lax.ppermute(sends[len(chips)], "dom", up)
+        upper = lax.ppermute(sends[len(chips) + 1], "dom", down)
+        return near[: len(late)], near[len(late) :], lower, upper, sends[-1]
 
     def arrive(flight, acc, square=()):
-        near, lower, upper, to_core = flight
-        near, (lower, upper, to_core, acc) = tie(near, lower, upper, to_core, acc)
-        passed = swap(jnp.concatenate([to_core] + [r[cap:] for r in near], axis=0), 1)
-        direct = [(lower, hcap), (upper, hcap)] + [(r, cap) for r in near]
-        return apply_dense(direct_a, direct, acc, square), [(passed, passed.shape[0])]
+        long, short, lower, upper, to_core = flight
+        (to_core, *short), (lower, upper, acc) = tie([to_core] + short, lower, upper, acc)
+        across = [swap(to_core, 1)] + [swap(r[cap:], 1) for r in short]
+        arrived = [(lower, hcap), (upper, hcap)] + [(r, cap) for r in short + across]
+        acc = apply_dense(early_a, arrived, acc, square)
+        long, (acc,) = tie(long, acc)
+        passed = swap(jnp.concatenate([r[cap:] for r in long], axis=0), 1)
+        return acc, [(r, cap) for r in long] + [(passed, passed.shape[0])]
 
     current = features.reshape(row_blocks, TILE, width)
     sends = pick(current, route)
@@ -355,12 +362,12 @@
     for layer in range(layers):
         flight = start(sends)
         skew, square = [(w, layer) for w in parts[:2]], [(w, layer) for w in parts[2:]]
-        acc, passed = arrive(flight, apply_dense(own_a, [(current, row_blocks)]))
-        once, *sends = finish(core_a, passed, acc, route)
+        acc, arrived = arrive(flight, apply_dense(own_a, [(current, row_blocks)]))
+        once, *sends = finish(late_a, arrived, acc, route)
         flight = start(sends)
         base = mix(current, once, apply_dense(own_a, [(once, row_blocks)]), skew, square)
-        base, passed = arrive(flight, base, square)
-        current, *sends = finish(core_a, passed, base, route, square, layer < layers - 1)
+        base, arrived = arrive(flight, base, square)
+        current, *sends = finish(late_a, arrived, base, route, square, layer < layers - 1)
     return current.reshape(features.shape)
 
 

time: 252 us -> 239 us (0.948)
  waiting for transfers between devices: 110 us -> 123 us
  Pallas kernels: 85.7 us -> 73.4 us
  local copies, waits for them, and re-layouts: 17.4 us -> 6.46 us
    ppermute x8, waiting for transfers between devices: 0.02 us -> 34.1 us  [the longest x4 31.3 us: start(): upper = lax.ppermute(sends[len(chips) + 1], 'dom', down)]
    ppermute x16 -> x24, waiting for transfers between devices: 110 us -> 88.4 us  [swap(): return lax.ppermute(x, 'dev', [(i, i ^ k) for i in range(peers)])]
    unnamed x66 -> x18, local copies, waits for them, and re-layouts: 12.9 us -> 4.78 us
    pallas_call x1, Pallas kernels: 9.27 us -> 4.09 us  [dense_adjacency(): pl.pallas_call(dense_kernel, out_shape=out_shape, in_specs=[smem(), smem(...]
    pallas_call x8, Pallas kernels: 40.4 us -> 36.8 us  [apply_dense(): pl.pallas_call(functools.partial(apply_kernel, len(xs), acc is not None,...]
    pallas_call x4, Pallas kernels: 21.6 us -> 18.3 us  [finish(): pl.pallas_call(functools.partial(finish_kernel, plan, len(xs), bool(squar...]
    slice x12, local copies, waits for them, and re-layouts: 3.08 us -> 0.22 us  [the longest x8 0.15 us: arrive(): passed = swap(jnp.concatenate([r[cap:] for r in long], axis=0), 1)]
    ppermute x16 -> x24, starting transfers between devices: 19.3 us -> 18.7 us  [swap(): return lax.ppermute(x, 'dev', [(i, i ^ k) for i in range(peers)])]
  transfers between devices with their start and end apart: 24 -> 32, of which waited for: 6 -> 23; matrix products, arithmetic and copies ran while one was open for 1% -> 0% of each run, Pallas kernels for 25% -> 22%
where the time goes in v1:
time: 239 us
  waiting for transfers between devices  123 us (51%)
  Pallas kernels  73.4 us (31%)
  starting transfers between devices  30.6 us (13%)
  local copies, waits for them, and re-layouts  6.46 us (3%)
  between operations  6.08 us (3%)
    ppermute x24, waiting for transfers between devices, swap(): return lax.ppermute(x, 'dev', [(i, i ^ k) for i in range(peers)])  88.4 us
    pallas_call x8, Pallas kernels, apply_dense(): pl.pallas_call(functools.partial(apply_kernel, len(xs), acc is not None,...  36.8 us
    ppermute x4, waiting for transfers between devices, start(): upper = lax.ppermute(sends[len(chips) + 1], 'dom', down)  31.3 us
    ppermute x24, starting transfers between devices, swap(): return lax.ppermute(x, 'dev', [(i, i ^ k) for i in range(peers)])  18.7 us
    pallas_call x4, Pallas kernels, finish(): pl.pallas_call(functools.partial(finish_kernel, plan, len(xs), bool(squar...  18.3 us
    ppermute x4, starting transfers between devices, start(): upper = lax.ppermute(sends[len(chips) + 1], 'dom', down)  8.94 us
    pallas_call x2, Pallas kernels, mix(): pl.pallas_call(mix_kernel, grid=(x.shape[0] // STEP,), out_shape=jax.Shap...  8.11 us
  transfers between devices with their start and end apart: 32, of which 23 were waited for; matrix products, arithmetic and copies ran while one was open for 0% of the time, Pallas kernels for 22%

profile of v1, /device:TPU:0, one launch (start us, length us, event | category | flops | bytes accessed | tf_op | source)
XLA Modules:
  0.0 239.2 jit_solution(15451753204729056828)
XLA Ops:
  22.6 4.1 %shard_map.91 = (bf16[8,128,1024]{2,1,0:T(8,128)(2,1)S(1)}, bf16[8,128,1024]{2,1,0:T(8,128)(2,1)S(1)}, bf16[8,128,896]{2,1,0:T(8,128)(2,1)S(1)}, bf16[8,128,896]...) custom-call(s32[80]{0:T(128)S(1)} %copy-done.6, ...), custom_call_target="tpu_custom_call" | custom-call | flops 1 | bytes 1 | tf_op jit(solution)/shard_map/pallas_call | solution.py:72
  26.7 4.3 %shard_map.93.refs_5_ = f32[8,128,512]{2,1,0:T(8,128)S(1)} custom-call(bf16[8,128,1024]{2,1,0:T(8,128)(2,1)S(1)} %get-tuple-element.84.ah_ref, bf16[8,128,1024]{2,1,0:T(8,128)(2,1)S(1)} %get-tuple-element.85.al_ref, f32[8,128,512]{2,1,0:T(8,128)S(1)} %bitcast.14), custom_call_target="tpu_custom_call" | custom-call | flops 1 | bytes 1 | tf_op jit(solution)/shard_map/pallas_call | solution.py:158
  36.0 4.3 %shard_map.94.acc_ref = f32[8,128,512]{2,1,0:T(8,128)S(1)} custom-call(bf16[8,128,896]{2,1,0:T(8,128)(2,1)S(1)} %get-tuple-element.78.ah_ref, bf16[8,128,896]{2,1,0:T(8,128)(2,1)S(1)} %get-tuple-element.79.al_ref, f32[2,128,512]{2,1,0:T(8,128)S(1)} %collective-permute-done.3.refs_0_, f32[2,128,512]{2,1,0:T(8,128)S(1)} %collective-permute-done.4.refs_1_, ...), custom_call_target="tpu_custom_call" | custom-call | flops 1 | bytes 1 | tf_op jit(solution)/shard_map/pallas_call | solution.py:158
  40.3 18.4 %collective-permute-done.1.refs_1_ = f32[2,128,512]{2,1,0:T(8,128)S(1)} collective-permute-done((f32[2,128,512]{2,1,0:T(8,128)S(1)}, f32[2,128,512]{2,1,0:T(8,128)S(1)}, u32[]{:S(2)}, u32[]{:S(2)}) %collective-permute-start.1) | collective-permute-done | bytes 524320 | tf_op jit(solution)/shard_map/ppermute | solution.py:336
  60.8 3.5 %shard_map.95 = (f32[8,128,512]{2,1,0:T(8,128)S(1)}, f32[2,128,512]{2,1,0:T(8,128)S(1)}, f32[2,128,512]{2,1,0:T(8,128)S(1)}, f32[2,128,512]{2,1,0:T(8,128)S(1)},...) custom-call(s32[1]{0:T(128)} %bitcast.me_ref, s32[8,1]{1,0:T(8,128)S(1)} %copy.14.near_ref, ...), custom_call_target="tpu_custom_call" | custom-call | flops 1 | bytes 1 | tf_op jit(solution)/shard_map/pallas_call | solution.py:280
  70.8 4.1 %shard_map.97 = (bf16[2,512,512]{2,1,0:T(8,128)(2,1)S(1)}, bf16[2,512,512]{2,1,0:T(8,128)(2,1)S(1)}, bf16[2,512,512]{2,1,0:T(8,128)(2,1)S(1)}, bf16[2,512,512]{2,1,0:T(8,128)(2,1)S(1)}) custom-call(f32[2,512,512]{2,1,0:T(8,128)S(1)} %copy-done.3), custom_call_target="tpu_custom_call" | custom-call | flops 1 | bytes 1 | tf_op jit(solution)/shard_map/pallas_call | solution.py:96
  74.9 4.3 %shard_map.96.twice_ref = f32[8,128,512]{2,1,0:T(8,128)S(1)} custom-call(bf16[8,128,1024]{2,1,0:T(8,128)(2,1)S(1)} %get-tuple-element.84.ah_ref, bf16[8,128,1024]{2,1,0:T(8,128)(2,1)S(1)} %get-tuple-element.85.al_ref, f32[8,128,512]{2,1,0:T(8,128)S(1)} %get-tuple-element.100.refs_0_.once_ref), custom_call_target="tpu_custom_call" | custom-call | flops 1 | bytes 1 | tf_op jit(solution)/shard_map/pallas_call | solution.py:158
  79.2 4.0 %shard_map.98.refs_5_ = f32[8,128,512]{2,1,0:T(8,128)S(1)} custom-call(f32[8,128,512]{2,1,0:T(8,128)S(1)} %bitcast.15, f32[8,128,512]{2,1,0:T(8,128)S(1)} %get-tuple-element.100.refs_0_.once_ref, f32[8,128,512]{2,1,0:T(8,128)S(1)} %shard_map.96.twice_ref, bf16[2,512,512]{2,1,0:T(8,128)(2,1)S(1)} %get-tuple-element.101.sh_ref, ...), custom_call_target="tpu_custom_call" | custom-call | flops 1 | bytes 1 | tf_op jit(solution)/shard_map/pallas_call | solution.py:180
  83.3 7.3 %collective-permute-done.12.refs_1_ = f32[2,128,512]{2,1,0:T(8,128)S(1)} collective-permute-done((f32[2,128,512]{2,1,0:T(8,128)S(1)}, f32[2,128,512]{2,1,0:T(8,128)S(1)}, u32[]{:S(2)}, u32[]{:S(2)}) %collective-permute-start.12) | collective-permute-done | bytes 524320 | tf_op jit(solution)/shard_map/ppermute | solution.py:345
  92.6 5.6 %shard_map.99.acc_ref = f32[8,128,512]{2,1,0:T(8,128)S(1)} custom-call(bf16[8,128,896]{2,1,0:T(8,128)(2,1)S(1)} %get-tuple-element.78.ah_ref, bf16[8,128,896]{2,1,0:T(8,128)(2,1)S(1)} %get-tuple-element.79.al_ref, f32[2,128,512]{2,1,0:T(8,128)S(1)} %collective-permute-done.11.refs_0_, f32[2,128,512]{2,1,0:T(8,128)S(1)} %collective-permute-done.12.refs_1_, ...), custom_call_target="tpu_custom_call" | custom-call | flops 1 | bytes 1 | tf_op jit(solution)/shard_map/pallas_call | solution.py:158
  98.2 17.4 %collective-permute-done.9.refs_1_ = f32[2,128,512]{2,1,0:T(8,128)S(1)} collective-permute-done((f32[2,128,512]{2,1,0:T(8,128)S(1)}, f32[2,128,512]{2,1,0:T(8,128)S(1)}, u32[]{:S(2)}, u32[]{:S(2)}) %collective-permute-start.9) | collective-permute-done | bytes 524320 | tf_op jit(solution)/shard_map/ppermute | solution.py:336
  117.7 5.4 %shard_map.100 = (f32[8,128,512]{2,1,0:T(8,128)S(1)}, f32[2,128,512]{2,1,0:T(8,128)S(1)}, f32[2,128,512]{2,1,0:T(8,128)S(1)}, f32[2,128,512]{2,1,0:T(8,128)S(1)}...) custom-call(s32[1]{0:T(128)} %bitcast.me_ref, s32[8,1]{1,0:T(8,128)S(1)} %copy.14.near_ref, ...), custom_call_target="tpu_custom_call" | custom-call | flops 1 | bytes 1 | tf_op jit(solution)/shard_map/pallas_call | solution.py:280
  129.6 4.3 %shard_map.101.refs_5_ = f32[8,128,512]{2,1,0:T(8,128)S(1)} custom-call(bf16[8,128,1024]{2,1,0:T(8,128)(2,1)S(1)} %get-tuple-element.84.ah_ref, bf16[8,128,1024]{2,1,0:T(8,128)(2,1)S(1)} %get-tuple-element.85.al_ref, f32[8,128,512]{2,1,0:T(8,128)S(1)} %get-tuple-element.119.refs_0_.x_ref), custom_call_target="tpu_custom_call" | custom-call | flops 1 | bytes 1 | tf_op jit(solution)/shard_map/pallas_call | solution.py:158
  133.8 3.3 %collective-permute-done.18.refs_2_ = f32[2,128,512]{2,1,0:T(8,128)S(1)} collective-permute-done((f32[2,128,512]{2,1,0:T(8,128)S(1)}, f32[2,128,512]{2,1,0:T(8,128)S(1)}, u32[]{:S(2)}, u32[]{:S(2)}) %collective-permute-start.18) | collective-permute-done | bytes 524320 | tf_op jit(solution)/shard_map/ppermute | solution.py:336
  138.9 10.5 %collective-permute-done.20.refs_1_ = f32[2,128,512]{2,1,0:T(8,128)S(1)} collective-permute-done((f32[2,128,512]{2,1,0:T(8,128)S(1)}, f32[2,128,512]{2,1,0:T(8,128)S(1)}, u32[]{:S(2)}, u32[]{:S(2)}) %collective-permute-start.20) | collective-permute-done | bytes 524320 | tf_op jit(solution)/shard_map/ppermute | solution.py:345
  151.4 4.3 %shard_map.102.acc_ref = f32[8,128,512]{2,1,0:T(8,128)S(1)} custom-call(bf16[8,128,896]{2,1,0:T(8,128)(2,1)S(1)} %get-tuple-element.78.ah_ref, bf16[8,128,896]{2,1,0:T(8,128)(2,1)S(1)} %get-tuple-element.79.al_ref, f32[2,128,512]{2,1,0:T(8,128)S(1)} %collective-permute-done.19.refs_0_, f32[2,128,512]{2,1,0:T(8,128)S(1)} %collective-permute-done.20.refs_1_, ...), custom_call_target="tpu_custom_call" | custom-call | flops 1 | bytes 1 | tf_op jit(solution)/shard_map/pallas_call | solution.py:158
  155.7 18.7 %collective-permute-done.17.refs_1_ = f32[2,128,512]{2,1,0:T(8,128)S(1)} collective-permute-done((f32[2,128,512]{2,1,0:T(8,128)S(1)}, f32[2,128,512]{2,1,0:T(8,128)S(1)}, u32[]{:S(2)}, u32[]{:S(2)}) %collective-permute-start.17) | collective-permute-done | bytes 524320 | tf_op jit(solution)/shard_map/ppermute | solution.py:336
  176.5 3.5 %shard_map.103 = (f32[8,128,512]{2,1,0:T(8,128)S(1)}, f32[2,128,512]{2,1,0:T(8,128)S(1)}, f32[2,128,512]{2,1,0:T(8,128)S(1)}, f32[2,128,512]{2,1,0:T(8,128)S(1)}...) custom-call(s32[1]{0:T(128)} %bitcast.me_ref, s32[8,1]{1,0:T(8,128)S(1)} %copy.14.near_ref, ...), custom_call_target="tpu_custom_call" | custom-call | flops 1 | bytes 1 | tf_op jit(solution)/shard_map/pallas_call | solution.py:280
  186.4 4.3 %shard_map.104.twice_ref = f32[8,128,512]{2,1,0:T(8,128)S(1)} custom-call(bf16[8,128,1024]{2,1,0:T(8,128)(2,1)S(1)} %get-tuple-element.84.ah_ref, bf16[8,128,1024]{2,1,0:T(8,128)(2,1)S(1)} %get-tuple-element.85.al_ref, f32[8,128,512]{2,1,0:T(8,128)S(1)} %get-tuple-element.134.refs_0_.once_ref), custom_call_target="tpu_custom_call" | custom-call | flops 1 | bytes 1 | tf_op jit(solution)/shard_map/pallas_call | solution.py:158
  190.7 4.1 %shard_map.105.refs_5_ = f32[8,128,512]{2,1,0:T(8,128)S(1)} custom-call(f32[8,128,512]{2,1,0:T(8,128)S(1)} %get-tuple-element.119.refs_0_.x_ref, f32[8,128,512]{2,1,0:T(8,128)S(1)} %get-tuple-element.134.refs_0_.once_ref, f32[8,128,512]{2,1,0:T(8,128)S(1)} %shard_map.104.twice_ref, bf16[2,512,512]{2,1,0:T(8,128)(2,1)S(1)} %get-tuple-element.101.sh_ref, ...), custom_call_target="tpu_custom_call" | custom-call | flops 1 | bytes 1 | tf_op jit(solution)/shard_map/pallas_call | solution.py:180
  195.8 10.5 %collective-permute-done.28.refs_1_ = f32[2,128,512]{2,1,0:T(8,128)S(1)} collective-permute-done((f32[2,128,512]{2,1,0:T(8,128)S(1)}, f32[2,128,512]{2,1,0:T(8,128)S(1)}, u32[]{:S(2)}, u32[]{:S(2)}) %collective-permute-start.28) | collective-permute-done | bytes 524320 | tf_op jit(solution)/shard_map/ppermute | solution.py:345
  208.2 5.6 %shard_map.106.acc_ref = f32[8,128,512]{2,1,0:T(8,128)S(1)} custom-call(bf16[8,128,896]{2,1,0:T(8,128)(2,1)S(1)} %get-tuple-element.78.ah_ref, bf16[8,128,896]{2,1,0:T(8,128)(2,1)S(1)} %get-tuple-element.79.al_ref, f32[2,128,512]{2,1,0:T(8,128)S(1)} %collective-permute-done.27.refs_0_, f32[2,128,512]{2,1,0:T(8,128)S(1)} %collective-permute-done.28.refs_1_, ...), custom_call_target="tpu_custom_call" | custom-call | flops 1 | bytes 1 | tf_op jit(solution)/shard_map/pallas_call | solution.py:158
  213.9 17.4 %collective-permute-done.25.refs_1_ = f32[2,128,512]{2,1,0:T(8,128)S(1)} collective-permute-done((f32[2,128,512]{2,1,0:T(8,128)S(1)}, f32[2,128,512]{2,1,0:T(8,128)S(1)}, u32[]{:S(2)}, u32[]{:S(2)}) %collective-permute-start.25) | collective-permute-done | bytes 524320 | tf_op jit(solution)/shard_map/ppermute | solution.py:336
  233.3 5.9 %shard_map.107 = f32[8,128,512]{2,1,0:T(8,128)} custom-call(s32[1]{0:T(128)} %bitcast.me_ref, s32[8,1]{1,0:T(8,128)S(1)} %copy.14.near_ref, s32[2,2]{1,0:T(2,128)S(1)} %bitcast.20, bf16[8,128,512]{2,1,0:T(8,128)(2,1)S(1)} %get-tuple-element.74.ah_ref, bf16[8,128,512]{2,1,0:T(8,128)(2,1)S(1)} %get-tuple-element.75.al_ref, ...), custom_call_target="tpu_custom_call" | custom-call | flops 1 | bytes 1 | tf_op jit(solution)/shard_map/pallas_call | solution.py:280
  (94 shorter events, 58.2 us)
Async XLA Ops:
  5.1 25.8 %collective-permute-start.2 = (f32[2,128,512]{2,1,0:T(8,128)}, f32[2,128,512]{2,1,0:T(8,128)S(1)}, u32[]{:S(2)}, u32[]{:S(2)}) collective-permute-start(f32[2,128,512]{2,1,0:T(8,128)} %get-tuple-element.81), channel_id=1, source_target_pairs={{0,2},{1,3},{2,0},{3,1},{4,6},{5,7},{6,4},{7,5},{8,10},{9,11},{10,... | collective-permute-start | bytes 1572872 | tf_op jit(solution)/shard_map/ppermute | solution.py:336
  8.2 22.8 %collective-permute-start.3 = (f32[2,128,512]{2,1,0:T(8,128)}, f32[2,128,512]{2,1,0:T(8,128)S(1)}, u32[]{:S(2)}, u32[]{:S(2)}) collective-permute-start(f32[2,128,512]{2,1,0:T(8,128)} %get-tuple-element.82), channel_id=1, source_target_pairs={{0,8},{8,16},{16,24},{24,0},{1,9},{9,17},{17,25},{25,1},{2,10},{10... | collective-permute-start | bytes 1572872 | tf_op jit(solution)/shard_map/ppermute | solution.py:344
  9.7 24.3 %collective-permute-start.4 = (f32[2,128,512]{2,1,0:T(8,128)}, f32[2,128,512]{2,1,0:T(8,128)S(1)}, u32[]{:S(2)}, u32[]{:S(2)}) collective-permute-start(f32[2,128,512]{2,1,0:T(8,128)} %get-tuple-element.83), channel_id=1, source_target_pairs={{8,0},{16,8},{24,16},{0,24},{9,1},{17,9},{25,17},{1,25},{10,2},{18... | collective-permute-start | bytes 1572872 | tf_op jit(solution)/shard_map/ppermute | solution.py:345
  11.1 29.1 %collective-permute-start = (f32[2,128,512]{2,1,0:T(8,128)}, f32[2,128,512]{2,1,0:T(8,128)S(1)}, u32[]{:S(2)}, u32[]{:S(2)}) collective-permute-start(f32[2,128,512]{2,1,0:T(8,128)} %get-tuple-element.76), channel_id=1, source_target_pairs={{0,6},{1,7},{2,4},{3,5},{4,2},{5,3},{6,0},{7,1},{8,14},{9,15},{10,... | collective-permute-start | bytes 1572872 | tf_op jit(solution)/shard_map/ppermute | solution.py:336
  13.6 45.1 %collective-permute-start.1 = (f32[2,128,512]{2,1,0:T(8,128)S(1)}, f32[2,128,512]{2,1,0:T(8,128)S(1)}, u32[]{:S(2)}, u32[]{:S(2)}) collective-permute-start(f32[2,128,512]{2,1,0:T(8,128)S(1)} %get-tuple-element.77), channel_id=1, source_target_pairs={{0,4},{1,5},{2,6},{3,7},{4,0},{5,1},{6,2},{7,3},{8,12},{9,13},{10,... | collective-permute-start | bytes 1572872 | tf_op jit(solution)/shard_map/ppermute | solution.py:336
  58.8 2.0 collective-permute-start.7
  64.3 18.9 %collective-permute-start.10 = (f32[2,128,512]{2,1,0:T(8,128)S(1)}, f32[2,128,512]{2,1,0:T(8,128)S(1)}, u32[]{:S(2)}, u32[]{:S(2)}) collective-permute-start(f32[2,128,512]{2,1,0:T(8,128)S(1)} %get-tuple-element.97), channel_id=1, source_target_pairs={{0,2},{1,3},{2,0},{3,1},{4,6},{5,7},{6,4},{7,5},{8,10},{9,11},{10,... | collective-permute-start | bytes 1572872 | tf_op jit(solution)/shard_map/ppermute | solution.py:336
  64.4 18.9 %collective-permute-start.11 = (f32[2,128,512]{2,1,0:T(8,128)S(1)}, f32[2,128,512]{2,1,0:T(8,128)S(1)}, u32[]{:S(2)}, u32[]{:S(2)}) collective-permute-start(f32[2,128,512]{2,1,0:T(8,128)S(1)} %get-tuple-element.98), channel_id=1, source_target_pairs={{0,8},{8,16},{16,24},{24,0},{1,9},{9,17},{17,25},{25,1},{2,10},{10... | collective-permute-start | bytes 1572872 | tf_op jit(solution)/shard_map/ppermute | solution.py:344
  65.0 25.6 %collective-permute-start.12 = (f32[2,128,512]{2,1,0:T(8,128)S(1)}, f32[2,128,512]{2,1,0:T(8,128)S(1)}, u32[]{:S(2)}, u32[]{:S(2)}) collective-permute-start(f32[2,128,512]{2,1,0:T(8,128)S(1)} %get-tuple-element.99), channel_id=1, source_target_pairs={{8,0},{16,8},{24,16},{0,24},{9,1},{17,9},{25,17},{1,25},{10,2},{18... | collective-permute-start | bytes 1572872 | tf_op jit(solution)/shard_map/ppermute | solution.py:345
  67.4 30.8 %collective-permute-start.8 = (f32[2,128,512]{2,1,0:T(8,128)S(1)}, f32[2,128,512]{2,1,0:T(8,128)S(1)}, u32[]{:S(2)}, u32[]{:S(2)}) collective-permute-start(f32[2,128,512]{2,1,0:T(8,128)S(1)} %get-tuple-element.94), channel_id=1, source_target_pairs={{0,6},{1,7},{2,4},{3,5},{4,2},{5,3},{6,0},{7,1},{8,14},{9,15},{10,... | collective-permute-start | bytes 1572872 | tf_op jit(solution)/shard_map/ppermute | solution.py:336
  70.0 45.6 %collective-permute-start.9 = (f32[2,128,512]{2,1,0:T(8,128)S(1)}, f32[2,128,512]{2,1,0:T(8,128)S(1)}, u32[]{:S(2)}, u32[]{:S(2)}) collective-permute-start(f32[2,128,512]{2,1,0:T(8,128)S(1)} %get-tuple-element.95), channel_id=1, source_target_pairs={{0,4},{1,5},{2,6},{3,7},{4,0},{5,1},{6,2},{7,3},{8,12},{9,13},{10,... | collective-permute-start | bytes 1572872 | tf_op jit(solution)/shard_map/ppermute | solution.py:336
  115.7 2.0 collective-permute-start.15
  123.1 14.0 %collective-permute-start.18 = (f32[2,128,512]{2,1,0:T(8,128)S(1)}, f32[2,128,512]{2,1,0:T(8,128)S(1)}, u32[]{:S(2)}, u32[]{:S(2)}) collective-permute-start(f32[2,128,512]{2,1,0:T(8,128)S(1)} %get-tuple-element.116), channel_id=1, source_target_pairs={{0,2},{1,3},{2,0},{3,1},{4,6},{5,7},{6,4},{7,5},{8,10},{9,11},{10,... | collective-permute-start | bytes 1572872 | tf_op jit(solution)/shard_map/ppermute | solution.py:336
  123.2 15.7 %collective-permute-start.19 = (f32[2,128,512]{2,1,0:T(8,128)S(1)}, f32[2,128,512]{2,1,0:T(8,128)S(1)}, u32[]{:S(2)}, u32[]{:S(2)}) collective-permute-start(f32[2,128,512]{2,1,0:T(8,128)S(1)} %get-tuple-element.117), channel_id=1, source_target_pairs={{0,8},{8,16},{16,24},{24,0},{1,9},{9,17},{17,25},{25,1},{2,10},{10... | collective-permute-start | bytes 1572872 | tf_op jit(solution)/shard_map/ppermute | solution.py:344
  123.6 25.8 %collective-permute-start.20 = (f32[2,128,512]{2,1,0:T(8,128)S(1)}, f32[2,128,512]{2,1,0:T(8,128)S(1)}, u32[]{:S(2)}, u32[]{:S(2)}) collective-permute-start(f32[2,128,512]{2,1,0:T(8,128)S(1)} %get-tuple-element.118), channel_id=1, source_target_pairs={{8,0},{16,8},{24,16},{0,24},{9,1},{17,9},{25,17},{1,25},{10,2},{18... | collective-permute-start | bytes 1572872 | tf_op jit(solution)/shard_map/ppermute | solution.py:345
  126.2 29.5 %collective-permute-start.16 = (f32[2,128,512]{2,1,0:T(8,128)S(1)}, f32[2,128,512]{2,1,0:T(8,128)S(1)}, u32[]{:S(2)}, u32[]{:S(2)}) collective-permute-start(f32[2,128,512]{2,1,0:T(8,128)S(1)} %get-tuple-element.113), channel_id=1, source_target_pairs={{0,6},{1,7},{2,4},{3,5},{4,2},{5,3},{6,0},{7,1},{8,14},{9,15},{10,... | collective-permute-start | bytes 1572872 | tf_op jit(solution)/shard_map/ppermute | solution.py:336
  128.8 45.6 %collective-permute-start.17 = (f32[2,128,512]{2,1,0:T(8,128)S(1)}, f32[2,128,512]{2,1,0:T(8,128)S(1)}, u32[]{:S(2)}, u32[]{:S(2)}) collective-permute-start(f32[2,128,512]{2,1,0:T(8,128)S(1)} %get-tuple-element.114), channel_id=1, source_target_pairs={{0,4},{1,5},{2,6},{3,7},{4,0},{5,1},{6,2},{7,3},{8,12},{9,13},{10,... | collective-permute-start | bytes 1572872 | tf_op jit(solution)/shard_map/ppermute | solution.py:336
  174.5 2.0 collective-permute-start.23
  180.0 14.8 %collective-permute-start.26 = (f32[2,128,512]{2,1,0:T(8,128)S(1)}, f32[2,128,512]{2,1,0:T(8,128)S(1)}, u32[]{:S(2)}, u32[]{:S(2)}) collective-permute-start(f32[2,128,512]{2,1,0:T(8,128)S(1)} %get-tuple-element.131), channel_id=1, source_target_pairs={{0,2},{1,3},{2,0},{3,1},{4,6},{5,7},{6,4},{7,5},{8,10},{9,11},{10,... | collective-permute-start | bytes 1572872 | tf_op jit(solution)/shard_map/ppermute | solution.py:336
  180.0 15.7 %collective-permute-start.27 = (f32[2,128,512]{2,1,0:T(8,128)S(1)}, f32[2,128,512]{2,1,0:T(8,128)S(1)}, u32[]{:S(2)}, u32[]{:S(2)}) collective-permute-start(f32[2,128,512]{2,1,0:T(8,128)S(1)} %get-tuple-element.132), channel_id=1, source_target_pairs={{0,8},{8,16},{16,24},{24,0},{1,9},{9,17},{17,25},{25,1},{2,10},{10... | collective-permute-start | bytes 1572872 | tf_op jit(solution)/shard_map/ppermute | solution.py:344
  180.4 25.8 %collective-permute-start.28 = (f32[2,128,512]{2,1,0:T(8,128)S(1)}, f32[2,128,512]{2,1,0:T(8,128)S(1)}, u32[]{:S(2)}, u32[]{:S(2)}) collective-permute-start(f32[2,128,512]{2,1,0:T(8,128)S(1)} %get-tuple-element.133), channel_id=1, source_target_pairs={{8,0},{16,8},{24,16},{0,24},{9,1},{17,9},{25,17},{1,25},{10,2},{18... | collective-permute-start | bytes 1572872 | tf_op jit(solution)/shard_map/ppermute | solution.py:345
  183.0 30.8 %collective-permute-start.24 = (f32[2,128,512]{2,1,0:T(8,128)S(1)}, f32[2,128,512]{2,1,0:T(8,128)S(1)}, u32[]{:S(2)}, u32[]{:S(2)}) collective-permute-start(f32[2,128,512]{2,1,0:T(8,128)S(1)} %get-tuple-element.128), channel_id=1, source_target_pairs={{0,6},{1,7},{2,4},{3,5},{4,2},{5,3},{6,0},{7,1},{8,14},{9,15},{10,... | collective-permute-start | bytes 1572872 | tf_op jit(solution)/shard_map/ppermute | solution.py:336
  185.7 45.6 %collective-permute-start.25 = (f32[2,128,512]{2,1,0:T(8,128)S(1)}, f32[2,128,512]{2,1,0:T(8,128)S(1)}, u32[]{:S(2)}, u32[]{:S(2)}) collective-permute-start(f32[2,128,512]{2,1,0:T(8,128)S(1)} %get-tuple-element.129), channel_id=1, source_target_pairs={{0,4},{1,5},{2,6},{3,7},{4,0},{5,1},{6,2},{7,3},{8,12},{9,13},{10,... | collective-permute-start | bytes 1572872 | tf_op jit(solution)/shard_map/ppermute | solution.py:336
  231.3 2.0 collective-permute-start.31
  (17 other events, 107.2 us)

commit v2 on v1

--- a/solution.py
+++ b/solution.py
@@ -162,7 +162,7 @@
         in_specs=specs,
         out_specs=rows_of(out.shape),
         scratch_shapes=[pltpu.VMEM((depth, width), jnp.bfloat16)] * 2,
-        compiler_params=pltpu.CompilerParams(vmem_limit_bytes=24 * MIB),
+        compiler_params=pltpu.CompilerParams(vmem_limit_bytes=8 * MIB + 22 * depth * width),
         cost_estimate=SMALL,
     )(*args)
 
@@ -310,14 +310,12 @@
     )
     route = (plan, me, near_send[0], far_send[0])
 
-    early_k = [2 * j for j in early] + [1] + [2 * j + 1 for j in early]
-    late_k = [2 * j for j in late] + [2 * j + 1 for j in late]
-    widths = (row_blocks, 2 * hcap + cap * len(early_k), cap * len(late_k))
+    first_k = [2 * j for j in early + late[:-1]] + [1] + [2 * j + 1 for j in early + late[:-1]]
+    last_k = [2 * late[-1], 2 * late[-1] + 1]
+    widths = (row_blocks, 2 * hcap + cap * len(first_k), cap * len(last_k))
     place_of = [0] * peers
-    for at, k in enumerate(early_k):
+    for at, k in enumerate(first_k + last_k):
         place_of[k] = row_blocks + 2 * hcap + at * cap
-    for at, k in enumerate(late_k):
-        place_of[k] = row_blocks + widths[1] + at * cap
     slot = tile_cols
     near_at = slot - row_blocks
     source, item = near_at // cap, near_at % cap
@@ -330,7 +328,7 @@
         slot < row_blocks, slot, jnp.where(slot < row_blocks + peers * cap, near_place, far_place)
     ).astype(jnp.int32)
 
-    own_a, early_a, late_a = dense_adjacency(tile_rows, places, tile_count, tile_vals, row_blocks, widths)
+    own_a, first_a, last_a = dense_adjacency(tile_rows, places, tile_count, tile_vals, row_blocks, widths)
 
     def swap(x, k):
         return lax.ppermute(x, "dev", [(i, i ^ k) for i in range(peers)])
@@ -347,13 +345,13 @@
 
     def arrive(flight, acc, square=()):
         long, short, lower, upper, to_core = flight
-        (to_core, *short), (lower, upper, acc) = tie([to_core] + short, lower, upper, acc)
-        across = [swap(to_core, 1)] + [swap(r[cap:], 1) for r in short]
-        arrived = [(lower, hcap), (upper, hcap)] + [(r, cap) for r in short + across]
-        acc = apply_dense(early_a, arrived, acc, square)
-        long, (acc,) = tie(long, acc)
-        passed = swap(jnp.concatenate([r[cap:] for r in long], axis=0), 1)
-        return acc, [(r, cap) for r in long] + [(passed, passed.shape[0])]
+        *later, last = long
+        (to_core, *near), (acc,) = tie([to_core] + short + later, acc)
+        across = [swap(to_core, 1)] + [swap(r[cap:], 1) for r in near]
+        arrived = [(lower, hcap), (upper, hcap)] + [(r, cap) for r in near + across]
+        acc = apply_dense(first_a, arrived, acc, square)
+        (last,), (acc,) = tie([last], acc)
+        return acc, [(last, cap), (swap(last[cap:], 1), cap)]
 
     current = features.reshape(row_blocks, TILE, width)
     sends = pick(current, route)
@@ -363,11 +361,11 @@
         flight = start(sends)
         skew, square = [(w, layer) for w in parts[:2]], [(w, layer) for w in parts[2:]]
         acc, arrived = arrive(flight, apply_dense(own_a, [(current, row_blocks)]))
-        once, *sends = finish(late_a, arrived, acc, route)
+        once, *sends = finish(last_a, arrived, acc, route)
         flight = start(sends)
         base = mix(current, once, apply_dense(own_a, [(once, row_blocks)]), skew, square)
         base, arrived = arrive(flight, base, square)
-        current, *sends = finish(late_a, arrived, base, route, square, layer < layers - 1)
+        current, *sends = finish(last_a, arrived, base, route, square, layer < layers - 1)
     return current.reshape(features.shape)
 
 

time: 239 us -> 224 us (0.937)
  waiting for transfers between devices: 123 us -> 108 us
    ppermute x4, waiting for transfers between devices: 31.3 us -> 4.07 us  [start(): upper = lax.ppermute(sends[len(chips) + 1], 'dom', down)]
    ppermute x24 -> x28, waiting for transfers between devices: 88.4 us -> 104 us  [swap(): return lax.ppermute(x, 'dev', [(i, i ^ k) for i in range(peers)])]
    pallas_call x8, Pallas kernels: 36.8 us -> 40.9 us  [apply_dense(): pl.pallas_call(functools.partial(apply_kernel, len(xs), acc is not None,...]
    pallas_call x4, Pallas kernels: 18.3 us -> 14.1 us  [finish(): pl.pallas_call(functools.partial(finish_kernel, plan, len(xs), bool(squar...]
    ppermute x4, starting transfers between devices: 8.94 us -> 5.73 us  [start(): upper = lax.ppermute(sends[len(chips) + 1], 'dom', down)]
    ppermute x4, starting transfers between devices: 2.92 us -> 5.97 us  [start(): lower = lax.ppermute(sends[len(chips)], 'dom', up)]
    ppermute x4, waiting for transfers between devices: 2.74 us -> 0.01 us  [start(): lower = lax.ppermute(sends[len(chips)], 'dom', up)]
    ppermute x24 -> x28, starting transfers between devices: 18.7 us -> 19.2 us  [swap(): return lax.ppermute(x, 'dev', [(i, i ^ k) for i in range(peers)])]
  transfers between devices with their start and end apart: 32 -> 36, of which waited for: 23 -> 26; matrix products, arithmetic and copies ran while one was open for 0% -> 0% of each run, Pallas kernels for 22% -> 25%
where the time goes in v2:
time: 224 us
  waiting for transfers between devices  108 us (48%)
  Pallas kernels  72.8 us (32%)
  starting transfers between devices  30.9 us (14%)
  local copies, waits for them, and re-layouts  6.47 us (3%)
  between operations  6.03 us (3%)
    ppermute x28, waiting for transfers between devices, swap(): return lax.ppermute(x, 'dev', [(i, i ^ k) for i in range(peers)])  104 us
    pallas_call x8, Pallas kernels, apply_dense(): pl.pallas_call(functools.partial(apply_kernel, len(xs), acc is not None,...  40.9 us
    ppermute x28, starting transfers between devices, swap(): return lax.ppermute(x, 'dev', [(i, i ^ k) for i in range(peers)])  19.2 us
    pallas_call x4, Pallas kernels, finish(): pl.pallas_call(functools.partial(finish_kernel, plan, len(xs), bool(squar...  14.1 us
    pallas_call x2, Pallas kernels, mix(): pl.pallas_call(mix_kernel, grid=(x.shape[0] // STEP,), out_shape=jax.Shap...  8.06 us
    ppermute x4, starting transfers between devices, start(): lower = lax.ppermute(sends[len(chips)], 'dom', up)  5.97 us
    ppermute x4, starting transfers between devices, start(): upper = lax.ppermute(sends[len(chips) + 1], 'dom', down)  5.73 us
    unnamed x18, local copies, waits for them, and re-layouts  4.78 us
  transfers between devices with their start and end apart: 36, of which 26 were waited for; matrix products, arithmetic and copies ran while one was open for 0% of the time, Pallas kernels for 25%

profile of v2, /device:TPU:0, one launch (start us, length us, event | category | flops | bytes accessed | tf_op | source)
XLA Modules:
  0.0 223.8 jit_solution(5814787581646956973)
XLA Ops:
  5.1 3.1 %collective-permute-start.3 = (f32[2,128,512]{2,1,0:T(8,128)}, f32[2,128,512]{2,1,0:T(8,128)S(1)}, u32[]{:S(2)}, u32[]{:S(2)}) collective-permute-start(f32[2,128,512]{2,1,0:T(8,128)} %get-tuple-element.74), channel_id=1, source_target_pairs={{0,2},{1,3},{2,0},{3,1},{4,6},{5,7},{6,4},{7,5},{8,10},{9,11},{10,... | collective-permute-start | bytes 1572872 | tf_op jit(solution)/shard_map/ppermute | solution.py:334
  22.6 3.5 %shard_map.91 = (bf16[8,128,1024]{2,1,0:T(8,128)(2,1)S(1)}, bf16[8,128,1024]{2,1,0:T(8,128)(2,1)S(1)}, bf16[8,128,1152]{2,1,0:T(8,128)(2,1)S(1)}, bf16[8,128,115...) custom-call(s32[80]{0:T(128)S(1)} %copy-done.6, ...), custom_call_target="tpu_custom_call" | custom-call | flops 1 | bytes 1 | tf_op jit(solution)/shard_map/pallas_call | solution.py:72
  26.1 4.3 %shard_map.93.refs_7_ = f32[8,128,512]{2,1,0:T(8,128)S(1)} custom-call(bf16[8,128,1024]{2,1,0:T(8,128)(2,1)S(1)} %get-tuple-element.76.ah_ref, bf16[8,128,1024]{2,1,0:T(8,128)(2,1)S(1)} %get-tuple-element.77.al_ref, f32[8,128,512]{2,1,0:T(8,128)S(1)} %bitcast.14), custom_call_target="tpu_custom_call" | custom-call | flops 1 | bytes 1 | tf_op jit(solution)/shard_map/pallas_call | solution.py:158
  30.4 4.6 %collective-permute-done.4.refs_3_ = f32[2,128,512]{2,1,0:T(8,128)S(1)} collective-permute-done((f32[2,128,512]{2,1,0:T(8,128)}, f32[2,128,512]{2,1,0:T(8,128)S(1)}, u32[]{:S(2)}, u32[]{:S(2)}) %collective-permute-start.4) | collective-permute-done | bytes 524320 | tf_op jit(solution)/shard_map/ppermute | solution.py:334
  37.4 5.1 %shard_map.94.acc_ref = f32[8,128,512]{2,1,0:T(8,128)S(1)} custom-call(bf16[8,128,1152]{2,1,0:T(8,128)(2,1)S(1)} %get-tuple-element.69.ah_ref, bf16[8,128,1152]{2,1,0:T(8,128)(2,1)S(1)} %get-tuple-element.70.al_ref, f32[2,128,512]{2,1,0:T(8,128)S(1)} %collective-permute-done.1.refs_0_, f32[2,128,512]{2,1,0:T(8,128)S(1)} %collective-permute-done.2.refs_1_, ...), custom_call_target="tpu_custom_call" | custom-call | flops 1 | bytes 1 | tf_op jit(solution)/shard_map/pallas_call | solution.py:158
  42.5 13.8 %collective-permute-done.refs_0_ = f32[2,128,512]{2,1,0:T(8,128)S(1)} collective-permute-done((f32[2,128,512]{2,1,0:T(8,128)S(1)}, f32[2,128,512]{2,1,0:T(8,128)S(1)}, u32[]{:S(2)}, u32[]{:S(2)}) %collective-permute-start) | collective-permute-done | bytes 524320 | tf_op jit(solution)/shard_map/ppermute | solution.py:334
  67.1 4.1 %shard_map.97 = (bf16[2,512,512]{2,1,0:T(8,128)(2,1)S(1)}, bf16[2,512,512]{2,1,0:T(8,128)(2,1)S(1)}, bf16[2,512,512]{2,1,0:T(8,128)(2,1)S(1)}, bf16[2,512,512]{2,1,0:T(8,128)(2,1)S(1)}) custom-call(f32[2,512,512]{2,1,0:T(8,128)S(1)} %copy-done.3), custom_call_target="tpu_custom_call" | custom-call | flops 1 | bytes 1 | tf_op jit(solution)/shard_map/pallas_call | solution.py:96
  71.2 4.3 %shard_map.96.twice_ref = f32[8,128,512]{2,1,0:T(8,128)S(1)} custom-call(bf16[8,128,1024]{2,1,0:T(8,128)(2,1)S(1)} %get-tuple-element.76.ah_ref, bf16[8,128,1024]{2,1,0:T(8,128)(2,1)S(1)} %get-tuple-element.77.al_ref, f32[8,128,512]{2,1,0:T(8,128)S(1)} %get-tuple-element.90.refs_0_.once_ref), custom_call_target="tpu_custom_call" | custom-call | flops 1 | bytes 1 | tf_op jit(solution)/shard_map/pallas_call | solution.py:158
  75.5 4.0 %shard_map.98.refs_7_ = f32[8,128,512]{2,1,0:T(8,128)S(1)} custom-call(f32[8,128,512]{2,1,0:T(8,128)S(1)} %bitcast.15, f32[8,128,512]{2,1,0:T(8,128)S(1)} %get-tuple-element.90.refs_0_.once_ref, f32[8,128,512]{2,1,0:T(8,128)S(1)} %shard_map.96.twice_ref, bf16[2,512,512]{2,1,0:T(8,128)(2,1)S(1)} %get-tuple-element.91.sh_ref, ...), custom_call_target="tpu_custom_call" | custom-call | flops 1 | bytes 1 | tf_op jit(solution)/shard_map/pallas_call | solution.py:180
  79.5 7.8 %collective-permute-done.13.refs_3_ = f32[2,128,512]{2,1,0:T(8,128)S(1)} collective-permute-done((f32[2,128,512]{2,1,0:T(8,128)S(1)}, f32[2,128,512]{2,1,0:T(8,128)S(1)}, u32[]{:S(2)}, u32[]{:S(2)}) %collective-permute-start.13) | collective-permute-done | bytes 524320 | tf_op jit(solution)/shard_map/ppermute | solution.py:334
  89.8 6.8 %shard_map.99.acc_ref = f32[8,128,512]{2,1,0:T(8,128)S(1)} custom-call(bf16[8,128,1152]{2,1,0:T(8,128)(2,1)S(1)} %get-tuple-element.69.ah_ref, bf16[8,128,1152]{2,1,0:T(8,128)(2,1)S(1)} %get-tuple-element.70.al_ref, f32[2,128,512]{2,1,0:T(8,128)S(1)} %collective-permute-done.10.refs_0_, f32[2,128,512]{2,1,0:T(8,128)S(1)} %collective-permute-done.11.refs_1_, ...), custom_call_target="tpu_custom_call" | custom-call | flops 1 | bytes 1 | tf_op jit(solution)/shard_map/pallas_call | solution.py:158
  96.6 12.9 %collective-permute-done.9.refs_0_ = f32[2,128,512]{2,1,0:T(8,128)S(1)} collective-permute-done((f32[2,128,512]{2,1,0:T(8,128)S(1)}, f32[2,128,512]{2,1,0:T(8,128)S(1)}, u32[]{:S(2)}, u32[]{:S(2)}) %collective-permute-start.9) | collective-permute-done | bytes 524320 | tf_op jit(solution)/shard_map/ppermute | solution.py:334
  111.1 4.2 %shard_map.100 = (f32[8,128,512]{2,1,0:T(8,128)S(1)}, f32[2,128,512]{2,1,0:T(8,128)S(1)}, f32[2,128,512]{2,1,0:T(8,128)S(1)}, f32[2,128,512]{2,1,0:T(8,128)S(1)}...) custom-call(s32[1]{0:T(128)} %bitcast.me_ref, s32[8,1]{1,0:T(8,128)S(1)} %copy.14.near_ref, ...), custom_call_target="tpu_custom_call" | custom-call | flops 1 | bytes 1 | tf_op jit(solution)/shard_map/pallas_call | solution.py:280
  121.8 4.3 %shard_map.101.refs_7_ = f32[8,128,512]{2,1,0:T(8,128)S(1)} custom-call(bf16[8,128,1024]{2,1,0:T(8,128)(2,1)S(1)} %get-tuple-element.76.ah_ref, bf16[8,128,1024]{2,1,0:T(8,128)(2,1)S(1)} %get-tuple-element.77.al_ref, f32[8,128,512]{2,1,0:T(8,128)S(1)} %get-tuple-element.107.refs_0_.x_ref), custom_call_target="tpu_custom_call" | custom-call | flops 1 | bytes 1 | tf_op jit(solution)/shard_map/pallas_call | solution.py:158
  126.1 3.3 %collective-permute-done.21.refs_2_ = f32[2,128,512]{2,1,0:T(8,128)S(1)} collective-permute-done((f32[2,128,512]{2,1,0:T(8,128)S(1)}, f32[2,128,512]{2,1,0:T(8,128)S(1)}, u32[]{:S(2)}, u32[]{:S(2)}) %collective-permute-start.21) | collective-permute-done | bytes 524320 | tf_op jit(solution)/shard_map/ppermute | solution.py:334
  129.4 12.7 %collective-permute-done.22.refs_3_ = f32[2,128,512]{2,1,0:T(8,128)S(1)} collective-permute-done((f32[2,128,512]{2,1,0:T(8,128)S(1)}, f32[2,128,512]{2,1,0:T(8,128)S(1)}, u32[]{:S(2)}, u32[]{:S(2)}) %collective-permute-start.22) | collective-permute-done | bytes 524320 | tf_op jit(solution)/shard_map/ppermute | solution.py:334
  144.5 5.1 %shard_map.102.acc_ref = f32[8,128,512]{2,1,0:T(8,128)S(1)} custom-call(bf16[8,128,1152]{2,1,0:T(8,128)(2,1)S(1)} %get-tuple-element.69.ah_ref, bf16[8,128,1152]{2,1,0:T(8,128)(2,1)S(1)} %get-tuple-element.70.al_ref, f32[2,128,512]{2,1,0:T(8,128)S(1)} %collective-permute-done.19.refs_0_, f32[2,128,512]{2,1,0:T(8,128)S(1)} %collective-permute-done.20.refs_1_, ...), custom_call_target="tpu_custom_call" | custom-call | flops 1 | bytes 1 | tf_op jit(solution)/shard_map/pallas_call | solution.py:158
  149.6 14.6 %collective-permute-done.18.refs_0_ = f32[2,128,512]{2,1,0:T(8,128)S(1)} collective-permute-done((f32[2,128,512]{2,1,0:T(8,128)S(1)}, f32[2,128,512]{2,1,0:T(8,128)S(1)}, u32[]{:S(2)}, u32[]{:S(2)}) %collective-permute-start.18) | collective-permute-done | bytes 524320 | tf_op jit(solution)/shard_map/ppermute | solution.py:334
  175.0 4.3 %shard_map.104.twice_ref = f32[8,128,512]{2,1,0:T(8,128)S(1)} custom-call(bf16[8,128,1024]{2,1,0:T(8,128)(2,1)S(1)} %get-tuple-element.76.ah_ref, bf16[8,128,1024]{2,1,0:T(8,128)(2,1)S(1)} %get-tuple-element.77.al_ref, f32[8,128,512]{2,1,0:T(8,128)S(1)} %get-tuple-element.120.refs_0_.once_ref), custom_call_target="tpu_custom_call" | custom-call | flops 1 | bytes 1 | tf_op jit(solution)/shard_map/pallas_call | solution.py:158
  179.2 4.1 %shard_map.105.refs_7_ = f32[8,128,512]{2,1,0:T(8,128)S(1)} custom-call(f32[8,128,512]{2,1,0:T(8,128)S(1)} %get-tuple-element.107.refs_0_.x_ref, f32[8,128,512]{2,1,0:T(8,128)S(1)} %get-tuple-element.120.refs_0_.once_ref, f32[8,128,512]{2,1,0:T(8,128)S(1)} %shard_map.104.twice_ref, bf16[2,512,512]{2,1,0:T(8,128)(2,1)S(1)} %get-tuple-element.91.sh_ref, ...), custom_call_target="tpu_custom_call" | custom-call | flops 1 | bytes 1 | tf_op jit(solution)/shard_map/pallas_call | solution.py:180
  183.3 11.9 %collective-permute-done.31.refs_3_ = f32[2,128,512]{2,1,0:T(8,128)S(1)} collective-permute-done((f32[2,128,512]{2,1,0:T(8,128)S(1)}, f32[2,128,512]{2,1,0:T(8,128)S(1)}, u32[]{:S(2)}, u32[]{:S(2)}) %collective-permute-start.31) | collective-permute-done | bytes 524320 | tf_op jit(solution)/shard_map/ppermute | solution.py:334
  197.7 6.8 %shard_map.106.acc_ref = f32[8,128,512]{2,1,0:T(8,128)S(1)} custom-call(bf16[8,128,1152]{2,1,0:T(8,128)(2,1)S(1)} %get-tuple-element.69.ah_ref, bf16[8,128,1152]{2,1,0:T(8,128)(2,1)S(1)} %get-tuple-element.70.al_ref, f32[2,128,512]{2,1,0:T(8,128)S(1)} %collective-permute-done.28.refs_0_, f32[2,128,512]{2,1,0:T(8,128)S(1)} %collective-permute-done.29.refs_1_, ...), custom_call_target="tpu_custom_call" | custom-call | flops 1 | bytes 1 | tf_op jit(solution)/shard_map/pallas_call | solution.py:158
  204.5 12.9 %collective-permute-done.27.refs_0_ = f32[2,128,512]{2,1,0:T(8,128)S(1)} collective-permute-done((f32[2,128,512]{2,1,0:T(8,128)S(1)}, f32[2,128,512]{2,1,0:T(8,128)S(1)}, u32[]{:S(2)}, u32[]{:S(2)}) %collective-permute-start.27) | collective-permute-done | bytes 524320 | tf_op jit(solution)/shard_map/ppermute | solution.py:334
  219.0 4.7 %shard_map.107 = f32[8,128,512]{2,1,0:T(8,128)} custom-call(s32[1]{0:T(128)} %bitcast.me_ref, s32[8,1]{1,0:T(8,128)S(1)} %copy.14.near_ref, s32[2,2]{1,0:T(2,128)S(1)} %bitcast.20, bf16[8,128,256]{2,1,0:T(8,128)(2,1)S(1)} %get-tuple-element.66.ah_ref, bf16[8,128,256]{2,1,0:T(8,128)(2,1)S(1)} %get-tuple-element.67.al_ref, ...), custom_call_target="tpu_custom_call" | custom-call | flops 1 | bytes 1 | tf_op jit(solution)/shard_map/pallas_call | solution.py:280
  (98 shorter events, 54.4 us)
Async XLA Ops:
  5.1 25.3 %collective-permute-start.3 = (f32[2,128,512]{2,1,0:T(8,128)}, f32[2,128,512]{2,1,0:T(8,128)S(1)}, u32[]{:S(2)}, u32[]{:S(2)}) collective-permute-start(f32[2,128,512]{2,1,0:T(8,128)} %get-tuple-element.74), channel_id=1, source_target_pairs={{0,2},{1,3},{2,0},{3,1},{4,6},{5,7},{6,4},{7,5},{8,10},{9,11},{10,... | collective-permute-start | bytes 1572872 | tf_op jit(solution)/shard_map/ppermute | solution.py:334
  8.2 26.8 %collective-permute-start.4 = (f32[2,128,512]{2,1,0:T(8,128)}, f32[2,128,512]{2,1,0:T(8,128)S(1)}, u32[]{:S(2)}, u32[]{:S(2)}) collective-permute-start(f32[2,128,512]{2,1,0:T(8,128)} %get-tuple-element.75), channel_id=1, source_target_pairs={{0,6},{1,7},{2,4},{3,5},{4,2},{5,3},{6,0},{7,1},{8,14},{9,15},{10,... | collective-permute-start | bytes 1572872 | tf_op jit(solution)/shard_map/ppermute | solution.py:334
  10.7 25.0 %collective-permute-start.1 = (f32[2,128,512]{2,1,0:T(8,128)}, f32[2,128,512]{2,1,0:T(8,128)S(1)}, u32[]{:S(2)}, u32[]{:S(2)}) collective-permute-start(f32[2,128,512]{2,1,0:T(8,128)} %get-tuple-element.71), channel_id=1, source_target_pairs={{0,8},{8,16},{16,24},{24,0},{1,9},{9,17},{17,25},{25,1},{2,10},{10... | collective-permute-start | bytes 1572872 | tf_op jit(solution)/shard_map/ppermute | solution.py:342
  12.2 44.2 %collective-permute-start = (f32[2,128,512]{2,1,0:T(8,128)S(1)}, f32[2,128,512]{2,1,0:T(8,128)S(1)}, u32[]{:S(2)}, u32[]{:S(2)}) collective-permute-start(f32[2,128,512]{2,1,0:T(8,128)S(1)} %get-tuple-element.68), channel_id=1, source_target_pairs={{0,4},{1,5},{2,6},{3,7},{4,0},{5,1},{6,2},{7,3},{8,12},{9,13},{10,... | collective-permute-start | bytes 1572872 | tf_op jit(solution)/shard_map/ppermute | solution.py:334
  12.3 23.9 %collective-permute-start.2 = (f32[2,128,512]{2,1,0:T(8,128)}, f32[2,128,512]{2,1,0:T(8,128)S(1)}, u32[]{:S(2)}, u32[]{:S(2)}) collective-permute-start(f32[2,128,512]{2,1,0:T(8,128)} %get-tuple-element.72), channel_id=1, source_target_pairs={{8,0},{16,8},{24,16},{0,24},{9,1},{17,9},{25,17},{1,25},{10,2},{18... | collective-permute-start | bytes 1572872 | tf_op jit(solution)/shard_map/ppermute | solution.py:343
  35.1 1.9 collective-permute-start.6
  60.6 18.9 %collective-permute-start.12 = (f32[2,128,512]{2,1,0:T(8,128)S(1)}, f32[2,128,512]{2,1,0:T(8,128)S(1)}, u32[]{:S(2)}, u32[]{:S(2)}) collective-permute-start(f32[2,128,512]{2,1,0:T(8,128)S(1)} %get-tuple-element.88), channel_id=1, source_target_pairs={{0,2},{1,3},{2,0},{3,1},{4,6},{5,7},{6,4},{7,5},{8,10},{9,11},{10,... | collective-permute-start | bytes 1572872 | tf_op jit(solution)/shard_map/ppermute | solution.py:334
  60.7 26.7 %collective-permute-start.13 = (f32[2,128,512]{2,1,0:T(8,128)S(1)}, f32[2,128,512]{2,1,0:T(8,128)S(1)}, u32[]{:S(2)}, u32[]{:S(2)}) collective-permute-start(f32[2,128,512]{2,1,0:T(8,128)S(1)} %get-tuple-element.89), channel_id=1, source_target_pairs={{0,6},{1,7},{2,4},{3,5},{4,2},{5,3},{6,0},{7,1},{8,14},{9,15},{10,... | collective-permute-start | bytes 1572872 | tf_op jit(solution)/shard_map/ppermute | solution.py:334
  63.4 24.6 %collective-permute-start.10 = (f32[2,128,512]{2,1,0:T(8,128)S(1)}, f32[2,128,512]{2,1,0:T(8,128)S(1)}, u32[]{:S(2)}, u32[]{:S(2)}) collective-permute-start(f32[2,128,512]{2,1,0:T(8,128)S(1)} %get-tuple-element.85), channel_id=1, source_target_pairs={{0,8},{8,16},{16,24},{24,0},{1,9},{9,17},{17,25},{25,1},{2,10},{10... | collective-permute-start | bytes 1572872 | tf_op jit(solution)/shard_map/ppermute | solution.py:342
  64.9 24.4 %collective-permute-start.11 = (f32[2,128,512]{2,1,0:T(8,128)S(1)}, f32[2,128,512]{2,1,0:T(8,128)S(1)}, u32[]{:S(2)}, u32[]{:S(2)}) collective-permute-start(f32[2,128,512]{2,1,0:T(8,128)S(1)} %get-tuple-element.86), channel_id=1, source_target_pairs={{8,0},{16,8},{24,16},{0,24},{9,1},{17,9},{25,17},{1,25},{10,2},{18... | collective-permute-start | bytes 1572872 | tf_op jit(solution)/shard_map/ppermute | solution.py:343
  66.3 43.2 %collective-permute-start.9 = (f32[2,128,512]{2,1,0:T(8,128)S(1)}, f32[2,128,512]{2,1,0:T(8,128)S(1)}, u32[]{:S(2)}, u32[]{:S(2)}) collective-permute-start(f32[2,128,512]{2,1,0:T(8,128)S(1)} %get-tuple-element.84), channel_id=1, source_target_pairs={{0,4},{1,5},{2,6},{3,7},{4,0},{5,1},{6,2},{7,3},{8,12},{9,13},{10,... | collective-permute-start | bytes 1572872 | tf_op jit(solution)/shard_map/ppermute | solution.py:334
  87.5 1.9 collective-permute-start.15
  115.4 14.0 %collective-permute-start.21 = (f32[2,128,512]{2,1,0:T(8,128)S(1)}, f32[2,128,512]{2,1,0:T(8,128)S(1)}, u32[]{:S(2)}, u32[]{:S(2)}) collective-permute-start(f32[2,128,512]{2,1,0:T(8,128)S(1)} %get-tuple-element.105), channel_id=1, source_target_pairs={{0,2},{1,3},{2,0},{3,1},{4,6},{5,7},{6,4},{7,5},{8,10},{9,11},{10,... | collective-permute-start | bytes 1572872 | tf_op jit(solution)/shard_map/ppermute | solution.py:334
  115.4 26.7 %collective-permute-start.22 = (f32[2,128,512]{2,1,0:T(8,128)S(1)}, f32[2,128,512]{2,1,0:T(8,128)S(1)}, u32[]{:S(2)}, u32[]{:S(2)}) collective-permute-start(f32[2,128,512]{2,1,0:T(8,128)S(1)} %get-tuple-element.106), channel_id=1, source_target_pairs={{0,6},{1,7},{2,4},{3,5},{4,2},{5,3},{6,0},{7,1},{8,14},{9,15},{10,... | collective-permute-start | bytes 1572872 | tf_op jit(solution)/shard_map/ppermute | solution.py:334
  118.1 24.6 %collective-permute-start.19 = (f32[2,128,512]{2,1,0:T(8,128)S(1)}, f32[2,128,512]{2,1,0:T(8,128)S(1)}, u32[]{:S(2)}, u32[]{:S(2)}) collective-permute-start(f32[2,128,512]{2,1,0:T(8,128)S(1)} %get-tuple-element.102), channel_id=1, source_target_pairs={{0,8},{8,16},{16,24},{24,0},{1,9},{9,17},{17,25},{25,1},{2,10},{10... | collective-permute-start | bytes 1572872 | tf_op jit(solution)/shard_map/ppermute | solution.py:342
  119.6 24.4 %collective-permute-start.20 = (f32[2,128,512]{2,1,0:T(8,128)S(1)}, f32[2,128,512]{2,1,0:T(8,128)S(1)}, u32[]{:S(2)}, u32[]{:S(2)}) collective-permute-start(f32[2,128,512]{2,1,0:T(8,128)S(1)} %get-tuple-element.103), channel_id=1, source_target_pairs={{8,0},{16,8},{24,16},{0,24},{9,1},{17,9},{25,17},{1,25},{10,2},{18... | collective-permute-start | bytes 1572872 | tf_op jit(solution)/shard_map/ppermute | solution.py:343
  121.1 43.2 %collective-permute-start.18 = (f32[2,128,512]{2,1,0:T(8,128)S(1)}, f32[2,128,512]{2,1,0:T(8,128)S(1)}, u32[]{:S(2)}, u32[]{:S(2)}) collective-permute-start(f32[2,128,512]{2,1,0:T(8,128)S(1)} %get-tuple-element.101), channel_id=1, source_target_pairs={{0,4},{1,5},{2,6},{3,7},{4,0},{5,1},{6,2},{7,3},{8,12},{9,13},{10,... | collective-permute-start | bytes 1572872 | tf_op jit(solution)/shard_map/ppermute | solution.py:334
  142.2 1.9 collective-permute-start.24
  168.5 14.8 %collective-permute-start.30 = (f32[2,128,512]{2,1,0:T(8,128)S(1)}, f32[2,128,512]{2,1,0:T(8,128)S(1)}, u32[]{:S(2)}, u32[]{:S(2)}) collective-permute-start(f32[2,128,512]{2,1,0:T(8,128)S(1)} %get-tuple-element.118), channel_id=1, source_target_pairs={{0,2},{1,3},{2,0},{3,1},{4,6},{5,7},{6,4},{7,5},{8,10},{9,11},{10,... | collective-permute-start | bytes 1572872 | tf_op jit(solution)/shard_map/ppermute | solution.py:334
  168.6 26.7 %collective-permute-start.31 = (f32[2,128,512]{2,1,0:T(8,128)S(1)}, f32[2,128,512]{2,1,0:T(8,128)S(1)}, u32[]{:S(2)}, u32[]{:S(2)}) collective-permute-start(f32[2,128,512]{2,1,0:T(8,128)S(1)} %get-tuple-element.119), channel_id=1, source_target_pairs={{0,6},{1,7},{2,4},{3,5},{4,2},{5,3},{6,0},{7,1},{8,14},{9,15},{10,... | collective-permute-start | bytes 1572872 | tf_op jit(solution)/shard_map/ppermute | solution.py:334
  171.3 24.6 %collective-permute-start.28 = (f32[2,128,512]{2,1,0:T(8,128)S(1)}, f32[2,128,512]{2,1,0:T(8,128)S(1)}, u32[]{:S(2)}, u32[]{:S(2)}) collective-permute-start(f32[2,128,512]{2,1,0:T(8,128)S(1)} %get-tuple-element.115), channel_id=1, source_target_pairs={{0,8},{8,16},{16,24},{24,0},{1,9},{9,17},{17,25},{25,1},{2,10},{10... | collective-permute-start | bytes 1572872 | tf_op jit(solution)/shard_map/ppermute | solution.py:342
  172.8 24.4 %collective-permute-start.29 = (f32[2,128,512]{2,1,0:T(8,128)S(1)}, f32[2,128,512]{2,1,0:T(8,128)S(1)}, u32[]{:S(2)}, u32[]{:S(2)}) collective-permute-start(f32[2,128,512]{2,1,0:T(8,128)S(1)} %get-tuple-element.116), channel_id=1, source_target_pairs={{8,0},{16,8},{24,16},{0,24},{9,1},{17,9},{25,17},{1,25},{10,2},{18... | collective-permute-start | bytes 1572872 | tf_op jit(solution)/shard_map/ppermute | solution.py:343
  174.2 43.2 %collective-permute-start.27 = (f32[2,128,512]{2,1,0:T(8,128)S(1)}, f32[2,128,512]{2,1,0:T(8,128)S(1)}, u32[]{:S(2)}, u32[]{:S(2)}) collective-permute-start(f32[2,128,512]{2,1,0:T(8,128)S(1)} %get-tuple-element.114), channel_id=1, source_target_pairs={{0,4},{1,5},{2,6},{3,7},{4,0},{5,1},{6,2},{7,3},{8,12},{9,13},{10,... | collective-permute-start | bytes 1572872 | tf_op jit(solution)/shard_map/ppermute | solution.py:334
  195.4 1.9 collective-permute-start.33
  (21 other events, 114.1 us)

commit v3 on v2

--- a/solution.py
+++ b/solution.py
@@ -8,7 +8,7 @@
 from jax.sharding import PartitionSpec as P
 
 TILE = 128
-STEP = 2
+STEP = 4
 MIB = 1024 * 1024
 SMALL = pl.CostEstimate(flops=1, bytes_accessed=1, transcendentals=0)
 
@@ -310,7 +310,7 @@
     )
     route = (plan, me, near_send[0], far_send[0])
 
-    first_k = [2 * j for j in early + late[:-1]] + [1] + [2 * j + 1 for j in early + late[:-1]]
+    first_k = [2 * j for j in late[:-1] + early] + [1] + [2 * j + 1 for j in late[:-1] + early]
     last_k = [2 * late[-1], 2 * late[-1] + 1]
     widths = (row_blocks, 2 * hcap + cap * len(first_k), cap * len(last_k))
     place_of = [0] * peers
@@ -346,7 +346,7 @@
     def arrive(flight, acc, square=()):
         long, short, lower, upper, to_core = flight
         *later, last = long
-        (to_core, *near), (acc,) = tie([to_core] + short + later, acc)
+        (to_core, *near), (acc,) = tie([to_core] + later + short, acc)
         across = [swap(to_core, 1)] + [swap(r[cap:], 1) for r in near]
         arrived = [(lower, hcap), (upper, hcap)] + [(r, cap) for r in near + across]
         acc = apply_dense(first_a, arrived, acc, square)

time: 224 us -> 214 us (0.955)
  waiting for transfers between devices: 108 us -> 100 us
  Pallas kernels: 72.8 us -> 67.4 us
  starting transfers between devices: 30.9 us -> 33.7 us
    ppermute x28, waiting for transfers between devices: 104 us -> 99.5 us  [swap(): return lax.ppermute(x, 'dev', [(i, i ^ k) for i in range(peers)])]
    ppermute x4, waiting for transfers between devices: 4.07 us -> 0.58 us  [start(): upper = lax.ppermute(sends[len(chips) + 1], 'dom', down)]
    ppermute x28, starting transfers between devices: 19.2 us -> 22.1 us  [swap(): return lax.ppermute(x, 'dev', [(i, i ^ k) for i in range(peers)])]
    pallas_call x8, Pallas kernels: 40.9 us -> 38.2 us  [apply_dense(): pl.pallas_call(functools.partial(apply_kernel, len(xs), acc is not None,...]
  transfers between devices with their start and end apart: 36 -> 36, of which waited for: 26 -> 27; matrix products, arithmetic and copies ran while one was open for 0% -> 0% of each run, Pallas kernels for 25% -> 25%
where the time goes in v3:
time: 214 us
  waiting for transfers between devices  100 us (47%)
  Pallas kernels  67.4 us (31%)
  starting transfers between devices  33.7 us (16%)
  local copies, waits for them, and re-layouts  6.47 us (3%)
  between operations  5.99 us (3%)
    ppermute x28, waiting for transfers between devices, swap(): return lax.ppermute(x, 'dev', [(i, i ^ k) for i in range(peers)])  99.5 us
    pallas_call x8, Pallas kernels, apply_dense(): pl.pallas_call(functools.partial(apply_kernel, len(xs), acc is not None,...  38.2 us
    ppermute x28, starting transfers between devices, swap(): return lax.ppermute(x, 'dev', [(i, i ^ k) for i in range(peers)])  22.1 us
    pallas_call x4, Pallas kernels, finish(): pl.pallas_call(functools.partial(finish_kernel, plan, len(xs), bool(squar...  12.4 us
    pallas_call x2, Pallas kernels, mix(): pl.pallas_call(mix_kernel, grid=(x.shape[0] // STEP,), out_shape=jax.Shap...  7.24 us
    ppermute x4, starting transfers between devices, start(): lower = lax.ppermute(sends[len(chips)], 'dom', up)  5.96 us
    ppermute x4, starting transfers between devices, start(): upper = lax.ppermute(sends[len(chips) + 1], 'dom', down)  5.59 us
    unnamed x18, local copies, waits for them, and re-layouts  4.78 us
  transfers between devices with their start and end apart: 36, of which 27 were waited for; matrix products, arithmetic and copies ran while one was open for 0% of the time, Pallas kernels for 25%

profile of v3, /device:TPU:0, one launch (start us, length us, event | category | flops | bytes accessed | tf_op | source)
XLA Modules:
  0.0 213.7 jit_solution(6289866394133301238)
XLA Ops:
  5.1 5.1 %collective-permute-start.3 = (f32[2,128,512]{2,1,0:T(8,128)}, f32[2,128,512]{2,1,0:T(8,128)S(1)}, u32[]{:S(2)}, u32[]{:S(2)}) collective-permute-start(f32[2,128,512]{2,1,0:T(8,128)} %get-tuple-element.74), channel_id=1, source_target_pairs={{0,6},{1,7},{2,4},{3,5},{4,2},{5,3},{6,0},{7,1},{8,14},{9,15},{10,... | collective-permute-start | bytes 1572872 | tf_op jit(solution)/shard_map/ppermute | solution.py:334
  22.7 3.4 %shard_map.91 = (bf16[8,128,1024]{2,1,0:T(8,128)(2,1)S(1)}, bf16[8,128,1024]{2,1,0:T(8,128)(2,1)S(1)}, bf16[8,128,1152]{2,1,0:T(8,128)(2,1)S(1)}, bf16[8,128,115...) custom-call(s32[80]{0:T(128)S(1)} %copy-done.6, ...), custom_call_target="tpu_custom_call" | custom-call | flops 1 | bytes 1 | tf_op jit(solution)/shard_map/pallas_call | solution.py:72
  26.1 3.9 %shard_map.93.refs_7_ = f32[8,128,512]{2,1,0:T(8,128)S(1)} custom-call(bf16[8,128,1024]{2,1,0:T(8,128)(2,1)S(1)} %get-tuple-element.76.ah_ref, bf16[8,128,1024]{2,1,0:T(8,128)(2,1)S(1)} %get-tuple-element.77.al_ref, f32[8,128,512]{2,1,0:T(8,128)S(1)} %bitcast.14), custom_call_target="tpu_custom_call" | custom-call | flops 1 | bytes 1 | tf_op jit(solution)/shard_map/pallas_call | solution.py:158
  30.1 4.7 %collective-permute-done.4.refs_3_ = f32[2,128,512]{2,1,0:T(8,128)S(1)} collective-permute-done((f32[2,128,512]{2,1,0:T(8,128)}, f32[2,128,512]{2,1,0:T(8,128)S(1)}, u32[]{:S(2)}, u32[]{:S(2)}) %collective-permute-start.4) | collective-permute-done | bytes 524320 | tf_op jit(solution)/shard_map/ppermute | solution.py:334
  37.1 4.8 %shard_map.94.acc_ref = f32[8,128,512]{2,1,0:T(8,128)S(1)} custom-call(bf16[8,128,1152]{2,1,0:T(8,128)(2,1)S(1)} %get-tuple-element.69.ah_ref, bf16[8,128,1152]{2,1,0:T(8,128)(2,1)S(1)} %get-tuple-element.70.al_ref, f32[2,128,512]{2,1,0:T(8,128)S(1)} %collective-permute-done.1.refs_0_, f32[2,128,512]{2,1,0:T(8,128)S(1)} %collective-permute-done.2.refs_1_, ...), custom_call_target="tpu_custom_call" | custom-call | flops 1 | bytes 1 | tf_op jit(solution)/shard_map/pallas_call | solution.py:158
  41.9 13.3 %collective-permute-done.refs_0_ = f32[2,128,512]{2,1,0:T(8,128)S(1)} collective-permute-done((f32[2,128,512]{2,1,0:T(8,128)S(1)}, f32[2,128,512]{2,1,0:T(8,128)S(1)}, u32[]{:S(2)}, u32[]{:S(2)}) %collective-permute-start) | collective-permute-done | bytes 524320 | tf_op jit(solution)/shard_map/ppermute | solution.py:334
  66.5 4.1 %shard_map.97 = (bf16[2,512,512]{2,1,0:T(8,128)(2,1)S(1)}, bf16[2,512,512]{2,1,0:T(8,128)(2,1)S(1)}, bf16[2,512,512]{2,1,0:T(8,128)(2,1)S(1)}, bf16[2,512,512]{2,1,0:T(8,128)(2,1)S(1)}) custom-call(f32[2,512,512]{2,1,0:T(8,128)S(1)} %copy-done.3), custom_call_target="tpu_custom_call" | custom-call | flops 1 | bytes 1 | tf_op jit(solution)/shard_map/pallas_call | solution.py:96
  70.6 3.9 %shard_map.96.twice_ref = f32[8,128,512]{2,1,0:T(8,128)S(1)} custom-call(bf16[8,128,1024]{2,1,0:T(8,128)(2,1)S(1)} %get-tuple-element.76.ah_ref, bf16[8,128,1024]{2,1,0:T(8,128)(2,1)S(1)} %get-tuple-element.77.al_ref, f32[8,128,512]{2,1,0:T(8,128)S(1)} %get-tuple-element.90.refs_0_.once_ref), custom_call_target="tpu_custom_call" | custom-call | flops 1 | bytes 1 | tf_op jit(solution)/shard_map/pallas_call | solution.py:158
  74.5 3.6 %shard_map.98.refs_7_ = f32[8,128,512]{2,1,0:T(8,128)S(1)} custom-call(f32[8,128,512]{2,1,0:T(8,128)S(1)} %bitcast.15, f32[8,128,512]{2,1,0:T(8,128)S(1)} %get-tuple-element.90.refs_0_.once_ref, f32[8,128,512]{2,1,0:T(8,128)S(1)} %shard_map.96.twice_ref, bf16[2,512,512]{2,1,0:T(8,128)(2,1)S(1)} %get-tuple-element.91.sh_ref, ...), custom_call_target="tpu_custom_call" | custom-call | flops 1 | bytes 1 | tf_op jit(solution)/shard_map/pallas_call | solution.py:180
  78.2 10.9 %collective-permute-done.13.refs_3_ = f32[2,128,512]{2,1,0:T(8,128)S(1)} collective-permute-done((f32[2,128,512]{2,1,0:T(8,128)S(1)}, f32[2,128,512]{2,1,0:T(8,128)S(1)}, u32[]{:S(2)}, u32[]{:S(2)}) %collective-permute-start.13) | collective-permute-done | bytes 524320 | tf_op jit(solution)/shard_map/ppermute | solution.py:334
  91.5 6.5 %shard_map.99.acc_ref = f32[8,128,512]{2,1,0:T(8,128)S(1)} custom-call(bf16[8,128,1152]{2,1,0:T(8,128)(2,1)S(1)} %get-tuple-element.69.ah_ref, bf16[8,128,1152]{2,1,0:T(8,128)(2,1)S(1)} %get-tuple-element.70.al_ref, f32[2,128,512]{2,1,0:T(8,128)S(1)} %collective-permute-done.10.refs_0_, f32[2,128,512]{2,1,0:T(8,128)S(1)} %collective-permute-done.11.refs_1_, ...), custom_call_target="tpu_custom_call" | custom-call | flops 1 | bytes 1 | tf_op jit(solution)/shard_map/pallas_call | solution.py:158
  98.0 8.0 %collective-permute-done.9.refs_0_ = f32[2,128,512]{2,1,0:T(8,128)S(1)} collective-permute-done((f32[2,128,512]{2,1,0:T(8,128)S(1)}, f32[2,128,512]{2,1,0:T(8,128)S(1)}, u32[]{:S(2)}, u32[]{:S(2)}) %collective-permute-start.9) | collective-permute-done | bytes 524320 | tf_op jit(solution)/shard_map/ppermute | solution.py:334
  107.6 3.7 %shard_map.100 = (f32[8,128,512]{2,1,0:T(8,128)S(1)}, f32[2,128,512]{2,1,0:T(8,128)S(1)}, f32[2,128,512]{2,1,0:T(8,128)S(1)}, f32[2,128,512]{2,1,0:T(8,128)S(1)}...) custom-call(s32[1]{0:T(128)} %bitcast.me_ref, s32[8,1]{1,0:T(8,128)S(1)} %copy.14.near_ref, ...), custom_call_target="tpu_custom_call" | custom-call | flops 1 | bytes 1 | tf_op jit(solution)/shard_map/pallas_call | solution.py:280
  118.7 3.9 %shard_map.101.refs_7_ = f32[8,128,512]{2,1,0:T(8,128)S(1)} custom-call(bf16[8,128,1024]{2,1,0:T(8,128)(2,1)S(1)} %get-tuple-element.76.ah_ref, bf16[8,128,1024]{2,1,0:T(8,128)(2,1)S(1)} %get-tuple-element.77.al_ref, f32[8,128,512]{2,1,0:T(8,128)S(1)} %get-tuple-element.107.refs_0_.x_ref), custom_call_target="tpu_custom_call" | custom-call | flops 1 | bytes 1 | tf_op jit(solution)/shard_map/pallas_call | solution.py:158
  122.6 5.4 %collective-permute-done.21.refs_2_ = f32[2,128,512]{2,1,0:T(8,128)S(1)} collective-permute-done((f32[2,128,512]{2,1,0:T(8,128)S(1)}, f32[2,128,512]{2,1,0:T(8,128)S(1)}, u32[]{:S(2)}, u32[]{:S(2)}) %collective-permute-start.21) | collective-permute-done | bytes 524320 | tf_op jit(solution)/shard_map/ppermute | solution.py:334
  128.0 13.6 %collective-permute-done.22.refs_3_ = f32[2,128,512]{2,1,0:T(8,128)S(1)} collective-permute-done((f32[2,128,512]{2,1,0:T(8,128)S(1)}, f32[2,128,512]{2,1,0:T(8,128)S(1)}, u32[]{:S(2)}, u32[]{:S(2)}) %collective-permute-start.22) | collective-permute-done | bytes 524320 | tf_op jit(solution)/shard_map/ppermute | solution.py:334
  144.0 4.8 %shard_map.102.acc_ref = f32[8,128,512]{2,1,0:T(8,128)S(1)} custom-call(bf16[8,128,1152]{2,1,0:T(8,128)(2,1)S(1)} %get-tuple-element.69.ah_ref, bf16[8,128,1152]{2,1,0:T(8,128)(2,1)S(1)} %get-tuple-element.70.al_ref, f32[2,128,512]{2,1,0:T(8,128)S(1)} %collective-permute-done.19.refs_0_, f32[2,128,512]{2,1,0:T(8,128)S(1)} %collective-permute-done.20.refs_1_, ...), custom_call_target="tpu_custom_call" | custom-call | flops 1 | bytes 1 | tf_op jit(solution)/shard_map/pallas_call | solution.py:158
  148.7 8.3 %collective-permute-done.18.refs_0_ = f32[2,128,512]{2,1,0:T(8,128)S(1)} collective-permute-done((f32[2,128,512]{2,1,0:T(8,128)S(1)}, f32[2,128,512]{2,1,0:T(8,128)S(1)}, u32[]{:S(2)}, u32[]{:S(2)}) %collective-permute-start.18) | collective-permute-done | bytes 524320 | tf_op jit(solution)/shard_map/ppermute | solution.py:334
  168.3 3.9 %shard_map.104.twice_ref = f32[8,128,512]{2,1,0:T(8,128)S(1)} custom-call(bf16[8,128,1024]{2,1,0:T(8,128)(2,1)S(1)} %get-tuple-element.76.ah_ref, bf16[8,128,1024]{2,1,0:T(8,128)(2,1)S(1)} %get-tuple-element.77.al_ref, f32[8,128,512]{2,1,0:T(8,128)S(1)} %get-tuple-element.120.refs_0_.once_ref), custom_call_target="tpu_custom_call" | custom-call | flops 1 | bytes 1 | tf_op jit(solution)/shard_map/pallas_call | solution.py:158
  172.2 3.6 %shard_map.105.refs_7_ = f32[8,128,512]{2,1,0:T(8,128)S(1)} custom-call(f32[8,128,512]{2,1,0:T(8,128)S(1)} %get-tuple-element.107.refs_0_.x_ref, f32[8,128,512]{2,1,0:T(8,128)S(1)} %get-tuple-element.120.refs_0_.once_ref, f32[8,128,512]{2,1,0:T(8,128)S(1)} %shard_map.104.twice_ref, bf16[2,512,512]{2,1,0:T(8,128)(2,1)S(1)} %get-tuple-element.91.sh_ref, ...), custom_call_target="tpu_custom_call" | custom-call | flops 1 | bytes 1 | tf_op jit(solution)/shard_map/pallas_call | solution.py:180
  177.6 13.3 %collective-permute-done.31.refs_3_ = f32[2,128,512]{2,1,0:T(8,128)S(1)} collective-permute-done((f32[2,128,512]{2,1,0:T(8,128)S(1)}, f32[2,128,512]{2,1,0:T(8,128)S(1)}, u32[]{:S(2)}, u32[]{:S(2)}) %collective-permute-start.31) | collective-permute-done | bytes 524320 | tf_op jit(solution)/shard_map/ppermute | solution.py:334
  193.3 6.5 %shard_map.106.acc_ref = f32[8,128,512]{2,1,0:T(8,128)S(1)} custom-call(bf16[8,128,1152]{2,1,0:T(8,128)(2,1)S(1)} %get-tuple-element.69.ah_ref, bf16[8,128,1152]{2,1,0:T(8,128)(2,1)S(1)} %get-tuple-element.70.al_ref, f32[2,128,512]{2,1,0:T(8,128)S(1)} %collective-permute-done.28.refs_0_, f32[2,128,512]{2,1,0:T(8,128)S(1)} %collective-permute-done.29.refs_1_, ...), custom_call_target="tpu_custom_call" | custom-call | flops 1 | bytes 1 | tf_op jit(solution)/shard_map/pallas_call | solution.py:158
  199.8 8.0 %collective-permute-done.27.refs_0_ = f32[2,128,512]{2,1,0:T(8,128)S(1)} collective-permute-done((f32[2,128,512]{2,1,0:T(8,128)S(1)}, f32[2,128,512]{2,1,0:T(8,128)S(1)}, u32[]{:S(2)}, u32[]{:S(2)}) %collective-permute-start.27) | collective-permute-done | bytes 524320 | tf_op jit(solution)/shard_map/ppermute | solution.py:334
  209.4 4.3 %shard_map.107 = f32[8,128,512]{2,1,0:T(8,128)} custom-call(s32[1]{0:T(128)} %bitcast.me_ref, s32[8,1]{1,0:T(8,128)S(1)} %copy.14.near_ref, s32[2,2]{1,0:T(2,128)S(1)} %bitcast.20, bf16[8,128,256]{2,1,0:T(8,128)(2,1)S(1)} %get-tuple-element.66.ah_ref, bf16[8,128,256]{2,1,0:T(8,128)(2,1)S(1)} %get-tuple-element.67.al_ref, ...), custom_call_target="tpu_custom_call" | custom-call | flops 1 | bytes 1 | tf_op jit(solution)/shard_map/pallas_call | solution.py:280
  (98 shorter events, 56.2 us)
Async XLA Ops:
  5.1 24.9 %collective-permute-start.3 = (f32[2,128,512]{2,1,0:T(8,128)}, f32[2,128,512]{2,1,0:T(8,128)S(1)}, u32[]{:S(2)}, u32[]{:S(2)}) collective-permute-start(f32[2,128,512]{2,1,0:T(8,128)} %get-tuple-element.74), channel_id=1, source_target_pairs={{0,6},{1,7},{2,4},{3,5},{4,2},{5,3},{6,0},{7,1},{8,14},{9,15},{10,... | collective-permute-start | bytes 1572872 | tf_op jit(solution)/shard_map/ppermute | solution.py:334
  10.2 24.5 %collective-permute-start.4 = (f32[2,128,512]{2,1,0:T(8,128)}, f32[2,128,512]{2,1,0:T(8,128)S(1)}, u32[]{:S(2)}, u32[]{:S(2)}) collective-permute-start(f32[2,128,512]{2,1,0:T(8,128)} %get-tuple-element.75), channel_id=1, source_target_pairs={{0,2},{1,3},{2,0},{3,1},{4,6},{5,7},{6,4},{7,5},{8,10},{9,11},{10,... | collective-permute-start | bytes 1572872 | tf_op jit(solution)/shard_map/ppermute | solution.py:334
  10.2 25.1 %collective-permute-start.1 = (f32[2,128,512]{2,1,0:T(8,128)}, f32[2,128,512]{2,1,0:T(8,128)S(1)}, u32[]{:S(2)}, u32[]{:S(2)}) collective-permute-start(f32[2,128,512]{2,1,0:T(8,128)} %get-tuple-element.71), channel_id=1, source_target_pairs={{0,8},{8,16},{16,24},{24,0},{1,9},{9,17},{17,25},{25,1},{2,10},{10... | collective-permute-start | bytes 1572872 | tf_op jit(solution)/shard_map/ppermute | solution.py:342
  11.7 43.5 %collective-permute-start = (f32[2,128,512]{2,1,0:T(8,128)S(1)}, f32[2,128,512]{2,1,0:T(8,128)S(1)}, u32[]{:S(2)}, u32[]{:S(2)}) collective-permute-start(f32[2,128,512]{2,1,0:T(8,128)S(1)} %get-tuple-element.68), channel_id=1, source_target_pairs={{0,4},{1,5},{2,6},{3,7},{4,0},{5,1},{6,2},{7,3},{8,12},{9,13},{10,... | collective-permute-start | bytes 1572872 | tf_op jit(solution)/shard_map/ppermute | solution.py:334
  12.5 23.5 %collective-permute-start.2 = (f32[2,128,512]{2,1,0:T(8,128)}, f32[2,128,512]{2,1,0:T(8,128)S(1)}, u32[]{:S(2)}, u32[]{:S(2)}) collective-permute-start(f32[2,128,512]{2,1,0:T(8,128)} %get-tuple-element.72), channel_id=1, source_target_pairs={{8,0},{16,8},{24,16},{0,24},{9,1},{17,9},{25,17},{1,25},{10,2},{18... | collective-permute-start | bytes 1572872 | tf_op jit(solution)/shard_map/ppermute | solution.py:343
  34.9 1.9 collective-permute-start.6
  59.1 19.1 %collective-permute-start.12 = (f32[2,128,512]{2,1,0:T(8,128)S(1)}, f32[2,128,512]{2,1,0:T(8,128)S(1)}, u32[]{:S(2)}, u32[]{:S(2)}) collective-permute-start(f32[2,128,512]{2,1,0:T(8,128)S(1)} %get-tuple-element.88), channel_id=1, source_target_pairs={{0,6},{1,7},{2,4},{3,5},{4,2},{5,3},{6,0},{7,1},{8,14},{9,15},{10,... | collective-permute-start | bytes 1572872 | tf_op jit(solution)/shard_map/ppermute | solution.py:334
  61.6 27.5 %collective-permute-start.13 = (f32[2,128,512]{2,1,0:T(8,128)S(1)}, f32[2,128,512]{2,1,0:T(8,128)S(1)}, u32[]{:S(2)}, u32[]{:S(2)}) collective-permute-start(f32[2,128,512]{2,1,0:T(8,128)S(1)} %get-tuple-element.89), channel_id=1, source_target_pairs={{0,2},{1,3},{2,0},{3,1},{4,6},{5,7},{6,4},{7,5},{8,10},{9,11},{10,... | collective-permute-start | bytes 1572872 | tf_op jit(solution)/shard_map/ppermute | solution.py:334
  61.6 28.1 %collective-permute-start.10 = (f32[2,128,512]{2,1,0:T(8,128)S(1)}, f32[2,128,512]{2,1,0:T(8,128)S(1)}, u32[]{:S(2)}, u32[]{:S(2)}) collective-permute-start(f32[2,128,512]{2,1,0:T(8,128)S(1)} %get-tuple-element.85), channel_id=1, source_target_pairs={{0,8},{8,16},{16,24},{24,0},{1,9},{9,17},{17,25},{25,1},{2,10},{10... | collective-permute-start | bytes 1572872 | tf_op jit(solution)/shard_map/ppermute | solution.py:342
  63.1 26.7 %collective-permute-start.11 = (f32[2,128,512]{2,1,0:T(8,128)S(1)}, f32[2,128,512]{2,1,0:T(8,128)S(1)}, u32[]{:S(2)}, u32[]{:S(2)}) collective-permute-start(f32[2,128,512]{2,1,0:T(8,128)S(1)} %get-tuple-element.86), channel_id=1, source_target_pairs={{8,0},{16,8},{24,16},{0,24},{9,1},{17,9},{25,17},{1,25},{10,2},{18... | collective-permute-start | bytes 1572872 | tf_op jit(solution)/shard_map/ppermute | solution.py:343
  64.6 41.4 %collective-permute-start.9 = (f32[2,128,512]{2,1,0:T(8,128)S(1)}, f32[2,128,512]{2,1,0:T(8,128)S(1)}, u32[]{:S(2)}, u32[]{:S(2)}) collective-permute-start(f32[2,128,512]{2,1,0:T(8,128)S(1)} %get-tuple-element.84), channel_id=1, source_target_pairs={{0,4},{1,5},{2,6},{3,7},{4,0},{5,1},{6,2},{7,3},{8,12},{9,13},{10,... | collective-permute-start | bytes 1572872 | tf_op jit(solution)/shard_map/ppermute | solution.py:334
  89.2 1.9 collective-permute-start.15
  111.3 16.7 %collective-permute-start.21 = (f32[2,128,512]{2,1,0:T(8,128)S(1)}, f32[2,128,512]{2,1,0:T(8,128)S(1)}, u32[]{:S(2)}, u32[]{:S(2)}) collective-permute-start(f32[2,128,512]{2,1,0:T(8,128)S(1)} %get-tuple-element.105), channel_id=1, source_target_pairs={{0,6},{1,7},{2,4},{3,5},{4,2},{5,3},{6,0},{7,1},{8,14},{9,15},{10,... | collective-permute-start | bytes 1572872 | tf_op jit(solution)/shard_map/ppermute | solution.py:334
  112.7 28.9 %collective-permute-start.22 = (f32[2,128,512]{2,1,0:T(8,128)S(1)}, f32[2,128,512]{2,1,0:T(8,128)S(1)}, u32[]{:S(2)}, u32[]{:S(2)}) collective-permute-start(f32[2,128,512]{2,1,0:T(8,128)S(1)} %get-tuple-element.106), channel_id=1, source_target_pairs={{0,2},{1,3},{2,0},{3,1},{4,6},{5,7},{6,4},{7,5},{8,10},{9,11},{10,... | collective-permute-start | bytes 1572872 | tf_op jit(solution)/shard_map/ppermute | solution.py:334
  112.7 29.5 %collective-permute-start.19 = (f32[2,128,512]{2,1,0:T(8,128)S(1)}, f32[2,128,512]{2,1,0:T(8,128)S(1)}, u32[]{:S(2)}, u32[]{:S(2)}) collective-permute-start(f32[2,128,512]{2,1,0:T(8,128)S(1)} %get-tuple-element.102), channel_id=1, source_target_pairs={{0,8},{8,16},{16,24},{24,0},{1,9},{9,17},{17,25},{25,1},{2,10},{10... | collective-permute-start | bytes 1572872 | tf_op jit(solution)/shard_map/ppermute | solution.py:342
  114.2 28.1 %collective-permute-start.20 = (f32[2,128,512]{2,1,0:T(8,128)S(1)}, f32[2,128,512]{2,1,0:T(8,128)S(1)}, u32[]{:S(2)}, u32[]{:S(2)}) collective-permute-start(f32[2,128,512]{2,1,0:T(8,128)S(1)} %get-tuple-element.103), channel_id=1, source_target_pairs={{8,0},{16,8},{24,16},{0,24},{9,1},{17,9},{25,17},{1,25},{10,2},{18... | collective-permute-start | bytes 1572872 | tf_op jit(solution)/shard_map/ppermute | solution.py:343
  115.6 41.4 %collective-permute-start.18 = (f32[2,128,512]{2,1,0:T(8,128)S(1)}, f32[2,128,512]{2,1,0:T(8,128)S(1)}, u32[]{:S(2)}, u32[]{:S(2)}) collective-permute-start(f32[2,128,512]{2,1,0:T(8,128)S(1)} %get-tuple-element.101), channel_id=1, source_target_pairs={{0,4},{1,5},{2,6},{3,7},{4,0},{5,1},{6,2},{7,3},{8,12},{9,13},{10,... | collective-permute-start | bytes 1572872 | tf_op jit(solution)/shard_map/ppermute | solution.py:334
  141.7 1.9 collective-permute-start.24
  160.9 16.7 %collective-permute-start.30 = (f32[2,128,512]{2,1,0:T(8,128)S(1)}, f32[2,128,512]{2,1,0:T(8,128)S(1)}, u32[]{:S(2)}, u32[]{:S(2)}) collective-permute-start(f32[2,128,512]{2,1,0:T(8,128)S(1)} %get-tuple-element.118), channel_id=1, source_target_pairs={{0,6},{1,7},{2,4},{3,5},{4,2},{5,3},{6,0},{7,1},{8,14},{9,15},{10,... | collective-permute-start | bytes 1572872 | tf_op jit(solution)/shard_map/ppermute | solution.py:334
  163.4 27.5 %collective-permute-start.31 = (f32[2,128,512]{2,1,0:T(8,128)S(1)}, f32[2,128,512]{2,1,0:T(8,128)S(1)}, u32[]{:S(2)}, u32[]{:S(2)}) collective-permute-start(f32[2,128,512]{2,1,0:T(8,128)S(1)} %get-tuple-element.119), channel_id=1, source_target_pairs={{0,2},{1,3},{2,0},{3,1},{4,6},{5,7},{6,4},{7,5},{8,10},{9,11},{10,... | collective-permute-start | bytes 1572872 | tf_op jit(solution)/shard_map/ppermute | solution.py:334
  163.4 28.1 %collective-permute-start.28 = (f32[2,128,512]{2,1,0:T(8,128)S(1)}, f32[2,128,512]{2,1,0:T(8,128)S(1)}, u32[]{:S(2)}, u32[]{:S(2)}) collective-permute-start(f32[2,128,512]{2,1,0:T(8,128)S(1)} %get-tuple-element.115), channel_id=1, source_target_pairs={{0,8},{8,16},{16,24},{24,0},{1,9},{9,17},{17,25},{25,1},{2,10},{10... | collective-permute-start | bytes 1572872 | tf_op jit(solution)/shard_map/ppermute | solution.py:342
  164.9 26.7 %collective-permute-start.29 = (f32[2,128,512]{2,1,0:T(8,128)S(1)}, f32[2,128,512]{2,1,0:T(8,128)S(1)}, u32[]{:S(2)}, u32[]{:S(2)}) collective-permute-start(f32[2,128,512]{2,1,0:T(8,128)S(1)} %get-tuple-element.116), channel_id=1, source_target_pairs={{8,0},{16,8},{24,16},{0,24},{9,1},{17,9},{25,17},{1,25},{10,2},{18... | collective-permute-start | bytes 1572872 | tf_op jit(solution)/shard_map/ppermute | solution.py:343
  166.4 41.4 %collective-permute-start.27 = (f32[2,128,512]{2,1,0:T(8,128)S(1)}, f32[2,128,512]{2,1,0:T(8,128)S(1)}, u32[]{:S(2)}, u32[]{:S(2)}) collective-permute-start(f32[2,128,512]{2,1,0:T(8,128)S(1)} %get-tuple-element.114), channel_id=1, source_target_pairs={{0,4},{1,5},{2,6},{3,7},{4,0},{5,1},{6,2},{7,3},{8,12},{9,13},{10,... | collective-permute-start | bytes 1572872 | tf_op jit(solution)/shard_map/ppermute | solution.py:334
  191.0 1.9 collective-permute-start.33
  (21 other events, 113.1 us)

commit v4 on v3

--- a/solution.py
+++ b/solution.py
@@ -36,8 +36,8 @@
     return pl.BlockSpec((None,) + array.shape[1:], lambda i: (layer, 0, 0))
 
 
-def rows_of(shape):
-    return pl.BlockSpec((STEP,) + shape[1:], lambda i: (i,) + (0,) * (len(shape) - 1))
+def rows_of(shape, step=STEP):
+    return pl.BlockSpec((step,) + shape[1:], lambda i: (i,) + (0,) * (len(shape) - 1))
 
 
 def dense_kernel(rows_ref, cols_ref, count_ref, vals_ref, *refs):
@@ -191,12 +191,12 @@
 def picked(plan, me, near_ref, far_ref):
     for entries in plan:
         blocks = []
-        for kind, index in entries:
+        for kind, index, count in entries:
             if kind == "near":
                 peer = me ^ index
-                blocks += [near_ref[peer, i] for i in range(near_ref.shape[1])]
+                blocks += [near_ref[peer * count + i] for i in range(count)]
             else:
-                blocks += [far_ref[index, i] for i in range(far_ref.shape[1])]
+                blocks += [far_ref[index, i] for i in range(count)]
         yield blocks
 
 
@@ -210,8 +210,8 @@
         copy.wait()
 
 
-def plan_sizes(plan, near, far):
-    return [sum(near.shape[1] if kind == "near" else far.shape[1] for kind, _ in e) for e in plan]
+def plan_sizes(plan):
+    return [sum(count for _, _, count in entries) for entries in plan]
 
 
 def pick_kernel(plan, me_ref, near_ref, far_ref, x_ref, *refs):
@@ -220,15 +220,14 @@
 
 def pick(x, route):
     plan, me, near, far = route
-    sizes = plan_sizes(plan, near, far)
-    hbm = pl.BlockSpec(memory_space=pl.ANY)
+    sizes = plan_sizes(plan)
     return pl.pallas_call(
         functools.partial(pick_kernel, plan),
         out_shape=[jax.ShapeDtypeStruct((n,) + x.shape[1:], x.dtype) for n in sizes],
-        in_specs=[smem()] * 3 + [pl.BlockSpec(memory_space=pltpu.VMEM)],
-        out_specs=[hbm] * len(sizes),
+        in_specs=[smem()] * 3 + [pl.BlockSpec(memory_space=pl.ANY)],
+        out_specs=[pl.BlockSpec(memory_space=pltpu.VMEM)] * len(sizes),
         scratch_shapes=[pltpu.SemaphoreType.DMA((sum(sizes),))],
-        compiler_params=pltpu.CompilerParams(vmem_limit_bytes=16 * MIB),
+        compiler_params=pltpu.CompilerParams(vmem_limit_bytes=56 * MIB),
         cost_estimate=SMALL,
     )(me, near, far, x)
 
@@ -256,7 +255,7 @@
     o_ref[...] = out
     if n_send:
         kept, sems = refs
-        kept[pl.ds(step * STEP, STEP)] = out
+        kept[pl.ds(step * out.shape[0], out.shape[0])] = out
 
         @pl.when(step == pl.num_programs(0) - 1)
         def _():
@@ -265,12 +264,13 @@
 
 def finish(dense, xs, acc, route, square=(), send=True):
     plan, me, near, far = route
-    sizes = plan_sizes(plan, near, far) if send else []
+    sizes = plan_sizes(plan) if send else []
     ah, al = dense
+    step = acc.shape[0] if send else STEP
     depth, width = ah.shape[2], acc.shape[2]
     field = jax.ShapeDtypeStruct(acc.shape, jnp.float32)
     args = [me, near, far, ah, al, acc] + [x for x, _ in xs]
-    specs = [smem()] * 3 + [rows_of(ah.shape), rows_of(al.shape), rows_of(acc.shape)]
+    specs = [smem()] * 3 + [rows_of(ah.shape, step), rows_of(al.shape, step), rows_of(acc.shape, step)]
     specs += [front(x, n) for x, n in xs]
     args += [q for q, _ in square]
     specs += [of_layer(q) for q in square]
@@ -279,10 +279,10 @@
         scratch += [pltpu.VMEM(acc.shape, jnp.float32), pltpu.SemaphoreType.DMA((sum(sizes),))]
     return pl.pallas_call(
         functools.partial(finish_kernel, plan, len(xs), bool(square), len(sizes)),
-        grid=(acc.shape[0] // STEP,),
+        grid=(acc.shape[0] // step,),
         out_shape=[field] + [jax.ShapeDtypeStruct((n, TILE, width), jnp.float32) for n in sizes],
         in_specs=specs,
-        out_specs=[rows_of(acc.shape)] + [pl.BlockSpec(memory_space=pl.ANY)] * len(sizes),
+        out_specs=[rows_of(acc.shape, step)] + [pl.BlockSpec(memory_space=pl.ANY)] * len(sizes),
         scratch_shapes=scratch,
         compiler_params=pltpu.CompilerParams(vmem_limit_bytes=24 * MIB),
         cost_estimate=SMALL,
@@ -305,10 +305,10 @@
     late = list(range(peers // 4, peers // 2))[::-1]
     early = list(range(1, peers // 4))
     plan = tuple(
-        [(("near", 2 * j), ("near", 2 * j + 1)) for j in late + early]
-        + [(("far", 0),), (("far", 1),), (("near", 1),)]
+        [(("near", 2 * j, cap), ("near", 2 * j + 1, cap)) for j in late + early]
+        + [(("far", 0, hcap),), (("far", 1, hcap),), (("near", 1, cap),)]
     )
-    route = (plan, me, near_send[0], far_send[0])
+    route = (plan, me, near_send.reshape(-1), far_send[0])
 
     first_k = [2 * j for j in late[:-1] + early] + [1] + [2 * j + 1 for j in late[:-1] + early]
     last_k = [2 * late[-1], 2 * late[-1] + 1]

time: 214 us -> 212 us (level)
  local copies, waits for them, and re-layouts: 6.47 us -> 3.4 us
    unnamed x18 -> x16, local copies, waits for them, and re-layouts: 4.78 us -> 2.51 us
    pallas_call x1, Pallas kernels: 2.03 us -> 4.26 us  [pick(): pl.pallas_call(functools.partial(pick_kernel, plan), out_shape=[jax.Shape...]
  transfers between devices with their start and end apart: 36 -> 36, of which waited for: 27 -> 26; matrix products, arithmetic and copies ran while one was open for 0% -> 0% of each run, Pallas kernels for 25% -> 25%
where the time goes in v4:
time: 212 us
  waiting for transfers between devices  100 us (47%)
  Pallas kernels  68.8 us (32%)
  starting transfers between devices  33.8 us (16%)
  between operations  5.83 us (3%)
  local copies, waits for them, and re-layouts  3.4 us (2%)
    ppermute x28, waiting for transfers between devices, swap(): return lax.ppermute(x, 'dev', [(i, i ^ k) for i in range(peers)])  99 us
    pallas_call x8, Pallas kernels, apply_dense(): pl.pallas_call(functools.partial(apply_kernel, len(xs), acc is not None,...  38.2 us
    ppermute x28, starting transfers between devices, swap(): return lax.ppermute(x, 'dev', [(i, i ^ k) for i in range(peers)])  22.3 us
    pallas_call x4, Pallas kernels, finish(): pl.pallas_call(functools.partial(finish_kernel, plan, len(xs), bool(squar...  11.4 us
    pallas_call x2, Pallas kernels, mix(): pl.pallas_call(mix_kernel, grid=(x.shape[0] // STEP,), out_shape=jax.Shap...  7.24 us
    ppermute x4, starting transfers between devices, start(): lower = lax.ppermute(sends[len(chips)], 'dom', up)  5.81 us
    ppermute x4, starting transfers between devices, start(): upper = lax.ppermute(sends[len(chips) + 1], 'dom', down)  5.74 us
    pallas_call x1, Pallas kernels, pick(): pl.pallas_call(functools.partial(pick_kernel, plan), out_shape=[jax.Shape...  4.26 us
  transfers between devices with their start and end apart: 36, of which 26 were waited for; matrix products, arithmetic and copies ran while one was open for 0% of the time, Pallas kernels for 25%

profile of v4, /device:TPU:0, one launch (start us, length us, event | category | flops | bytes accessed | tf_op | source)
XLA Modules:
  0.0 212.0 jit_solution(13727329918542736068)
XLA Ops:
  0.0 4.3 %shard_map.92 = (f32[2,128,512]{2,1,0:T(8,128)}, f32[2,128,512]{2,1,0:T(8,128)}, f32[2,128,512]{2,1,0:T(8,128)}, f32[2,128,512]{2,1,0:T(8,128)}, f32[2,128,512]{2,1,0:T(8,128)}, /*index=5*/f32[1,128,512]{2,1,0:T(8,128)}) custom-call(s32[1]{0:T(128)} %bitcast.me_ref, s32[8]{0:T(128)} %bitcast.16, s32[2,2]{1,0:T(2,128)} %bitcast.21, f32[8,128,512]{2,1,0:T(8,128)} %bitcast.13), custom_call_target="tpu_custom_call" | custom-call | flops 1 | bytes 1 | tf_op jit(solution)/shard_map/pallas_call | solution.py:224
  4.3 5.2 %collective-permute-start.3 = (f32[2,128,512]{2,1,0:T(8,128)}, f32[2,128,512]{2,1,0:T(8,128)S(1)}, u32[]{:S(2)}, u32[]{:S(2)}) collective-permute-start(f32[2,128,512]{2,1,0:T(8,128)} %get-tuple-element.74), channel_id=1, source_target_pairs={{0,6},{1,7},{2,4},{3,5},{4,2},{5,3},{6,0},{7,1},{8,14},{9,15},{10,... | collective-permute-start | bytes 1572872 | tf_op jit(solution)/shard_map/ppermute | solution.py:334
  21.8 3.6 %shard_map.91 = (bf16[8,128,1024]{2,1,0:T(8,128)(2,1)S(1)}, bf16[8,128,1024]{2,1,0:T(8,128)(2,1)S(1)}, bf16[8,128,1152]{2,1,0:T(8,128)(2,1)S(1)}, bf16[8,128,115...) custom-call(s32[80]{0:T(128)S(1)} %copy-done.5, ...), custom_call_target="tpu_custom_call" | custom-call | flops 1 | bytes 1 | tf_op jit(solution)/shard_map/pallas_call | solution.py:72
  25.4 3.9 %shard_map.93.refs_7_ = f32[8,128,512]{2,1,0:T(8,128)S(1)} custom-call(bf16[8,128,1024]{2,1,0:T(8,128)(2,1)S(1)} %get-tuple-element.76.ah_ref, bf16[8,128,1024]{2,1,0:T(8,128)(2,1)S(1)} %get-tuple-element.77.al_ref, f32[8,128,512]{2,1,0:T(8,128)S(1)} %bitcast.14), custom_call_target="tpu_custom_call" | custom-call | flops 1 | bytes 1 | tf_op jit(solution)/shard_map/pallas_call | solution.py:158
  29.4 4.1 %collective-permute-done.4.refs_3_ = f32[2,128,512]{2,1,0:T(8,128)S(1)} collective-permute-done((f32[2,128,512]{2,1,0:T(8,128)}, f32[2,128,512]{2,1,0:T(8,128)S(1)}, u32[]{:S(2)}, u32[]{:S(2)}) %collective-permute-start.4) | collective-permute-done | bytes 524320 | tf_op jit(solution)/shard_map/ppermute | solution.py:334
  35.9 4.8 %shard_map.94.acc_ref = f32[8,128,512]{2,1,0:T(8,128)S(1)} custom-call(bf16[8,128,1152]{2,1,0:T(8,128)(2,1)S(1)} %get-tuple-element.69.ah_ref, bf16[8,128,1152]{2,1,0:T(8,128)(2,1)S(1)} %get-tuple-element.70.al_ref, f32[2,128,512]{2,1,0:T(8,128)S(1)} %collective-permute-done.1.refs_0_, f32[2,128,512]{2,1,0:T(8,128)S(1)} %collective-permute-done.2.refs_1_, ...), custom_call_target="tpu_custom_call" | custom-call | flops 1 | bytes 1 | tf_op jit(solution)/shard_map/pallas_call | solution.py:158
  40.7 14.0 %collective-permute-done.refs_0_ = f32[2,128,512]{2,1,0:T(8,128)S(1)} collective-permute-done((f32[2,128,512]{2,1,0:T(8,128)}, f32[2,128,512]{2,1,0:T(8,128)S(1)}, u32[]{:S(2)}, u32[]{:S(2)}) %collective-permute-start) | collective-permute-done | bytes 524320 | tf_op jit(solution)/shard_map/ppermute | solution.py:334
  65.5 4.1 %shard_map.97 = (bf16[2,512,512]{2,1,0:T(8,128)(2,1)S(1)}, bf16[2,512,512]{2,1,0:T(8,128)(2,1)S(1)}, bf16[2,512,512]{2,1,0:T(8,128)(2,1)S(1)}, bf16[2,512,512]{2,1,0:T(8,128)(2,1)S(1)}) custom-call(f32[2,512,512]{2,1,0:T(8,128)S(1)} %copy-done.2), custom_call_target="tpu_custom_call" | custom-call | flops 1 | bytes 1 | tf_op jit(solution)/shard_map/pallas_call | solution.py:96
  69.7 3.9 %shard_map.96.twice_ref = f32[8,128,512]{2,1,0:T(8,128)S(1)} custom-call(bf16[8,128,1024]{2,1,0:T(8,128)(2,1)S(1)} %get-tuple-element.76.ah_ref, bf16[8,128,1024]{2,1,0:T(8,128)(2,1)S(1)} %get-tuple-element.77.al_ref, f32[8,128,512]{2,1,0:T(8,128)S(1)} %get-tuple-element.90.refs_0_.once_ref), custom_call_target="tpu_custom_call" | custom-call | flops 1 | bytes 1 | tf_op jit(solution)/shard_map/pallas_call | solution.py:158
  73.6 3.6 %shard_map.98.refs_7_ = f32[8,128,512]{2,1,0:T(8,128)S(1)} custom-call(f32[8,128,512]{2,1,0:T(8,128)S(1)} %bitcast.15, f32[8,128,512]{2,1,0:T(8,128)S(1)} %get-tuple-element.90.refs_0_.once_ref, f32[8,128,512]{2,1,0:T(8,128)S(1)} %shard_map.96.twice_ref, bf16[2,512,512]{2,1,0:T(8,128)(2,1)S(1)} %get-tuple-element.91.sh_ref, ...), custom_call_target="tpu_custom_call" | custom-call | flops 1 | bytes 1 | tf_op jit(solution)/shard_map/pallas_call | solution.py:180
  77.2 10.9 %collective-permute-done.13.refs_3_ = f32[2,128,512]{2,1,0:T(8,128)S(1)} collective-permute-done((f32[2,128,512]{2,1,0:T(8,128)S(1)}, f32[2,128,512]{2,1,0:T(8,128)S(1)}, u32[]{:S(2)}, u32[]{:S(2)}) %collective-permute-start.13) | collective-permute-done | bytes 524320 | tf_op jit(solution)/shard_map/ppermute | solution.py:334
  90.6 6.5 %shard_map.99.acc_ref = f32[8,128,512]{2,1,0:T(8,128)S(1)} custom-call(bf16[8,128,1152]{2,1,0:T(8,128)(2,1)S(1)} %get-tuple-element.69.ah_ref, bf16[8,128,1152]{2,1,0:T(8,128)(2,1)S(1)} %get-tuple-element.70.al_ref, f32[2,128,512]{2,1,0:T(8,128)S(1)} %collective-permute-done.10.refs_0_, f32[2,128,512]{2,1,0:T(8,128)S(1)} %collective-permute-done.11.refs_1_, ...), custom_call_target="tpu_custom_call" | custom-call | flops 1 | bytes 1 | tf_op jit(solution)/shard_map/pallas_call | solution.py:158
  97.0 8.0 %collective-permute-done.9.refs_0_ = f32[2,128,512]{2,1,0:T(8,128)S(1)} collective-permute-done((f32[2,128,512]{2,1,0:T(8,128)S(1)}, f32[2,128,512]{2,1,0:T(8,128)S(1)}, u32[]{:S(2)}, u32[]{:S(2)}) %collective-permute-start.9) | collective-permute-done | bytes 524320 | tf_op jit(solution)/shard_map/ppermute | solution.py:334
  117.4 3.9 %shard_map.101.refs_7_ = f32[8,128,512]{2,1,0:T(8,128)S(1)} custom-call(bf16[8,128,1024]{2,1,0:T(8,128)(2,1)S(1)} %get-tuple-element.76.ah_ref, bf16[8,128,1024]{2,1,0:T(8,128)(2,1)S(1)} %get-tuple-element.77.al_ref, f32[8,128,512]{2,1,0:T(8,128)S(1)} %get-tuple-element.107.refs_0_.x_ref), custom_call_target="tpu_custom_call" | custom-call | flops 1 | bytes 1 | tf_op jit(solution)/shard_map/pallas_call | solution.py:158
  121.3 5.4 %collective-permute-done.21.refs_2_ = f32[2,128,512]{2,1,0:T(8,128)S(1)} collective-permute-done((f32[2,128,512]{2,1,0:T(8,128)S(1)}, f32[2,128,512]{2,1,0:T(8,128)S(1)}, u32[]{:S(2)}, u32[]{:S(2)}) %collective-permute-start.21) | collective-permute-done | bytes 524320 | tf_op jit(solution)/shard_map/ppermute | solution.py:334
  126.7 13.6 %collective-permute-done.22.refs_3_ = f32[2,128,512]{2,1,0:T(8,128)S(1)} collective-permute-done((f32[2,128,512]{2,1,0:T(8,128)S(1)}, f32[2,128,512]{2,1,0:T(8,128)S(1)}, u32[]{:S(2)}, u32[]{:S(2)}) %collective-permute-start.22) | collective-permute-done | bytes 524320 | tf_op jit(solution)/shard_map/ppermute | solution.py:334
  142.7 4.8 %shard_map.102.acc_ref = f32[8,128,512]{2,1,0:T(8,128)S(1)} custom-call(bf16[8,128,1152]{2,1,0:T(8,128)(2,1)S(1)} %get-tuple-element.69.ah_ref, bf16[8,128,1152]{2,1,0:T(8,128)(2,1)S(1)} %get-tuple-element.70.al_ref, f32[2,128,512]{2,1,0:T(8,128)S(1)} %collective-permute-done.19.refs_0_, f32[2,128,512]{2,1,0:T(8,128)S(1)} %collective-permute-done.20.refs_1_, ...), custom_call_target="tpu_custom_call" | custom-call | flops 1 | bytes 1 | tf_op jit(solution)/shard_map/pallas_call | solution.py:158
  147.5 8.4 %collective-permute-done.18.refs_0_ = f32[2,128,512]{2,1,0:T(8,128)S(1)} collective-permute-done((f32[2,128,512]{2,1,0:T(8,128)S(1)}, f32[2,128,512]{2,1,0:T(8,128)S(1)}, u32[]{:S(2)}, u32[]{:S(2)}) %collective-permute-start.18) | collective-permute-done | bytes 524320 | tf_op jit(solution)/shard_map/ppermute | solution.py:334
  166.7 3.9 %shard_map.104.twice_ref = f32[8,128,512]{2,1,0:T(8,128)S(1)} custom-call(bf16[8,128,1024]{2,1,0:T(8,128)(2,1)S(1)} %get-tuple-element.76.ah_ref, bf16[8,128,1024]{2,1,0:T(8,128)(2,1)S(1)} %get-tuple-element.77.al_ref, f32[8,128,512]{2,1,0:T(8,128)S(1)} %get-tuple-element.120.refs_0_.once_ref), custom_call_target="tpu_custom_call" | custom-call | flops 1 | bytes 1 | tf_op jit(solution)/shard_map/pallas_call | solution.py:158
  170.7 3.6 %shard_map.105.refs_7_ = f32[8,128,512]{2,1,0:T(8,128)S(1)} custom-call(f32[8,128,512]{2,1,0:T(8,128)S(1)} %get-tuple-element.107.refs_0_.x_ref, f32[8,128,512]{2,1,0:T(8,128)S(1)} %get-tuple-element.120.refs_0_.once_ref, f32[8,128,512]{2,1,0:T(8,128)S(1)} %shard_map.104.twice_ref, bf16[2,512,512]{2,1,0:T(8,128)(2,1)S(1)} %get-tuple-element.91.sh_ref, ...), custom_call_target="tpu_custom_call" | custom-call | flops 1 | bytes 1 | tf_op jit(solution)/shard_map/pallas_call | solution.py:180
  176.1 13.4 %collective-permute-done.31.refs_3_ = f32[2,128,512]{2,1,0:T(8,128)S(1)} collective-permute-done((f32[2,128,512]{2,1,0:T(8,128)S(1)}, f32[2,128,512]{2,1,0:T(8,128)S(1)}, u32[]{:S(2)}, u32[]{:S(2)}) %collective-permute-start.31) | collective-permute-done | bytes 524320 | tf_op jit(solution)/shard_map/ppermute | solution.py:334
  191.9 6.5 %shard_map.106.acc_ref = f32[8,128,512]{2,1,0:T(8,128)S(1)} custom-call(bf16[8,128,1152]{2,1,0:T(8,128)(2,1)S(1)} %get-tuple-element.69.ah_ref, bf16[8,128,1152]{2,1,0:T(8,128)(2,1)S(1)} %get-tuple-element.70.al_ref, f32[2,128,512]{2,1,0:T(8,128)S(1)} %collective-permute-done.28.refs_0_, f32[2,128,512]{2,1,0:T(8,128)S(1)} %collective-permute-done.29.refs_1_, ...), custom_call_target="tpu_custom_call" | custom-call | flops 1 | bytes 1 | tf_op jit(solution)/shard_map/pallas_call | solution.py:158
  198.4 7.8 %collective-permute-done.27.refs_0_ = f32[2,128,512]{2,1,0:T(8,128)S(1)} collective-permute-done((f32[2,128,512]{2,1,0:T(8,128)S(1)}, f32[2,128,512]{2,1,0:T(8,128)S(1)}, u32[]{:S(2)}, u32[]{:S(2)}) %collective-permute-start.27) | collective-permute-done | bytes 524320 | tf_op jit(solution)/shard_map/ppermute | solution.py:334
  207.8 4.2 %shard_map.107 = f32[8,128,512]{2,1,0:T(8,128)} custom-call(s32[1]{0:T(128)} %bitcast.me_ref, s32[8]{0:T(128)S(1)} %bitcast.20, s32[2,2]{1,0:T(2,128)S(1)} %bitcast.25, bf16[8,128,256]{2,1,0:T(8,128)(2,1)S(1)} %get-tuple-element.66.ah_ref, bf16[8,128,256]{2,1,0:T(8,128)(2,1)S(1)} %get-tuple-element.67.al_ref, f32[8,128,512]{2,1,0:T(8,128)S(1)} %shard_map.106.acc_ref, ...), custom_call_target="tpu_custom_call" | custom-call | flops 1 | bytes 1 | tf_op jit(solution)/shard_map/pallas_call | solution.py:280
  (95 shorter events, 53.8 us)
Async XLA Ops:
  4.3 25.1 %collective-permute-start.3 = (f32[2,128,512]{2,1,0:T(8,128)}, f32[2,128,512]{2,1,0:T(8,128)S(1)}, u32[]{:S(2)}, u32[]{:S(2)}) collective-permute-start(f32[2,128,512]{2,1,0:T(8,128)} %get-tuple-element.74), channel_id=1, source_target_pairs={{0,6},{1,7},{2,4},{3,5},{4,2},{5,3},{6,0},{7,1},{8,14},{9,15},{10,... | collective-permute-start | bytes 1572872 | tf_op jit(solution)/shard_map/ppermute | solution.py:334
  9.5 24.0 %collective-permute-start.4 = (f32[2,128,512]{2,1,0:T(8,128)}, f32[2,128,512]{2,1,0:T(8,128)S(1)}, u32[]{:S(2)}, u32[]{:S(2)}) collective-permute-start(f32[2,128,512]{2,1,0:T(8,128)} %get-tuple-element.75), channel_id=1, source_target_pairs={{0,2},{1,3},{2,0},{3,1},{4,6},{5,7},{6,4},{7,5},{8,10},{9,11},{10,... | collective-permute-start | bytes 1572872 | tf_op jit(solution)/shard_map/ppermute | solution.py:334
  9.5 24.6 %collective-permute-start.1 = (f32[2,128,512]{2,1,0:T(8,128)}, f32[2,128,512]{2,1,0:T(8,128)S(1)}, u32[]{:S(2)}, u32[]{:S(2)}) collective-permute-start(f32[2,128,512]{2,1,0:T(8,128)} %get-tuple-element.71), channel_id=1, source_target_pairs={{0,8},{8,16},{16,24},{24,0},{1,9},{9,17},{17,25},{25,1},{2,10},{10... | collective-permute-start | bytes 1572872 | tf_op jit(solution)/shard_map/ppermute | solution.py:342
  11.0 43.7 %collective-permute-start = (f32[2,128,512]{2,1,0:T(8,128)}, f32[2,128,512]{2,1,0:T(8,128)S(1)}, u32[]{:S(2)}, u32[]{:S(2)}) collective-permute-start(f32[2,128,512]{2,1,0:T(8,128)} %get-tuple-element.68), channel_id=1, source_target_pairs={{0,4},{1,5},{2,6},{3,7},{4,0},{5,1},{6,2},{7,3},{8,12},{9,13},{10,... | collective-permute-start | bytes 1572872 | tf_op jit(solution)/shard_map/ppermute | solution.py:334
  11.7 23.5 %collective-permute-start.2 = (f32[2,128,512]{2,1,0:T(8,128)}, f32[2,128,512]{2,1,0:T(8,128)S(1)}, u32[]{:S(2)}, u32[]{:S(2)}) collective-permute-start(f32[2,128,512]{2,1,0:T(8,128)} %get-tuple-element.72), channel_id=1, source_target_pairs={{8,0},{16,8},{24,16},{0,24},{9,1},{17,9},{25,17},{1,25},{10,2},{18... | collective-permute-start | bytes 1572872 | tf_op jit(solution)/shard_map/ppermute | solution.py:343
  33.6 1.9 collective-permute-start.6
  58.1 19.1 %collective-permute-start.12 = (f32[2,128,512]{2,1,0:T(8,128)S(1)}, f32[2,128,512]{2,1,0:T(8,128)S(1)}, u32[]{:S(2)}, u32[]{:S(2)}) collective-permute-start(f32[2,128,512]{2,1,0:T(8,128)S(1)} %get-tuple-element.88), channel_id=1, source_target_pairs={{0,6},{1,7},{2,4},{3,5},{4,2},{5,3},{6,0},{7,1},{8,14},{9,15},{10,... | collective-permute-start | bytes 1572872 | tf_op jit(solution)/shard_map/ppermute | solution.py:334
  60.6 27.6 %collective-permute-start.13 = (f32[2,128,512]{2,1,0:T(8,128)S(1)}, f32[2,128,512]{2,1,0:T(8,128)S(1)}, u32[]{:S(2)}, u32[]{:S(2)}) collective-permute-start(f32[2,128,512]{2,1,0:T(8,128)S(1)} %get-tuple-element.89), channel_id=1, source_target_pairs={{0,2},{1,3},{2,0},{3,1},{4,6},{5,7},{6,4},{7,5},{8,10},{9,11},{10,... | collective-permute-start | bytes 1572872 | tf_op jit(solution)/shard_map/ppermute | solution.py:334
  60.6 28.2 %collective-permute-start.10 = (f32[2,128,512]{2,1,0:T(8,128)S(1)}, f32[2,128,512]{2,1,0:T(8,128)S(1)}, u32[]{:S(2)}, u32[]{:S(2)}) collective-permute-start(f32[2,128,512]{2,1,0:T(8,128)S(1)} %get-tuple-element.85), channel_id=1, source_target_pairs={{0,8},{8,16},{16,24},{24,0},{1,9},{9,17},{17,25},{25,1},{2,10},{10... | collective-permute-start | bytes 1572872 | tf_op jit(solution)/shard_map/ppermute | solution.py:342
  62.1 26.8 %collective-permute-start.11 = (f32[2,128,512]{2,1,0:T(8,128)S(1)}, f32[2,128,512]{2,1,0:T(8,128)S(1)}, u32[]{:S(2)}, u32[]{:S(2)}) collective-permute-start(f32[2,128,512]{2,1,0:T(8,128)S(1)} %get-tuple-element.86), channel_id=1, source_target_pairs={{8,0},{16,8},{24,16},{0,24},{9,1},{17,9},{25,17},{1,25},{10,2},{18... | collective-permute-start | bytes 1572872 | tf_op jit(solution)/shard_map/ppermute | solution.py:343
  63.5 41.5 %collective-permute-start.9 = (f32[2,128,512]{2,1,0:T(8,128)S(1)}, f32[2,128,512]{2,1,0:T(8,128)S(1)}, u32[]{:S(2)}, u32[]{:S(2)}) collective-permute-start(f32[2,128,512]{2,1,0:T(8,128)S(1)} %get-tuple-element.84), channel_id=1, source_target_pairs={{0,4},{1,5},{2,6},{3,7},{4,0},{5,1},{6,2},{7,3},{8,12},{9,13},{10,... | collective-permute-start | bytes 1572872 | tf_op jit(solution)/shard_map/ppermute | solution.py:334
  88.3 1.9 collective-permute-start.15
  110.0 16.7 %collective-permute-start.21 = (f32[2,128,512]{2,1,0:T(8,128)S(1)}, f32[2,128,512]{2,1,0:T(8,128)S(1)}, u32[]{:S(2)}, u32[]{:S(2)}) collective-permute-start(f32[2,128,512]{2,1,0:T(8,128)S(1)} %get-tuple-element.105), channel_id=1, source_target_pairs={{0,6},{1,7},{2,4},{3,5},{4,2},{5,3},{6,0},{7,1},{8,14},{9,15},{10,... | collective-permute-start | bytes 1572872 | tf_op jit(solution)/shard_map/ppermute | solution.py:334
  111.5 28.8 %collective-permute-start.22 = (f32[2,128,512]{2,1,0:T(8,128)S(1)}, f32[2,128,512]{2,1,0:T(8,128)S(1)}, u32[]{:S(2)}, u32[]{:S(2)}) collective-permute-start(f32[2,128,512]{2,1,0:T(8,128)S(1)} %get-tuple-element.106), channel_id=1, source_target_pairs={{0,2},{1,3},{2,0},{3,1},{4,6},{5,7},{6,4},{7,5},{8,10},{9,11},{10,... | collective-permute-start | bytes 1572872 | tf_op jit(solution)/shard_map/ppermute | solution.py:334
  111.5 29.4 %collective-permute-start.19 = (f32[2,128,512]{2,1,0:T(8,128)S(1)}, f32[2,128,512]{2,1,0:T(8,128)S(1)}, u32[]{:S(2)}, u32[]{:S(2)}) collective-permute-start(f32[2,128,512]{2,1,0:T(8,128)S(1)} %get-tuple-element.102), channel_id=1, source_target_pairs={{0,8},{8,16},{16,24},{24,0},{1,9},{9,17},{17,25},{25,1},{2,10},{10... | collective-permute-start | bytes 1572872 | tf_op jit(solution)/shard_map/ppermute | solution.py:342
  112.9 28.1 %collective-permute-start.20 = (f32[2,128,512]{2,1,0:T(8,128)S(1)}, f32[2,128,512]{2,1,0:T(8,128)S(1)}, u32[]{:S(2)}, u32[]{:S(2)}) collective-permute-start(f32[2,128,512]{2,1,0:T(8,128)S(1)} %get-tuple-element.103), channel_id=1, source_target_pairs={{8,0},{16,8},{24,16},{0,24},{9,1},{17,9},{25,17},{1,25},{10,2},{18... | collective-permute-start | bytes 1572872 | tf_op jit(solution)/shard_map/ppermute | solution.py:343
  114.5 41.4 %collective-permute-start.18 = (f32[2,128,512]{2,1,0:T(8,128)S(1)}, f32[2,128,512]{2,1,0:T(8,128)S(1)}, u32[]{:S(2)}, u32[]{:S(2)}) collective-permute-start(f32[2,128,512]{2,1,0:T(8,128)S(1)} %get-tuple-element.101), channel_id=1, source_target_pairs={{0,4},{1,5},{2,6},{3,7},{4,0},{5,1},{6,2},{7,3},{8,12},{9,13},{10,... | collective-permute-start | bytes 1572872 | tf_op jit(solution)/shard_map/ppermute | solution.py:334
  140.4 1.9 collective-permute-start.24
  159.4 16.7 %collective-permute-start.30 = (f32[2,128,512]{2,1,0:T(8,128)S(1)}, f32[2,128,512]{2,1,0:T(8,128)S(1)}, u32[]{:S(2)}, u32[]{:S(2)}) collective-permute-start(f32[2,128,512]{2,1,0:T(8,128)S(1)} %get-tuple-element.118), channel_id=1, source_target_pairs={{0,6},{1,7},{2,4},{3,5},{4,2},{5,3},{6,0},{7,1},{8,14},{9,15},{10,... | collective-permute-start | bytes 1572872 | tf_op jit(solution)/shard_map/ppermute | solution.py:334
  161.8 27.7 %collective-permute-start.31 = (f32[2,128,512]{2,1,0:T(8,128)S(1)}, f32[2,128,512]{2,1,0:T(8,128)S(1)}, u32[]{:S(2)}, u32[]{:S(2)}) collective-permute-start(f32[2,128,512]{2,1,0:T(8,128)S(1)} %get-tuple-element.119), channel_id=1, source_target_pairs={{0,2},{1,3},{2,0},{3,1},{4,6},{5,7},{6,4},{7,5},{8,10},{9,11},{10,... | collective-permute-start | bytes 1572872 | tf_op jit(solution)/shard_map/ppermute | solution.py:334
  161.8 28.3 %collective-permute-start.28 = (f32[2,128,512]{2,1,0:T(8,128)S(1)}, f32[2,128,512]{2,1,0:T(8,128)S(1)}, u32[]{:S(2)}, u32[]{:S(2)}) collective-permute-start(f32[2,128,512]{2,1,0:T(8,128)S(1)} %get-tuple-element.115), channel_id=1, source_target_pairs={{0,8},{8,16},{16,24},{24,0},{1,9},{9,17},{17,25},{25,1},{2,10},{10... | collective-permute-start | bytes 1572872 | tf_op jit(solution)/shard_map/ppermute | solution.py:342
  163.3 26.9 %collective-permute-start.29 = (f32[2,128,512]{2,1,0:T(8,128)S(1)}, f32[2,128,512]{2,1,0:T(8,128)S(1)}, u32[]{:S(2)}, u32[]{:S(2)}) collective-permute-start(f32[2,128,512]{2,1,0:T(8,128)S(1)} %get-tuple-element.116), channel_id=1, source_target_pairs={{8,0},{16,8},{24,16},{0,24},{9,1},{17,9},{25,17},{1,25},{10,2},{18... | collective-permute-start | bytes 1572872 | tf_op jit(solution)/shard_map/ppermute | solution.py:343
  164.7 41.4 %collective-permute-start.27 = (f32[2,128,512]{2,1,0:T(8,128)S(1)}, f32[2,128,512]{2,1,0:T(8,128)S(1)}, u32[]{:S(2)}, u32[]{:S(2)}) collective-permute-start(f32[2,128,512]{2,1,0:T(8,128)S(1)} %get-tuple-element.114), channel_id=1, source_target_pairs={{0,4},{1,5},{2,6},{3,7},{4,0},{5,1},{6,2},{7,3},{8,12},{9,13},{10,... | collective-permute-start | bytes 1572872 | tf_op jit(solution)/shard_map/ppermute | solution.py:334
  189.6 1.9 collective-permute-start.33
  (20 other events, 117.7 us)

commit v5 on v4

--- a/solution.py
+++ b/solution.py
@@ -354,7 +354,7 @@
         return acc, [(last, cap), (swap(last[cap:], 1), cap)]
 
     current = features.reshape(row_blocks, TILE, width)
-    sends = pick(current, route)
+    sends = pick(current, (plan[:1],) + route[1:]) + pick(current, (plan[1:],) + route[1:])
     parts = weights(skew_raw)
     layers = skew_raw.shape[0]
     for layer in range(layers):

time: 212 us -> 211 us (level)
  waiting for transfers between devices: 100 us -> 96.1 us
  Pallas kernels: 68.8 us -> 71.4 us
    ppermute x28, waiting for transfers between devices: 99 us -> 91.5 us  [swap(): return lax.ppermute(x, 'dev', [(i, i ^ k) for i in range(peers)])]
    ppermute x4, waiting for transfers between devices: 1.05 us -> 4.63 us  [start(): upper = lax.ppermute(sends[len(chips) + 1], 'dom', down)]
    pallas_call x1 -> x2, Pallas kernels: 4.26 us -> 6.51 us  [pick(): pl.pallas_call(functools.partial(pick_kernel, plan), out_shape=[jax.Shape...]
  transfers between devices with their start and end apart: 36 -> 36, of which waited for: 26 -> 24; matrix products, arithmetic and copies ran while one was open for 0% -> 0% of each run, Pallas kernels for 25% -> 27%
where the time goes in v5:
time: 211 us; the launch traced here: 210 us
  waiting for transfers between devices  96.1 us (46%)
  Pallas kernels  71.4 us (34%)
  starting transfers between devices  33.6 us (16%)
  between operations  5.85 us (3%)
  local copies, waits for them, and re-layouts  3.4 us (2%)
    ppermute x28, waiting for transfers between devices, swap(): return lax.ppermute(x, 'dev', [(i, i ^ k) for i in range(peers)])  91.5 us
    pallas_call x8, Pallas kernels, apply_dense(): pl.pallas_call(functools.partial(apply_kernel, len(xs), acc is not None,...  38.6 us
    ppermute x28, starting transfers between devices, swap(): return lax.ppermute(x, 'dev', [(i, i ^ k) for i in range(peers)])  22.2 us
    pallas_call x4, Pallas kernels, finish(): pl.pallas_call(functools.partial(finish_kernel, plan, len(xs), bool(squar...  11.4 us
    pallas_call x2, Pallas kernels, mix(): pl.pallas_call(mix_kernel, grid=(x.shape[0] // STEP,), out_shape=jax.Shap...  7.28 us
    pallas_call x2, Pallas kernels, pick(): pl.pallas_call(functools.partial(pick_kernel, plan), out_shape=[jax.Shape...  6.51 us
    ppermute x4, starting transfers between devices, start(): lower = lax.ppermute(sends[len(chips)], 'dom', up)  5.96 us
    ppermute x4, starting transfers between devices, start(): upper = lax.ppermute(sends[len(chips) + 1], 'dom', down)  5.53 us
  transfers between devices with their start and end apart: 36, of which 24 were waited for; matrix products, arithmetic and copies ran while one was open for 0% of the time, Pallas kernels for 27%

profile of v5, /device:TPU:0, one launch (start us, length us, event | category | flops | bytes accessed | tf_op | source)
XLA Modules:
  0.0 210.4 jit_solution(8675214815833788481)
XLA Ops:
  2.7 5.1 %collective-permute-start.3 = (f32[2,128,512]{2,1,0:T(8,128)}, f32[2,128,512]{2,1,0:T(8,128)S(1)}, u32[]{:S(2)}, u32[]{:S(2)}) collective-permute-start(f32[2,128,512]{2,1,0:T(8,128)} %shard_map.93), channel_id=1, source_target_pairs={{0,6},{1,7},{2,4},{3,5},{4,2},{5,3},{6,0},{7,1},{8,14},{9,15},{10,... | collective-permute-start | bytes 1572872 | tf_op jit(solution)/shard_map/ppermute | solution.py:334
  7.8 3.8 %shard_map.92 = (f32[2,128,512]{2,1,0:T(8,128)}, f32[2,128,512]{2,1,0:T(8,128)}, f32[2,128,512]{2,1,0:T(8,128)}, f32[2,128,512]{2,1,0:T(8,128)}, f32[1,128,512]{2,1,0:T(8,128)}) custom-call(s32[1]{0:T(128)} %bitcast.me_ref, s32[8]{0:T(128)} %bitcast.18, s32[2,2]{1,0:T(2,128)} %bitcast.24, f32[8,128,512]{2,1,0:T(8,128)} %bitcast.14), custom_call_target="tpu_custom_call" | custom-call | flops 1 | bytes 1 | tf_op jit(solution)/shard_map/pallas_call | solution.py:224
  23.9 3.4 %shard_map.91 = (bf16[8,128,1024]{2,1,0:T(8,128)(2,1)S(1)}, bf16[8,128,1024]{2,1,0:T(8,128)(2,1)S(1)}, bf16[8,128,1152]{2,1,0:T(8,128)(2,1)S(1)}, bf16[8,128,115...) custom-call(s32[80]{0:T(128)S(1)} %copy-done.5, ...), custom_call_target="tpu_custom_call" | custom-call | flops 1 | bytes 1 | tf_op jit(solution)/shard_map/pallas_call | solution.py:72
  27.3 4.0 %shard_map.94.refs_7_ = f32[8,128,512]{2,1,0:T(8,128)S(1)} custom-call(bf16[8,128,1024]{2,1,0:T(8,128)(2,1)S(1)} %get-tuple-element.74.ah_ref, bf16[8,128,1024]{2,1,0:T(8,128)(2,1)S(1)} %get-tuple-element.75.al_ref, f32[8,128,512]{2,1,0:T(8,128)S(1)} %bitcast.15), custom_call_target="tpu_custom_call" | custom-call | flops 1 | bytes 1 | tf_op jit(solution)/shard_map/pallas_call | solution.py:158
  33.0 4.6 %collective-permute-done.2.refs_1_ = f32[2,128,512]{2,1,0:T(8,128)S(1)} collective-permute-done((f32[2,128,512]{2,1,0:T(8,128)}, f32[2,128,512]{2,1,0:T(8,128)S(1)}, u32[]{:S(2)}, u32[]{:S(2)}) %collective-permute-start.2) | collective-permute-done | bytes 524320 | tf_op jit(solution)/shard_map/ppermute | solution.py:343
  37.7 4.8 %shard_map.95.acc_ref = f32[8,128,512]{2,1,0:T(8,128)S(1)} custom-call(bf16[8,128,1152]{2,1,0:T(8,128)(2,1)S(1)} %get-tuple-element.68.ah_ref, bf16[8,128,1152]{2,1,0:T(8,128)(2,1)S(1)} %get-tuple-element.69.al_ref, f32[2,128,512]{2,1,0:T(8,128)S(1)} %collective-permute-done.1.refs_0_, f32[2,128,512]{2,1,0:T(8,128)S(1)} %collective-permute-done.2.refs_1_, ...), custom_call_target="tpu_custom_call" | custom-call | flops 1 | bytes 1 | tf_op jit(solution)/shard_map/pallas_call | solution.py:158
  42.5 10.3 %collective-permute-done.refs_0_ = f32[2,128,512]{2,1,0:T(8,128)S(1)} collective-permute-done((f32[2,128,512]{2,1,0:T(8,128)}, f32[2,128,512]{2,1,0:T(8,128)S(1)}, u32[]{:S(2)}, u32[]{:S(2)}) %collective-permute-start) | collective-permute-done | bytes 524320 | tf_op jit(solution)/shard_map/ppermute | solution.py:334
  63.7 4.1 %shard_map.98 = (bf16[2,512,512]{2,1,0:T(8,128)(2,1)S(1)}, bf16[2,512,512]{2,1,0:T(8,128)(2,1)S(1)}, bf16[2,512,512]{2,1,0:T(8,128)(2,1)S(1)}, bf16[2,512,512]{2,1,0:T(8,128)(2,1)S(1)}) custom-call(f32[2,512,512]{2,1,0:T(8,128)S(1)} %copy-done.2), custom_call_target="tpu_custom_call" | custom-call | flops 1 | bytes 1 | tf_op jit(solution)/shard_map/pallas_call | solution.py:96
  67.8 4.0 %shard_map.97.twice_ref = f32[8,128,512]{2,1,0:T(8,128)S(1)} custom-call(bf16[8,128,1024]{2,1,0:T(8,128)(2,1)S(1)} %get-tuple-element.74.ah_ref, bf16[8,128,1024]{2,1,0:T(8,128)(2,1)S(1)} %get-tuple-element.75.al_ref, f32[8,128,512]{2,1,0:T(8,128)S(1)} %get-tuple-element.88.refs_0_.once_ref), custom_call_target="tpu_custom_call" | custom-call | flops 1 | bytes 1 | tf_op jit(solution)/shard_map/pallas_call | solution.py:158
  71.8 3.6 %shard_map.99.refs_7_ = f32[8,128,512]{2,1,0:T(8,128)S(1)} custom-call(f32[8,128,512]{2,1,0:T(8,128)S(1)} %bitcast.16, f32[8,128,512]{2,1,0:T(8,128)S(1)} %get-tuple-element.88.refs_0_.once_ref, f32[8,128,512]{2,1,0:T(8,128)S(1)} %shard_map.97.twice_ref, bf16[2,512,512]{2,1,0:T(8,128)(2,1)S(1)} %get-tuple-element.89.sh_ref, ...), custom_call_target="tpu_custom_call" | custom-call | flops 1 | bytes 1 | tf_op jit(solution)/shard_map/pallas_call | solution.py:180
  75.5 10.7 %collective-permute-done.13.refs_3_ = f32[2,128,512]{2,1,0:T(8,128)S(1)} collective-permute-done((f32[2,128,512]{2,1,0:T(8,128)S(1)}, f32[2,128,512]{2,1,0:T(8,128)S(1)}, u32[]{:S(2)}, u32[]{:S(2)}) %collective-permute-start.13) | collective-permute-done | bytes 524320 | tf_op jit(solution)/shard_map/ppermute | solution.py:334
  88.6 6.5 %shard_map.100.acc_ref = f32[8,128,512]{2,1,0:T(8,128)S(1)} custom-call(bf16[8,128,1152]{2,1,0:T(8,128)(2,1)S(1)} %get-tuple-element.68.ah_ref, bf16[8,128,1152]{2,1,0:T(8,128)(2,1)S(1)} %get-tuple-element.69.al_ref, f32[2,128,512]{2,1,0:T(8,128)S(1)} %collective-permute-done.10.refs_0_, f32[2,128,512]{2,1,0:T(8,128)S(1)} %collective-permute-done.11.refs_1_, ...), custom_call_target="tpu_custom_call" | custom-call | flops 1 | bytes 1 | tf_op jit(solution)/shard_map/pallas_call | solution.py:158
  95.2 8.2 %collective-permute-done.9.refs_0_ = f32[2,128,512]{2,1,0:T(8,128)S(1)} collective-permute-done((f32[2,128,512]{2,1,0:T(8,128)S(1)}, f32[2,128,512]{2,1,0:T(8,128)S(1)}, u32[]{:S(2)}, u32[]{:S(2)}) %collective-permute-start.9) | collective-permute-done | bytes 524320 | tf_op jit(solution)/shard_map/ppermute | solution.py:334
  115.7 4.0 %shard_map.102.refs_7_ = f32[8,128,512]{2,1,0:T(8,128)S(1)} custom-call(bf16[8,128,1024]{2,1,0:T(8,128)(2,1)S(1)} %get-tuple-element.74.ah_ref, bf16[8,128,1024]{2,1,0:T(8,128)(2,1)S(1)} %get-tuple-element.75.al_ref, f32[8,128,512]{2,1,0:T(8,128)S(1)} %get-tuple-element.105.refs_0_.x_ref), custom_call_target="tpu_custom_call" | custom-call | flops 1 | bytes 1 | tf_op jit(solution)/shard_map/pallas_call | solution.py:158
  119.7 5.3 %collective-permute-done.21.refs_2_ = f32[2,128,512]{2,1,0:T(8,128)S(1)} collective-permute-done((f32[2,128,512]{2,1,0:T(8,128)S(1)}, f32[2,128,512]{2,1,0:T(8,128)S(1)}, u32[]{:S(2)}, u32[]{:S(2)}) %collective-permute-start.21) | collective-permute-done | bytes 524320 | tf_op jit(solution)/shard_map/ppermute | solution.py:334
  125.0 13.6 %collective-permute-done.22.refs_3_ = f32[2,128,512]{2,1,0:T(8,128)S(1)} collective-permute-done((f32[2,128,512]{2,1,0:T(8,128)S(1)}, f32[2,128,512]{2,1,0:T(8,128)S(1)}, u32[]{:S(2)}, u32[]{:S(2)}) %collective-permute-start.22) | collective-permute-done | bytes 524320 | tf_op jit(solution)/shard_map/ppermute | solution.py:334
  141.0 4.8 %shard_map.103.acc_ref = f32[8,128,512]{2,1,0:T(8,128)S(1)} custom-call(bf16[8,128,1152]{2,1,0:T(8,128)(2,1)S(1)} %get-tuple-element.68.ah_ref, bf16[8,128,1152]{2,1,0:T(8,128)(2,1)S(1)} %get-tuple-element.69.al_ref, f32[2,128,512]{2,1,0:T(8,128)S(1)} %collective-permute-done.19.refs_0_, f32[2,128,512]{2,1,0:T(8,128)S(1)} %collective-permute-done.20.refs_1_, ...), custom_call_target="tpu_custom_call" | custom-call | flops 1 | bytes 1 | tf_op jit(solution)/shard_map/pallas_call | solution.py:158
  145.8 8.3 %collective-permute-done.18.refs_0_ = f32[2,128,512]{2,1,0:T(8,128)S(1)} collective-permute-done((f32[2,128,512]{2,1,0:T(8,128)S(1)}, f32[2,128,512]{2,1,0:T(8,128)S(1)}, u32[]{:S(2)}, u32[]{:S(2)}) %collective-permute-start.18) | collective-permute-done | bytes 524320 | tf_op jit(solution)/shard_map/ppermute | solution.py:334
  165.0 4.0 %shard_map.105.twice_ref = f32[8,128,512]{2,1,0:T(8,128)S(1)} custom-call(bf16[8,128,1024]{2,1,0:T(8,128)(2,1)S(1)} %get-tuple-element.74.ah_ref, bf16[8,128,1024]{2,1,0:T(8,128)(2,1)S(1)} %get-tuple-element.75.al_ref, f32[8,128,512]{2,1,0:T(8,128)S(1)} %get-tuple-element.118.refs_0_.once_ref), custom_call_target="tpu_custom_call" | custom-call | flops 1 | bytes 1 | tf_op jit(solution)/shard_map/pallas_call | solution.py:158
  168.9 3.6 %shard_map.106.refs_7_ = f32[8,128,512]{2,1,0:T(8,128)S(1)} custom-call(f32[8,128,512]{2,1,0:T(8,128)S(1)} %get-tuple-element.105.refs_0_.x_ref, f32[8,128,512]{2,1,0:T(8,128)S(1)} %get-tuple-element.118.refs_0_.once_ref, f32[8,128,512]{2,1,0:T(8,128)S(1)} %shard_map.105.twice_ref, bf16[2,512,512]{2,1,0:T(8,128)(2,1)S(1)} %get-tuple-element.89.sh_ref, ...), custom_call_target="tpu_custom_call" | custom-call | flops 1 | bytes 1 | tf_op jit(solution)/shard_map/pallas_call | solution.py:180
  174.3 13.3 %collective-permute-done.31.refs_3_ = f32[2,128,512]{2,1,0:T(8,128)S(1)} collective-permute-done((f32[2,128,512]{2,1,0:T(8,128)S(1)}, f32[2,128,512]{2,1,0:T(8,128)S(1)}, u32[]{:S(2)}, u32[]{:S(2)}) %collective-permute-start.31) | collective-permute-done | bytes 524320 | tf_op jit(solution)/shard_map/ppermute | solution.py:334
  190.0 6.5 %shard_map.107.acc_ref = f32[8,128,512]{2,1,0:T(8,128)S(1)} custom-call(bf16[8,128,1152]{2,1,0:T(8,128)(2,1)S(1)} %get-tuple-element.68.ah_ref, bf16[8,128,1152]{2,1,0:T(8,128)(2,1)S(1)} %get-tuple-element.69.al_ref, f32[2,128,512]{2,1,0:T(8,128)S(1)} %collective-permute-done.28.refs_0_, f32[2,128,512]{2,1,0:T(8,128)S(1)} %collective-permute-done.29.refs_1_, ...), custom_call_target="tpu_custom_call" | custom-call | flops 1 | bytes 1 | tf_op jit(solution)/shard_map/pallas_call | solution.py:158
  196.5 7.9 %collective-permute-done.27.refs_0_ = f32[2,128,512]{2,1,0:T(8,128)S(1)} collective-permute-done((f32[2,128,512]{2,1,0:T(8,128)S(1)}, f32[2,128,512]{2,1,0:T(8,128)S(1)}, u32[]{:S(2)}, u32[]{:S(2)}) %collective-permute-start.27) | collective-permute-done | bytes 524320 | tf_op jit(solution)/shard_map/ppermute | solution.py:334
  206.1 4.3 %shard_map.108 = f32[8,128,512]{2,1,0:T(8,128)} custom-call(s32[1]{0:T(128)} %bitcast.me_ref, s32[8]{0:T(128)S(1)} %bitcast.22, s32[2,2]{1,0:T(2,128)S(1)} %bitcast.28, bf16[8,128,256]{2,1,0:T(8,128)(2,1)S(1)} %get-tuple-element.65.ah_ref, bf16[8,128,256]{2,1,0:T(8,128)(2,1)S(1)} %get-tuple-element.66.al_ref, f32[8,128,512]{2,1,0:T(8,128)S(1)} %shard_map.107.acc_ref, ...), custom_call_target="tpu_custom_call" | custom-call | flops 1 | bytes 1 | tf_op jit(solution)/shard_map/pallas_call | solution.py:280
  (96 shorter events, 55.7 us)
Async XLA Ops:
  2.7 28.6 %collective-permute-start.3 = (f32[2,128,512]{2,1,0:T(8,128)}, f32[2,128,512]{2,1,0:T(8,128)S(1)}, u32[]{:S(2)}, u32[]{:S(2)}) collective-permute-start(f32[2,128,512]{2,1,0:T(8,128)} %shard_map.93), channel_id=1, source_target_pairs={{0,6},{1,7},{2,4},{3,5},{4,2},{5,3},{6,0},{7,1},{8,14},{9,15},{10,... | collective-permute-start | bytes 1572872 | tf_op jit(solution)/shard_map/ppermute | solution.py:334
  11.7 20.7 %collective-permute-start.4 = (f32[2,128,512]{2,1,0:T(8,128)}, f32[2,128,512]{2,1,0:T(8,128)S(1)}, u32[]{:S(2)}, u32[]{:S(2)}) collective-permute-start(f32[2,128,512]{2,1,0:T(8,128)} %get-tuple-element.73), channel_id=1, source_target_pairs={{0,2},{1,3},{2,0},{3,1},{4,6},{5,7},{6,4},{7,5},{8,10},{9,11},{10,... | collective-permute-start | bytes 1572872 | tf_op jit(solution)/shard_map/ppermute | solution.py:334
  11.7 21.2 %collective-permute-start.1 = (f32[2,128,512]{2,1,0:T(8,128)}, f32[2,128,512]{2,1,0:T(8,128)S(1)}, u32[]{:S(2)}, u32[]{:S(2)}) collective-permute-start(f32[2,128,512]{2,1,0:T(8,128)} %get-tuple-element.70), channel_id=1, source_target_pairs={{0,8},{8,16},{16,24},{24,0},{1,9},{9,17},{17,25},{25,1},{2,10},{10... | collective-permute-start | bytes 1572872 | tf_op jit(solution)/shard_map/ppermute | solution.py:342
  13.2 39.6 %collective-permute-start = (f32[2,128,512]{2,1,0:T(8,128)}, f32[2,128,512]{2,1,0:T(8,128)S(1)}, u32[]{:S(2)}, u32[]{:S(2)}) collective-permute-start(f32[2,128,512]{2,1,0:T(8,128)} %get-tuple-element.67), channel_id=1, source_target_pairs={{0,4},{1,5},{2,6},{3,7},{4,0},{5,1},{6,2},{7,3},{8,12},{9,13},{10,... | collective-permute-start | bytes 1572872 | tf_op jit(solution)/shard_map/ppermute | solution.py:334
  13.9 23.7 %collective-permute-start.2 = (f32[2,128,512]{2,1,0:T(8,128)}, f32[2,128,512]{2,1,0:T(8,128)S(1)}, u32[]{:S(2)}, u32[]{:S(2)}) collective-permute-start(f32[2,128,512]{2,1,0:T(8,128)} %get-tuple-element.71), channel_id=1, source_target_pairs={{8,0},{16,8},{24,16},{0,24},{9,1},{17,9},{25,17},{1,25},{10,2},{18... | collective-permute-start | bytes 1572872 | tf_op jit(solution)/shard_map/ppermute | solution.py:343
  32.4 5.3 %collective-permute-start.7 = (f32[1,128,512]{2,1,0:T(8,128)S(1)}, f32[1,128,512]{2,1,0:T(8,128)S(1)}, u32[]{:S(2)}, u32[]{:S(2)}) collective-permute-start(f32[1,128,512]{2,1,0:T(8,128)S(1)} %slice.37), channel_id=1, source_target_pairs={{0,1},{1,0},{2,3},{3,2},{4,5},{5,4},{6,7},{7,6},{8,9},{9,8},{10,11... | collective-permute-start | bytes 786440 | tf_op jit(solution)/shard_map/ppermute | solution.py:334
  32.4 5.2 %collective-permute-start.6 = (f32[1,128,512]{2,1,0:T(8,128)S(1)}, f32[1,128,512]{2,1,0:T(8,128)S(1)}, u32[]{:S(2)}, u32[]{:S(2)}) collective-permute-start(f32[1,128,512]{2,1,0:T(8,128)S(1)} %slice.36), channel_id=1, source_target_pairs={{0,1},{1,0},{2,3},{3,2},{4,5},{5,4},{6,7},{7,6},{8,9},{9,8},{10,11... | collective-permute-start | bytes 786440 | tf_op jit(solution)/shard_map/ppermute | solution.py:334
  33.0 4.7 %collective-permute-start.5 = (f32[1,128,512]{2,1,0:T(8,128)S(1)}, f32[1,128,512]{2,1,0:T(8,128)S(1)}, u32[]{:S(2)}, u32[]{:S(2)}) collective-permute-start(f32[1,128,512]{2,1,0:T(8,128)S(1)} %copy-done.7), channel_id=1, source_target_pairs={{0,1},{1,0},{2,3},{3,2},{4,5},{5,4},{6,7},{7,6},{8,9},{9,8},{10,11... | collective-permute-start | bytes 786440 | tf_op jit(solution)/shard_map/ppermute | solution.py:334
  56.3 19.2 %collective-permute-start.12 = (f32[2,128,512]{2,1,0:T(8,128)S(1)}, f32[2,128,512]{2,1,0:T(8,128)S(1)}, u32[]{:S(2)}, u32[]{:S(2)}) collective-permute-start(f32[2,128,512]{2,1,0:T(8,128)S(1)} %get-tuple-element.86), channel_id=1, source_target_pairs={{0,6},{1,7},{2,4},{3,5},{4,2},{5,3},{6,0},{7,1},{8,14},{9,15},{10,... | collective-permute-start | bytes 1572872 | tf_op jit(solution)/shard_map/ppermute | solution.py:334
  58.9 27.4 %collective-permute-start.13 = (f32[2,128,512]{2,1,0:T(8,128)S(1)}, f32[2,128,512]{2,1,0:T(8,128)S(1)}, u32[]{:S(2)}, u32[]{:S(2)}) collective-permute-start(f32[2,128,512]{2,1,0:T(8,128)S(1)} %get-tuple-element.87), channel_id=1, source_target_pairs={{0,2},{1,3},{2,0},{3,1},{4,6},{5,7},{6,4},{7,5},{8,10},{9,11},{10,... | collective-permute-start | bytes 1572872 | tf_op jit(solution)/shard_map/ppermute | solution.py:334
  58.9 28.0 %collective-permute-start.10 = (f32[2,128,512]{2,1,0:T(8,128)S(1)}, f32[2,128,512]{2,1,0:T(8,128)S(1)}, u32[]{:S(2)}, u32[]{:S(2)}) collective-permute-start(f32[2,128,512]{2,1,0:T(8,128)S(1)} %get-tuple-element.83), channel_id=1, source_target_pairs={{0,8},{8,16},{16,24},{24,0},{1,9},{9,17},{17,25},{25,1},{2,10},{10... | collective-permute-start | bytes 1572872 | tf_op jit(solution)/shard_map/ppermute | solution.py:342
  60.4 26.6 %collective-permute-start.11 = (f32[2,128,512]{2,1,0:T(8,128)S(1)}, f32[2,128,512]{2,1,0:T(8,128)S(1)}, u32[]{:S(2)}, u32[]{:S(2)}) collective-permute-start(f32[2,128,512]{2,1,0:T(8,128)S(1)} %get-tuple-element.84), channel_id=1, source_target_pairs={{8,0},{16,8},{24,16},{0,24},{9,1},{17,9},{25,17},{1,25},{10,2},{18... | collective-permute-start | bytes 1572872 | tf_op jit(solution)/shard_map/ppermute | solution.py:343
  61.8 41.5 %collective-permute-start.9 = (f32[2,128,512]{2,1,0:T(8,128)S(1)}, f32[2,128,512]{2,1,0:T(8,128)S(1)}, u32[]{:S(2)}, u32[]{:S(2)}) collective-permute-start(f32[2,128,512]{2,1,0:T(8,128)S(1)} %get-tuple-element.82), channel_id=1, source_target_pairs={{0,4},{1,5},{2,6},{3,7},{4,0},{5,1},{6,2},{7,3},{8,12},{9,13},{10,... | collective-permute-start | bytes 1572872 | tf_op jit(solution)/shard_map/ppermute | solution.py:334
  108.3 16.7 %collective-permute-start.21 = (f32[2,128,512]{2,1,0:T(8,128)S(1)}, f32[2,128,512]{2,1,0:T(8,128)S(1)}, u32[]{:S(2)}, u32[]{:S(2)}) collective-permute-start(f32[2,128,512]{2,1,0:T(8,128)S(1)} %get-tuple-element.103), channel_id=1, source_target_pairs={{0,6},{1,7},{2,4},{3,5},{4,2},{5,3},{6,0},{7,1},{8,14},{9,15},{10,... | collective-permute-start | bytes 1572872 | tf_op jit(solution)/shard_map/ppermute | solution.py:334
  109.7 28.8 %collective-permute-start.22 = (f32[2,128,512]{2,1,0:T(8,128)S(1)}, f32[2,128,512]{2,1,0:T(8,128)S(1)}, u32[]{:S(2)}, u32[]{:S(2)}) collective-permute-start(f32[2,128,512]{2,1,0:T(8,128)S(1)} %get-tuple-element.104), channel_id=1, source_target_pairs={{0,2},{1,3},{2,0},{3,1},{4,6},{5,7},{6,4},{7,5},{8,10},{9,11},{10,... | collective-permute-start | bytes 1572872 | tf_op jit(solution)/shard_map/ppermute | solution.py:334
  109.8 29.5 %collective-permute-start.19 = (f32[2,128,512]{2,1,0:T(8,128)S(1)}, f32[2,128,512]{2,1,0:T(8,128)S(1)}, u32[]{:S(2)}, u32[]{:S(2)}) collective-permute-start(f32[2,128,512]{2,1,0:T(8,128)S(1)} %get-tuple-element.100), channel_id=1, source_target_pairs={{0,8},{8,16},{16,24},{24,0},{1,9},{9,17},{17,25},{25,1},{2,10},{10... | collective-permute-start | bytes 1572872 | tf_op jit(solution)/shard_map/ppermute | solution.py:342
  111.2 28.1 %collective-permute-start.20 = (f32[2,128,512]{2,1,0:T(8,128)S(1)}, f32[2,128,512]{2,1,0:T(8,128)S(1)}, u32[]{:S(2)}, u32[]{:S(2)}) collective-permute-start(f32[2,128,512]{2,1,0:T(8,128)S(1)} %get-tuple-element.101), channel_id=1, source_target_pairs={{8,0},{16,8},{24,16},{0,24},{9,1},{17,9},{25,17},{1,25},{10,2},{18... | collective-permute-start | bytes 1572872 | tf_op jit(solution)/shard_map/ppermute | solution.py:343
  112.7 41.4 %collective-permute-start.18 = (f32[2,128,512]{2,1,0:T(8,128)S(1)}, f32[2,128,512]{2,1,0:T(8,128)S(1)}, u32[]{:S(2)}, u32[]{:S(2)}) collective-permute-start(f32[2,128,512]{2,1,0:T(8,128)S(1)} %get-tuple-element.99), channel_id=1, source_target_pairs={{0,4},{1,5},{2,6},{3,7},{4,0},{5,1},{6,2},{7,3},{8,12},{9,13},{10,... | collective-permute-start | bytes 1572872 | tf_op jit(solution)/shard_map/ppermute | solution.py:334
  138.7 1.9 collective-permute-start.24
  157.6 16.7 %collective-permute-start.30 = (f32[2,128,512]{2,1,0:T(8,128)S(1)}, f32[2,128,512]{2,1,0:T(8,128)S(1)}, u32[]{:S(2)}, u32[]{:S(2)}) collective-permute-start(f32[2,128,512]{2,1,0:T(8,128)S(1)} %get-tuple-element.116), channel_id=1, source_target_pairs={{0,6},{1,7},{2,4},{3,5},{4,2},{5,3},{6,0},{7,1},{8,14},{9,15},{10,... | collective-permute-start | bytes 1572872 | tf_op jit(solution)/shard_map/ppermute | solution.py:334
  160.1 27.5 %collective-permute-start.31 = (f32[2,128,512]{2,1,0:T(8,128)S(1)}, f32[2,128,512]{2,1,0:T(8,128)S(1)}, u32[]{:S(2)}, u32[]{:S(2)}) collective-permute-start(f32[2,128,512]{2,1,0:T(8,128)S(1)} %get-tuple-element.117), channel_id=1, source_target_pairs={{0,2},{1,3},{2,0},{3,1},{4,6},{5,7},{6,4},{7,5},{8,10},{9,11},{10,... | collective-permute-start | bytes 1572872 | tf_op jit(solution)/shard_map/ppermute | solution.py:334
  160.1 28.1 %collective-permute-start.28 = (f32[2,128,512]{2,1,0:T(8,128)S(1)}, f32[2,128,512]{2,1,0:T(8,128)S(1)}, u32[]{:S(2)}, u32[]{:S(2)}) collective-permute-start(f32[2,128,512]{2,1,0:T(8,128)S(1)} %get-tuple-element.113), channel_id=1, source_target_pairs={{0,8},{8,16},{16,24},{24,0},{1,9},{9,17},{17,25},{25,1},{2,10},{10... | collective-permute-start | bytes 1572872 | tf_op jit(solution)/shard_map/ppermute | solution.py:342
  161.6 26.7 %collective-permute-start.29 = (f32[2,128,512]{2,1,0:T(8,128)S(1)}, f32[2,128,512]{2,1,0:T(8,128)S(1)}, u32[]{:S(2)}, u32[]{:S(2)}) collective-permute-start(f32[2,128,512]{2,1,0:T(8,128)S(1)} %get-tuple-element.114), channel_id=1, source_target_pairs={{8,0},{16,8},{24,16},{0,24},{9,1},{17,9},{25,17},{1,25},{10,2},{18... | collective-permute-start | bytes 1572872 | tf_op jit(solution)/shard_map/ppermute | solution.py:343
  163.1 41.4 %collective-permute-start.27 = (f32[2,128,512]{2,1,0:T(8,128)S(1)}, f32[2,128,512]{2,1,0:T(8,128)S(1)}, u32[]{:S(2)}, u32[]{:S(2)}) collective-permute-start(f32[2,128,512]{2,1,0:T(8,128)S(1)} %get-tuple-element.112), channel_id=1, source_target_pairs={{0,4},{1,5},{2,6},{3,7},{4,0},{5,1},{6,2},{7,3},{8,12},{9,13},{10,... | collective-permute-start | bytes 1572872 | tf_op jit(solution)/shard_map/ppermute | solution.py:334
  (20 other events, 117.4 us)

commit v6 on v5

--- a/solution.py
+++ b/solution.py
@@ -218,16 +218,16 @@
     copy_out(plan, me_ref, near_ref, far_ref, x_ref, refs[:-1], refs[-1])
 
 
-def pick(x, route):
+def pick(x, route, space, limit):
     plan, me, near, far = route
     sizes = plan_sizes(plan)
     return pl.pallas_call(
         functools.partial(pick_kernel, plan),
         out_shape=[jax.ShapeDtypeStruct((n,) + x.shape[1:], x.dtype) for n in sizes],
-        in_specs=[smem()] * 3 + [pl.BlockSpec(memory_space=pl.ANY)],
-        out_specs=[pl.BlockSpec(memory_space=pltpu.VMEM)] * len(sizes),
+        in_specs=[smem()] * 3 + [pl.BlockSpec(memory_space=space)],
+        out_specs=[pl.BlockSpec(memory_space=pltpu.VMEM if space == pl.ANY else pl.ANY)] * len(sizes),
         scratch_shapes=[pltpu.SemaphoreType.DMA((sum(sizes),))],
-        compiler_params=pltpu.CompilerParams(vmem_limit_bytes=56 * MIB),
+        compiler_params=pltpu.CompilerParams(vmem_limit_bytes=limit * MIB),
         cost_estimate=SMALL,
     )(me, near, far, x)
 
@@ -354,7 +354,8 @@
         return acc, [(last, cap), (swap(last[cap:], 1), cap)]
 
     current = features.reshape(row_blocks, TILE, width)
-    sends = pick(current, (plan[:1],) + route[1:]) + pick(current, (plan[1:],) + route[1:])
+    sends = pick(current, (plan[:1],) + route[1:], pl.ANY, 56)
+    sends += pick(current, (plan[1:],) + route[1:], pltpu.VMEM, 16)
     parts = weights(skew_raw)
     layers = skew_raw.shape[0]
     for layer in range(layers):

time: 211 us -> 211 us (level)
    ppermute x4, waiting for transfers between devices: 4.63 us -> 1.75 us  [start(): upper = lax.ppermute(sends[len(chips) + 1], 'dom', down)]
    ppermute x28, waiting for transfers between devices: 91.5 us -> 94 us  [swap(): return lax.ppermute(x, 'dev', [(i, i ^ k) for i in range(peers)])]
  transfers between devices with their start and end apart: 36 -> 36, of which waited for: 24 -> 24; matrix products, arithmetic and copies ran while one was open for 0% -> 1% of each run, Pallas kernels for 27% -> 27%
where the time goes in v6:
time: 211 us; the launch traced here: 210 us
  waiting for transfers between devices  95.8 us (45%)
  Pallas kernels  70.3 us (33%)
  starting transfers between devices  33.7 us (16%)
  between operations  6.11 us (3%)
  local copies, waits for them, and re-layouts  4.36 us (2%)
    ppermute x28, waiting for transfers between devices, swap(): return lax.ppermute(x, 'dev', [(i, i ^ k) for i in range(peers)])  94 us
    pallas_call x8, Pallas kernels, apply_dense(): pl.pallas_call(functools.partial(apply_kernel, len(xs), acc is not None,...  39.5 us
    ppermute x28, starting transfers between devices, swap(): return lax.ppermute(x, 'dev', [(i, i ^ k) for i in range(peers)])  22.2 us
    pallas_call x4, Pallas kernels, finish(): pl.pallas_call(functools.partial(finish_kernel, plan, len(xs), bool(squar...  11.4 us
    pallas_call x2, Pallas kernels, mix(): pl.pallas_call(mix_kernel, grid=(x.shape[0] // STEP,), out_shape=jax.Shap...  7.22 us
    ppermute x4, starting transfers between devices, start(): lower = lax.ppermute(sends[len(chips)], 'dom', up)  6.03 us
    ppermute x4, starting transfers between devices, start(): upper = lax.ppermute(sends[len(chips) + 1], 'dom', down)  5.54 us
    pallas_call x2, Pallas kernels, pick(): pl.pallas_call(functools.partial(pick_kernel, plan), out_shape=[jax.Shape...  4.64 us
  transfers between devices with their start and end apart: 36, of which 24 were waited for; matrix products, arithmetic and copies ran while one was open for 1% of the time, Pallas kernels for 27%

profile of v6, /device:TPU:0, one launch (start us, length us, event | category | flops | bytes accessed | tf_op | source)
XLA Modules:
  0.0 210.3 jit_solution(12368928638343263074)
XLA Ops:
  2.7 5.1 %collective-permute-start.3 = (f32[2,128,512]{2,1,0:T(8,128)}, f32[2,128,512]{2,1,0:T(8,128)S(1)}, u32[]{:S(2)}, u32[]{:S(2)}) collective-permute-start(f32[2,128,512]{2,1,0:T(8,128)} %shard_map.93), channel_id=1, source_target_pairs={{0,6},{1,7},{2,4},{3,5},{4,2},{5,3},{6,0},{7,1},{8,14},{9,15},{10,... | collective-permute-start | bytes 1572872 | tf_op jit(solution)/shard_map/ppermute | solution.py:334
  22.4 3.4 %shard_map.91 = (bf16[8,128,1024]{2,1,0:T(8,128)(2,1)S(1)}, bf16[8,128,1024]{2,1,0:T(8,128)(2,1)S(1)}, bf16[8,128,1152]{2,1,0:T(8,128)(2,1)S(1)}, bf16[8,128,115...) custom-call(s32[80]{0:T(128)S(1)} %copy-done.5, ...), custom_call_target="tpu_custom_call" | custom-call | flops 1 | bytes 1 | tf_op jit(solution)/shard_map/pallas_call | solution.py:72
  25.8 3.9 %shard_map.94.refs_7_ = f32[8,128,512]{2,1,0:T(8,128)S(1)} custom-call(bf16[8,128,1024]{2,1,0:T(8,128)(2,1)S(1)} %get-tuple-element.74.ah_ref, bf16[8,128,1024]{2,1,0:T(8,128)(2,1)S(1)} %get-tuple-element.75.al_ref, f32[8,128,512]{2,1,0:T(8,128)S(1)} %bitcast.15), custom_call_target="tpu_custom_call" | custom-call | flops 1 | bytes 1 | tf_op jit(solution)/shard_map/pallas_call | solution.py:158
  35.8 6.1 %shard_map.95.acc_ref = f32[8,128,512]{2,1,0:T(8,128)S(1)} custom-call(bf16[8,128,1152]{2,1,0:T(8,128)(2,1)S(1)} %get-tuple-element.68.ah_ref, bf16[8,128,1152]{2,1,0:T(8,128)(2,1)S(1)} %get-tuple-element.69.al_ref, f32[2,128,512]{2,1,0:T(8,128)} %collective-permute-done.1.refs_0_, f32[2,128,512]{2,1,0:T(8,128)} %collective-permute-done.2.refs_1_, ...), custom_call_target="tpu_custom_call" | custom-call | flops 1 | bytes 1 | tf_op jit(solution)/shard_map/pallas_call | solution.py:158
  41.9 10.9 %collective-permute-done.refs_0_ = f32[2,128,512]{2,1,0:T(8,128)S(1)} collective-permute-done((f32[2,128,512]{2,1,0:T(8,128)}, f32[2,128,512]{2,1,0:T(8,128)S(1)}, u32[]{:S(2)}, u32[]{:S(2)}) %collective-permute-start) | collective-permute-done | bytes 524320 | tf_op jit(solution)/shard_map/ppermute | solution.py:334
  63.7 4.1 %shard_map.98 = (bf16[2,512,512]{2,1,0:T(8,128)(2,1)S(1)}, bf16[2,512,512]{2,1,0:T(8,128)(2,1)S(1)}, bf16[2,512,512]{2,1,0:T(8,128)(2,1)S(1)}, bf16[2,512,512]{2,1,0:T(8,128)(2,1)S(1)}) custom-call(f32[2,512,512]{2,1,0:T(8,128)S(1)} %copy-done.2), custom_call_target="tpu_custom_call" | custom-call | flops 1 | bytes 1 | tf_op jit(solution)/shard_map/pallas_call | solution.py:96
  67.8 3.9 %shard_map.97.twice_ref = f32[8,128,512]{2,1,0:T(8,128)S(1)} custom-call(bf16[8,128,1024]{2,1,0:T(8,128)(2,1)S(1)} %get-tuple-element.74.ah_ref, bf16[8,128,1024]{2,1,0:T(8,128)(2,1)S(1)} %get-tuple-element.75.al_ref, f32[8,128,512]{2,1,0:T(8,128)S(1)} %get-tuple-element.88.refs_0_.once_ref), custom_call_target="tpu_custom_call" | custom-call | flops 1 | bytes 1 | tf_op jit(solution)/shard_map/pallas_call | solution.py:158
  71.8 3.6 %shard_map.99.refs_7_ = f32[8,128,512]{2,1,0:T(8,128)S(1)} custom-call(f32[8,128,512]{2,1,0:T(8,128)S(1)} %bitcast.16, f32[8,128,512]{2,1,0:T(8,128)S(1)} %get-tuple-element.88.refs_0_.once_ref, f32[8,128,512]{2,1,0:T(8,128)S(1)} %shard_map.97.twice_ref, bf16[2,512,512]{2,1,0:T(8,128)(2,1)S(1)} %get-tuple-element.89.sh_ref, ...), custom_call_target="tpu_custom_call" | custom-call | flops 1 | bytes 1 | tf_op jit(solution)/shard_map/pallas_call | solution.py:180
  75.4 10.8 %collective-permute-done.13.refs_3_ = f32[2,128,512]{2,1,0:T(8,128)S(1)} collective-permute-done((f32[2,128,512]{2,1,0:T(8,128)S(1)}, f32[2,128,512]{2,1,0:T(8,128)S(1)}, u32[]{:S(2)}, u32[]{:S(2)}) %collective-permute-start.13) | collective-permute-done | bytes 524320 | tf_op jit(solution)/shard_map/ppermute | solution.py:334
  88.6 6.5 %shard_map.100.acc_ref = f32[8,128,512]{2,1,0:T(8,128)S(1)} custom-call(bf16[8,128,1152]{2,1,0:T(8,128)(2,1)S(1)} %get-tuple-element.68.ah_ref, bf16[8,128,1152]{2,1,0:T(8,128)(2,1)S(1)} %get-tuple-element.69.al_ref, f32[2,128,512]{2,1,0:T(8,128)S(1)} %collective-permute-done.10.refs_0_, f32[2,128,512]{2,1,0:T(8,128)S(1)} %collective-permute-done.11.refs_1_, ...), custom_call_target="tpu_custom_call" | custom-call | flops 1 | bytes 1 | tf_op jit(solution)/shard_map/pallas_call | solution.py:158
  95.1 8.2 %collective-permute-done.9.refs_0_ = f32[2,128,512]{2,1,0:T(8,128)S(1)} collective-permute-done((f32[2,128,512]{2,1,0:T(8,128)S(1)}, f32[2,128,512]{2,1,0:T(8,128)S(1)}, u32[]{:S(2)}, u32[]{:S(2)}) %collective-permute-start.9) | collective-permute-done | bytes 524320 | tf_op jit(solution)/shard_map/ppermute | solution.py:334
  104.9 3.4 %shard_map.101 = (f32[8,128,512]{2,1,0:T(8,128)S(1)}, f32[2,128,512]{2,1,0:T(8,128)S(1)}, f32[2,128,512]{2,1,0:T(8,128)S(1)}, f32[2,128,512]{2,1,0:T(8,128)S(1)}...) custom-call(s32[1]{0:T(128)} %bitcast.me_ref, s32[8]{0:T(128)S(1)} %bitcast.20, ...), custom_call_target="tpu_custom_call" | custom-call | flops 1 | bytes 1 | tf_op jit(solution)/shard_map/pallas_call | solution.py:280
  112.7 3.0 %collective-permute-start.18 = (f32[2,128,512]{2,1,0:T(8,128)S(1)}, f32[2,128,512]{2,1,0:T(8,128)S(1)}, u32[]{:S(2)}, u32[]{:S(2)}) collective-permute-start(f32[2,128,512]{2,1,0:T(8,128)S(1)} %get-tuple-element.99), channel_id=1, source_target_pairs={{0,4},{1,5},{2,6},{3,7},{4,0},{5,1},{6,2},{7,3},{8,12},{9,13},{10,... | collective-permute-start | bytes 1572872 | tf_op jit(solution)/shard_map/ppermute | solution.py:334
  115.7 3.9 %shard_map.102.refs_7_ = f32[8,128,512]{2,1,0:T(8,128)S(1)} custom-call(bf16[8,128,1024]{2,1,0:T(8,128)(2,1)S(1)} %get-tuple-element.74.ah_ref, bf16[8,128,1024]{2,1,0:T(8,128)(2,1)S(1)} %get-tuple-element.75.al_ref, f32[8,128,512]{2,1,0:T(8,128)S(1)} %get-tuple-element.105.refs_0_.x_ref), custom_call_target="tpu_custom_call" | custom-call | flops 1 | bytes 1 | tf_op jit(solution)/shard_map/pallas_call | solution.py:158
  119.6 5.4 %collective-permute-done.21.refs_2_ = f32[2,128,512]{2,1,0:T(8,128)S(1)} collective-permute-done((f32[2,128,512]{2,1,0:T(8,128)S(1)}, f32[2,128,512]{2,1,0:T(8,128)S(1)}, u32[]{:S(2)}, u32[]{:S(2)}) %collective-permute-start.21) | collective-permute-done | bytes 524320 | tf_op jit(solution)/shard_map/ppermute | solution.py:334
  125.0 13.6 %collective-permute-done.22.refs_3_ = f32[2,128,512]{2,1,0:T(8,128)S(1)} collective-permute-done((f32[2,128,512]{2,1,0:T(8,128)S(1)}, f32[2,128,512]{2,1,0:T(8,128)S(1)}, u32[]{:S(2)}, u32[]{:S(2)}) %collective-permute-start.22) | collective-permute-done | bytes 524320 | tf_op jit(solution)/shard_map/ppermute | solution.py:334
  141.0 4.8 %shard_map.103.acc_ref = f32[8,128,512]{2,1,0:T(8,128)S(1)} custom-call(bf16[8,128,1152]{2,1,0:T(8,128)(2,1)S(1)} %get-tuple-element.68.ah_ref, bf16[8,128,1152]{2,1,0:T(8,128)(2,1)S(1)} %get-tuple-element.69.al_ref, f32[2,128,512]{2,1,0:T(8,128)S(1)} %collective-permute-done.19.refs_0_, f32[2,128,512]{2,1,0:T(8,128)S(1)} %collective-permute-done.20.refs_1_, ...), custom_call_target="tpu_custom_call" | custom-call | flops 1 | bytes 1 | tf_op jit(solution)/shard_map/pallas_call | solution.py:158
  145.8 8.3 %collective-permute-done.18.refs_0_ = f32[2,128,512]{2,1,0:T(8,128)S(1)} collective-permute-done((f32[2,128,512]{2,1,0:T(8,128)S(1)}, f32[2,128,512]{2,1,0:T(8,128)S(1)}, u32[]{:S(2)}, u32[]{:S(2)}) %collective-permute-start.18) | collective-permute-done | bytes 524320 | tf_op jit(solution)/shard_map/ppermute | solution.py:334
  165.0 3.9 %shard_map.105.twice_ref = f32[8,128,512]{2,1,0:T(8,128)S(1)} custom-call(bf16[8,128,1024]{2,1,0:T(8,128)(2,1)S(1)} %get-tuple-element.74.ah_ref, bf16[8,128,1024]{2,1,0:T(8,128)(2,1)S(1)} %get-tuple-element.75.al_ref, f32[8,128,512]{2,1,0:T(8,128)S(1)} %get-tuple-element.118.refs_0_.once_ref), custom_call_target="tpu_custom_call" | custom-call | flops 1 | bytes 1 | tf_op jit(solution)/shard_map/pallas_call | solution.py:158
  168.9 3.6 %shard_map.106.refs_7_ = f32[8,128,512]{2,1,0:T(8,128)S(1)} custom-call(f32[8,128,512]{2,1,0:T(8,128)S(1)} %get-tuple-element.105.refs_0_.x_ref, f32[8,128,512]{2,1,0:T(8,128)S(1)} %get-tuple-element.118.refs_0_.once_ref, f32[8,128,512]{2,1,0:T(8,128)S(1)} %shard_map.105.twice_ref, bf16[2,512,512]{2,1,0:T(8,128)(2,1)S(1)} %get-tuple-element.89.sh_ref, ...), custom_call_target="tpu_custom_call" | custom-call | flops 1 | bytes 1 | tf_op jit(solution)/shard_map/pallas_call | solution.py:180
  174.3 13.3 %collective-permute-done.31.refs_3_ = f32[2,128,512]{2,1,0:T(8,128)S(1)} collective-permute-done((f32[2,128,512]{2,1,0:T(8,128)S(1)}, f32[2,128,512]{2,1,0:T(8,128)S(1)}, u32[]{:S(2)}, u32[]{:S(2)}) %collective-permute-start.31) | collective-permute-done | bytes 524320 | tf_op jit(solution)/shard_map/ppermute | solution.py:334
  190.0 6.5 %shard_map.107.acc_ref = f32[8,128,512]{2,1,0:T(8,128)S(1)} custom-call(bf16[8,128,1152]{2,1,0:T(8,128)(2,1)S(1)} %get-tuple-element.68.ah_ref, bf16[8,128,1152]{2,1,0:T(8,128)(2,1)S(1)} %get-tuple-element.69.al_ref, f32[2,128,512]{2,1,0:T(8,128)S(1)} %collective-permute-done.28.refs_0_, f32[2,128,512]{2,1,0:T(8,128)S(1)} %collective-permute-done.29.refs_1_, ...), custom_call_target="tpu_custom_call" | custom-call | flops 1 | bytes 1 | tf_op jit(solution)/shard_map/pallas_call | solution.py:158
  196.5 7.9 %collective-permute-done.27.refs_0_ = f32[2,128,512]{2,1,0:T(8,128)S(1)} collective-permute-done((f32[2,128,512]{2,1,0:T(8,128)S(1)}, f32[2,128,512]{2,1,0:T(8,128)S(1)}, u32[]{:S(2)}, u32[]{:S(2)}) %collective-permute-start.27) | collective-permute-done | bytes 524320 | tf_op jit(solution)/shard_map/ppermute | solution.py:334
  206.1 4.3 %shard_map.108 = f32[8,128,512]{2,1,0:T(8,128)} custom-call(s32[1]{0:T(128)} %bitcast.me_ref, s32[8]{0:T(128)S(1)} %bitcast.22, s32[2,2]{1,0:T(2,128)S(1)} %bitcast.28, bf16[8,128,256]{2,1,0:T(8,128)(2,1)S(1)} %get-tuple-element.65.ah_ref, bf16[8,128,256]{2,1,0:T(8,128)(2,1)S(1)} %get-tuple-element.66.al_ref, f32[8,128,512]{2,1,0:T(8,128)S(1)} %shard_map.107.acc_ref, ...), custom_call_target="tpu_custom_call" | custom-call | flops 1 | bytes 1 | tf_op jit(solution)/shard_map/pallas_call | solution.py:280
  (94 shorter events, 55.7 us)
Async XLA Ops:
  2.7 27.1 %collective-permute-start.3 = (f32[2,128,512]{2,1,0:T(8,128)}, f32[2,128,512]{2,1,0:T(8,128)S(1)}, u32[]{:S(2)}, u32[]{:S(2)}) collective-permute-start(f32[2,128,512]{2,1,0:T(8,128)} %shard_map.93), channel_id=1, source_target_pairs={{0,6},{1,7},{2,4},{3,5},{4,2},{5,3},{6,0},{7,1},{8,14},{9,15},{10,... | collective-permute-start | bytes 1572872 | tf_op jit(solution)/shard_map/ppermute | solution.py:334
  9.8 22.6 %collective-permute-start.4 = (f32[2,128,512]{2,1,0:T(8,128)}, f32[2,128,512]{2,1,0:T(8,128)}, u32[]{:S(2)}, u32[]{:S(2)}) collective-permute-start(f32[2,128,512]{2,1,0:T(8,128)} %get-tuple-element.73), channel_id=1, source_target_pairs={{0,2},{1,3},{2,0},{3,1},{4,6},{5,7},{6,4},{7,5},{8,10},{9,11},{10,... | collective-permute-start | bytes 1572872 | tf_op jit(solution)/shard_map/ppermute | solution.py:334
  9.9 24.1 %collective-permute-start.1 = (f32[2,128,512]{2,1,0:T(8,128)}, f32[2,128,512]{2,1,0:T(8,128)}, u32[]{:S(2)}, u32[]{:S(2)}) collective-permute-start(f32[2,128,512]{2,1,0:T(8,128)} %get-tuple-element.70), channel_id=1, source_target_pairs={{0,8},{8,16},{16,24},{24,0},{1,9},{9,17},{17,25},{25,1},{2,10},{10... | collective-permute-start | bytes 1572872 | tf_op jit(solution)/shard_map/ppermute | solution.py:342
  11.4 41.4 %collective-permute-start = (f32[2,128,512]{2,1,0:T(8,128)}, f32[2,128,512]{2,1,0:T(8,128)S(1)}, u32[]{:S(2)}, u32[]{:S(2)}) collective-permute-start(f32[2,128,512]{2,1,0:T(8,128)} %get-tuple-element.67), channel_id=1, source_target_pairs={{0,4},{1,5},{2,6},{3,7},{4,0},{5,1},{6,2},{7,3},{8,12},{9,13},{10,... | collective-permute-start | bytes 1572872 | tf_op jit(solution)/shard_map/ppermute | solution.py:334
  12.2 23.7 %collective-permute-start.2 = (f32[2,128,512]{2,1,0:T(8,128)}, f32[2,128,512]{2,1,0:T(8,128)}, u32[]{:S(2)}, u32[]{:S(2)}) collective-permute-start(f32[2,128,512]{2,1,0:T(8,128)} %get-tuple-element.71), channel_id=1, source_target_pairs={{8,0},{16,8},{24,16},{0,24},{9,1},{17,9},{25,17},{1,25},{10,2},{18... | collective-permute-start | bytes 1572872 | tf_op jit(solution)/shard_map/ppermute | solution.py:343
  33.4 2.4 %collective-permute-start.7 = (f32[1,128,512]{2,1,0:T(8,128)S(1)}, f32[1,128,512]{2,1,0:T(8,128)S(1)}, u32[]{:S(2)}, u32[]{:S(2)}) collective-permute-start(f32[1,128,512]{2,1,0:T(8,128)S(1)} %slice.37), channel_id=1, source_target_pairs={{0,1},{1,0},{2,3},{3,2},{4,5},{5,4},{6,7},{7,6},{8,9},{9,8},{10,11... | collective-permute-start | bytes 786440 | tf_op jit(solution)/shard_map/ppermute | solution.py:334
  33.5 2.3 %collective-permute-start.6 = (f32[1,128,512]{2,1,0:T(8,128)S(1)}, f32[1,128,512]{2,1,0:T(8,128)S(1)}, u32[]{:S(2)}, u32[]{:S(2)}) collective-permute-start(f32[1,128,512]{2,1,0:T(8,128)S(1)} %slice.36), channel_id=1, source_target_pairs={{0,1},{1,0},{2,3},{3,2},{4,5},{5,4},{6,7},{7,6},{8,9},{9,8},{10,11... | collective-permute-start | bytes 786440 | tf_op jit(solution)/shard_map/ppermute | solution.py:334
  56.3 19.1 %collective-permute-start.12 = (f32[2,128,512]{2,1,0:T(8,128)S(1)}, f32[2,128,512]{2,1,0:T(8,128)S(1)}, u32[]{:S(2)}, u32[]{:S(2)}) collective-permute-start(f32[2,128,512]{2,1,0:T(8,128)S(1)} %get-tuple-element.86), channel_id=1, source_target_pairs={{0,6},{1,7},{2,4},{3,5},{4,2},{5,3},{6,0},{7,1},{8,14},{9,15},{10,... | collective-permute-start | bytes 1572872 | tf_op jit(solution)/shard_map/ppermute | solution.py:334
  58.9 27.4 %collective-permute-start.13 = (f32[2,128,512]{2,1,0:T(8,128)S(1)}, f32[2,128,512]{2,1,0:T(8,128)S(1)}, u32[]{:S(2)}, u32[]{:S(2)}) collective-permute-start(f32[2,128,512]{2,1,0:T(8,128)S(1)} %get-tuple-element.87), channel_id=1, source_target_pairs={{0,2},{1,3},{2,0},{3,1},{4,6},{5,7},{6,4},{7,5},{8,10},{9,11},{10,... | collective-permute-start | bytes 1572872 | tf_op jit(solution)/shard_map/ppermute | solution.py:334
  58.9 28.0 %collective-permute-start.10 = (f32[2,128,512]{2,1,0:T(8,128)S(1)}, f32[2,128,512]{2,1,0:T(8,128)S(1)}, u32[]{:S(2)}, u32[]{:S(2)}) collective-permute-start(f32[2,128,512]{2,1,0:T(8,128)S(1)} %get-tuple-element.83), channel_id=1, source_target_pairs={{0,8},{8,16},{16,24},{24,0},{1,9},{9,17},{17,25},{25,1},{2,10},{10... | collective-permute-start | bytes 1572872 | tf_op jit(solution)/shard_map/ppermute | solution.py:342
  60.4 26.6 %collective-permute-start.11 = (f32[2,128,512]{2,1,0:T(8,128)S(1)}, f32[2,128,512]{2,1,0:T(8,128)S(1)}, u32[]{:S(2)}, u32[]{:S(2)}) collective-permute-start(f32[2,128,512]{2,1,0:T(8,128)S(1)} %get-tuple-element.84), channel_id=1, source_target_pairs={{8,0},{16,8},{24,16},{0,24},{9,1},{17,9},{25,17},{1,25},{10,2},{18... | collective-permute-start | bytes 1572872 | tf_op jit(solution)/shard_map/ppermute | solution.py:343
  61.8 41.5 %collective-permute-start.9 = (f32[2,128,512]{2,1,0:T(8,128)S(1)}, f32[2,128,512]{2,1,0:T(8,128)S(1)}, u32[]{:S(2)}, u32[]{:S(2)}) collective-permute-start(f32[2,128,512]{2,1,0:T(8,128)S(1)} %get-tuple-element.82), channel_id=1, source_target_pairs={{0,4},{1,5},{2,6},{3,7},{4,0},{5,1},{6,2},{7,3},{8,12},{9,13},{10,... | collective-permute-start | bytes 1572872 | tf_op jit(solution)/shard_map/ppermute | solution.py:334
  86.4 1.9 collective-permute-start.15
  108.3 16.7 %collective-permute-start.21 = (f32[2,128,512]{2,1,0:T(8,128)S(1)}, f32[2,128,512]{2,1,0:T(8,128)S(1)}, u32[]{:S(2)}, u32[]{:S(2)}) collective-permute-start(f32[2,128,512]{2,1,0:T(8,128)S(1)} %get-tuple-element.103), channel_id=1, source_target_pairs={{0,6},{1,7},{2,4},{3,5},{4,2},{5,3},{6,0},{7,1},{8,14},{9,15},{10,... | collective-permute-start | bytes 1572872 | tf_op jit(solution)/shard_map/ppermute | solution.py:334
  109.7 28.9 %collective-permute-start.22 = (f32[2,128,512]{2,1,0:T(8,128)S(1)}, f32[2,128,512]{2,1,0:T(8,128)S(1)}, u32[]{:S(2)}, u32[]{:S(2)}) collective-permute-start(f32[2,128,512]{2,1,0:T(8,128)S(1)} %get-tuple-element.104), channel_id=1, source_target_pairs={{0,2},{1,3},{2,0},{3,1},{4,6},{5,7},{6,4},{7,5},{8,10},{9,11},{10,... | collective-permute-start | bytes 1572872 | tf_op jit(solution)/shard_map/ppermute | solution.py:334
  109.7 29.5 %collective-permute-start.19 = (f32[2,128,512]{2,1,0:T(8,128)S(1)}, f32[2,128,512]{2,1,0:T(8,128)S(1)}, u32[]{:S(2)}, u32[]{:S(2)}) collective-permute-start(f32[2,128,512]{2,1,0:T(8,128)S(1)} %get-tuple-element.100), channel_id=1, source_target_pairs={{0,8},{8,16},{16,24},{24,0},{1,9},{9,17},{17,25},{25,1},{2,10},{10... | collective-permute-start | bytes 1572872 | tf_op jit(solution)/shard_map/ppermute | solution.py:342
  111.2 28.1 %collective-permute-start.20 = (f32[2,128,512]{2,1,0:T(8,128)S(1)}, f32[2,128,512]{2,1,0:T(8,128)S(1)}, u32[]{:S(2)}, u32[]{:S(2)}) collective-permute-start(f32[2,128,512]{2,1,0:T(8,128)S(1)} %get-tuple-element.101), channel_id=1, source_target_pairs={{8,0},{16,8},{24,16},{0,24},{9,1},{17,9},{25,17},{1,25},{10,2},{18... | collective-permute-start | bytes 1572872 | tf_op jit(solution)/shard_map/ppermute | solution.py:343
  112.7 41.4 %collective-permute-start.18 = (f32[2,128,512]{2,1,0:T(8,128)S(1)}, f32[2,128,512]{2,1,0:T(8,128)S(1)}, u32[]{:S(2)}, u32[]{:S(2)}) collective-permute-start(f32[2,128,512]{2,1,0:T(8,128)S(1)} %get-tuple-element.99), channel_id=1, source_target_pairs={{0,4},{1,5},{2,6},{3,7},{4,0},{5,1},{6,2},{7,3},{8,12},{9,13},{10,... | collective-permute-start | bytes 1572872 | tf_op jit(solution)/shard_map/ppermute | solution.py:334
  138.7 1.9 collective-permute-start.24
  157.6 16.7 %collective-permute-start.30 = (f32[2,128,512]{2,1,0:T(8,128)S(1)}, f32[2,128,512]{2,1,0:T(8,128)S(1)}, u32[]{:S(2)}, u32[]{:S(2)}) collective-permute-start(f32[2,128,512]{2,1,0:T(8,128)S(1)} %get-tuple-element.116), channel_id=1, source_target_pairs={{0,6},{1,7},{2,4},{3,5},{4,2},{5,3},{6,0},{7,1},{8,14},{9,15},{10,... | collective-permute-start | bytes 1572872 | tf_op jit(solution)/shard_map/ppermute | solution.py:334
  160.1 27.5 %collective-permute-start.31 = (f32[2,128,512]{2,1,0:T(8,128)S(1)}, f32[2,128,512]{2,1,0:T(8,128)S(1)}, u32[]{:S(2)}, u32[]{:S(2)}) collective-permute-start(f32[2,128,512]{2,1,0:T(8,128)S(1)} %get-tuple-element.117), channel_id=1, source_target_pairs={{0,2},{1,3},{2,0},{3,1},{4,6},{5,7},{6,4},{7,5},{8,10},{9,11},{10,... | collective-permute-start | bytes 1572872 | tf_op jit(solution)/shard_map/ppermute | solution.py:334
  160.1 28.1 %collective-permute-start.28 = (f32[2,128,512]{2,1,0:T(8,128)S(1)}, f32[2,128,512]{2,1,0:T(8,128)S(1)}, u32[]{:S(2)}, u32[]{:S(2)}) collective-permute-start(f32[2,128,512]{2,1,0:T(8,128)S(1)} %get-tuple-element.113), channel_id=1, source_target_pairs={{0,8},{8,16},{16,24},{24,0},{1,9},{9,17},{17,25},{25,1},{2,10},{10... | collective-permute-start | bytes 1572872 | tf_op jit(solution)/shard_map/ppermute | solution.py:342
  161.6 26.7 %collective-permute-start.29 = (f32[2,128,512]{2,1,0:T(8,128)S(1)}, f32[2,128,512]{2,1,0:T(8,128)S(1)}, u32[]{:S(2)}, u32[]{:S(2)}) collective-permute-start(f32[2,128,512]{2,1,0:T(8,128)S(1)} %get-tuple-element.114), channel_id=1, source_target_pairs={{8,0},{16,8},{24,16},{0,24},{9,1},{17,9},{25,17},{1,25},{10,2},{18... | collective-permute-start | bytes 1572872 | tf_op jit(solution)/shard_map/ppermute | solution.py:343
  163.0 41.4 %collective-permute-start.27 = (f32[2,128,512]{2,1,0:T(8,128)S(1)}, f32[2,128,512]{2,1,0:T(8,128)S(1)}, u32[]{:S(2)}, u32[]{:S(2)}) collective-permute-start(f32[2,128,512]{2,1,0:T(8,128)S(1)} %get-tuple-element.112), channel_id=1, source_target_pairs={{0,4},{1,5},{2,6},{3,7},{4,0},{5,1},{6,2},{7,3},{8,12},{9,13},{10,... | collective-permute-start | bytes 1572872 | tf_op jit(solution)/shard_map/ppermute | solution.py:334
  (19 other events, 96.8 us)
